TPU v7x, 32 devices: a whole 2x2x4 slice. The times are simulated.
32 devices in a mesh: dp: 16 (over z, x, core), tensor: 2 (over y).
Axes of the slice: x: 2, y: 2, z: 4, core: 2. Of those that a mesh axis runs over, the one named last changes fastest.
Arguments:
- history: bfloat16 [9, 2048, 4096], P(None, 'dp'), may hold values from -6 to 6
- mix_weights: float32 [4096, 4, 9], P('dp'), may hold values from -2 to 2
- w_qkv: bfloat16 [3, 2048, 2048], P(None, 'dp', 'tensor'), may hold values from -0.125 to 0.125
- w_out: bfloat16 [2048, 2048], P('dp', 'tensor'), may hold values from -0.5 to 0.5
- w_up: bfloat16 [2048, 8192], P('dp', 'tensor'), may hold values from -0.125 to 0.125
- w_down: bfloat16 [2048, 8192], P('dp', 'tensor'), may hold values from -0.0625 to 0.0625
- norm_gain: bfloat16 [2, 2048], P(None, 'dp'), may hold values from 0.25 to 1.75
- norm_bias: bfloat16 [2, 2048], P(None, 'dp'), may hold values from -1.796875 to 1.796875
- mix_in: bfloat16 [2048, 40], P('dp'), may hold values from -0.125 to 0.125
- mix_out: bfloat16 [40, 40], replicated, may hold values from -1 to 1
- mix_static: float32 [40], replicated, may hold values from -3 to 3
- out_cot: bfloat16 [4096, 2048], P('dp'), may hold values from -6 to 6
- next_cot: float32 [4096, 4, 10], P('dp'), may hold values from -6 to 6
Outputs:
- block_out: bfloat16 [4096, 2048], P('dp')
- next_mix: float32 [4096, 4, 10], P('dp')
- history_grad: bfloat16 [9, 2048, 4096], P(None, 'dp')
- mix_grad: float32 [4096, 4, 9], P('dp')
- w_qkv_grad: float32 [3, 2048, 2048], P(None, 'dp', 'tensor')
- w_out_grad: float32 [2048, 2048], P('dp', 'tensor')
- w_up_grad: float32 [2048, 8192], P('dp', 'tensor')
- w_down_grad: float32 [2048, 8192], P('dp', 'tensor')
- gain_grad: float32 [2, 2048], P(None, 'dp')
- bias_grad: float32 [2, 2048], P(None, 'dp')
- mix_in_grad: float32 [2048, 40], P('dp')
- mix_out_grad: float32 [40, 40], replicated
- static_grad: float32 [40], replicated
All inputs are finite; a program needn't handle non-finite values.
Results may differ from a plain program's by a relative error of at most 0.015.
Values may be sent and summed in bfloat16 or wider, within the bound.
A program may use at most 384 MiB of HBM per device.

v0:
```python
import math

import jax
import jax.numpy as jnp
from jax import lax
from jax.sharding import PartitionSpec as P

HD = 128
ROT = 32
HIST = 9
STREAMS = 4
NEXT = 10


NORM_EPS = 1e-05
ROOT_EPS = 1e-06
MASKED = -1e30


def layer_norm(values, norm_weight, norm_shift):
    centre = jnp.mean(values, axis=-1, keepdims=True)
    offset = values - centre
    spread = jnp.mean(offset * offset, axis=-1, keepdims=True)
    return offset * lax.rsqrt(spread + NORM_EPS) * norm_weight + norm_shift


def root_norm(values):
    return values * lax.rsqrt(jnp.mean(values * values, axis=-1, keepdims=True) + ROOT_EPS)


def exact_gelu(values):
    return jax.nn.gelu(values, approximate=False)


def rotary_tables(length, rotary, float_type):
    half_rot = rotary // 2
    places = jnp.arange(length).astype(float_type)
    frequency = jnp.exp(
        jnp.arange(half_rot).astype(float_type) * (-2.0 * math.log(10000.0) / rotary)
    )
    angles = places[:, None] * frequency[None, :]
    return (jnp.cos(angles), jnp.sin(angles))


def rotate(values, cos_table, sin_table):
    half_rot = cos_table.shape[-1]
    first_half = values[..., :half_rot]
    second = values[..., half_rot : 2 * half_rot]
    return jnp.concatenate(
        [
            first_half * cos_table - second * sin_table,
            second * cos_table + first_half * sin_table,
            values[..., 2 * half_rot :],
        ],
        axis=-1,
    )


def masked_scores(queries, key_rows):
    length = queries.shape[1]
    score_scale = 1.0 / math.sqrt(queries.shape[2])
    causal = lax.broadcasted_iota(jnp.int32, (length, length), 0) >= lax.broadcasted_iota(
        jnp.int32, (length, length), 1
    )
    scores = (
        jnp.einsum("hqd,hkd->hqk", queries, key_rows, preferred_element_type=jnp.float32)
        * score_scale
    )
    return (jnp.where(causal[None], scores, MASKED), score_scale)


def attend_forward(queries, key_rows, value_rows):
    scores, score_scale = masked_scores(queries, key_rows)
    row_peak = jnp.max(scores, axis=-1, keepdims=True)
    raised = jnp.exp(scores - row_peak)
    row_total = jnp.sum(raised, axis=-1, keepdims=True)
    prob_low = (raised / row_total).astype(jnp.bfloat16)
    context = jnp.einsum("hqk,hkd->hqd", prob_low, value_rows, preferred_element_type=jnp.float32)
    return (context.astype(jnp.bfloat16), row_peak + jnp.log(row_total))


def attend_backward(queries, key_rows, value_rows, log_sum, context_grad):
    scores, score_scale = masked_scores(queries, key_rows)
    attn_prob = jnp.exp(scores - log_sum)
    prob_low = attn_prob.astype(jnp.bfloat16)
    value_grad = jnp.einsum(
        "hqk,hqd->hkd", prob_low, context_grad, preferred_element_type=jnp.float32
    )
    prob_grad = jnp.einsum(
        "hqd,hkd->hqk", context_grad, value_rows, preferred_element_type=jnp.float32
    )
    inner_sum = jnp.sum(attn_prob * prob_grad, axis=-1, keepdims=True)
    score_grad = (attn_prob * (prob_grad - inner_sum)).astype(jnp.bfloat16)
    query_grad = (
        jnp.einsum("hqk,hkd->hqd", score_grad, key_rows, preferred_element_type=jnp.float32)
        * score_scale
    )
    key_grad = (
        jnp.einsum("hqk,hqd->hkd", score_grad, queries, preferred_element_type=jnp.float32)
        * score_scale
    )
    return (query_grad, key_grad, value_grad)


def per_device(
    history,
    mix_weights,
    w_qkv,
    w_out,
    w_up,
    w_down,
    norm_gain,
    norm_bias,
    mix_in,
    mix_out,
    mix_static,
    out_cot,
    next_cot,
):
    hist_rows = lax.all_to_all(history, "dp", split_axis=2, concat_axis=1, tiled=True)
    gathered = (
        lax.all_gather(w_qkv, "dp", axis=1, tiled=True),
        lax.all_gather(w_out, "dp", axis=0, tiled=True),
        lax.all_gather(w_up, "dp", axis=0, tiled=True),
        lax.all_gather(w_down, "dp", axis=0, tiled=True),
        lax.all_gather(norm_gain, "dp", axis=1, tiled=True),
        lax.all_gather(norm_bias, "dp", axis=1, tiled=True),
        lax.all_gather(mix_in, "dp", axis=0, tiled=True),
    )
    qkv_full, out_full, up_full, down_full, gain_full, bias_full, mixin_full = gathered
    seq_len = mix_weights.shape[0]
    head_count = qkv_full.shape[2] // HD
    mix_order = jnp.transpose(mix_weights, (1, 2, 0))
    stream_cols = sum(
        (
            mix_order[:, source, None, :] * hist_rows[source].astype(jnp.float32)[None]
            for source in range(HIST)
        )
    )
    streams = jnp.transpose(stream_cols, (0, 2, 1))
    gain_wide = gain_full.astype(jnp.float32)
    bias_wide = bias_full.astype(jnp.float32)
    attn_norm, attn_norm_back = jax.vjp(layer_norm, streams[:3], gain_wide[0], bias_wide[0])
    attn_in = attn_norm.astype(jnp.bfloat16)
    projected = jnp.einsum("std,sde->ste", attn_in, qkv_full, preferred_element_type=jnp.float32)
    head_rows = jnp.transpose(projected.reshape(3, seq_len, head_count, HD), (0, 2, 1, 3))
    cos_table, sin_table = rotary_tables(seq_len, ROT, jnp.float32)
    queries = rotate(head_rows[0], cos_table, sin_table).astype(jnp.bfloat16)
    key_rows = rotate(head_rows[1], cos_table, sin_table).astype(jnp.bfloat16)
    value_rows = head_rows[2].astype(jnp.bfloat16)
    context, log_sum = attend_forward(queries, key_rows, value_rows)
    context_rows = jnp.transpose(context, (1, 0, 2)).reshape(seq_len, head_count * HD)
    attn_part = jnp.einsum("te,de->td", context_rows, out_full, preferred_element_type=jnp.float32)
    mlp_norm, mlp_norm_back = jax.vjp(layer_norm, streams[3], gain_wide[1], bias_wide[1])
    mlp_in = mlp_norm.astype(jnp.bfloat16)
    up_pre = jnp.dot(mlp_in, up_full, preferred_element_type=jnp.float32)
    hidden_wide, gelu_back = jax.vjp(exact_gelu, up_pre)
    hidden = hidden_wide.astype(jnp.bfloat16)
    mlp_part = jnp.einsum("tf,df->td", hidden, down_full, preferred_element_type=jnp.float32)
    branch = lax.psum((attn_part + mlp_part).astype(jnp.bfloat16), "tensor").astype(jnp.float32)
    block_wide = streams[3] + branch
    normed_wide, root_back = jax.vjp(root_norm, block_wide)
    normed = normed_wide.astype(jnp.bfloat16)
    inner_pre = jnp.dot(normed, mixin_full, preferred_element_type=jnp.float32)
    inner_wide, inner_back = jax.vjp(exact_gelu, inner_pre)
    inner_low = inner_wide.astype(jnp.bfloat16)
    next_flat = jnp.dot(inner_low, mix_out, preferred_element_type=jnp.float32) + mix_static
    next_mix = next_flat.reshape(seq_len, STREAMS, NEXT)
    qkv_full, out_full, up_full, down_full, mixin_full = (
        lax.all_gather(w_qkv, "dp", axis=1, tiled=True),
        lax.all_gather(w_out, "dp", axis=0, tiled=True),
        lax.all_gather(w_up, "dp", axis=0, tiled=True),
        lax.all_gather(w_down, "dp", axis=0, tiled=True),
        lax.all_gather(mix_in, "dp", axis=0, tiled=True),
    )
    next_grad = next_cot.reshape(seq_len, STREAMS * NEXT)
    static_grad = jnp.sum(next_grad, axis=0)
    next_low = next_grad.astype(jnp.bfloat16)
    mixout_grad = jnp.einsum("tm,tn->mn", inner_low, next_low, preferred_element_type=jnp.float32)
    inner_grad = inner_back(
        jnp.einsum("tn,mn->tm", next_low, mix_out, preferred_element_type=jnp.float32)
    )[0].astype(jnp.bfloat16)
    normed_grad = jnp.einsum(
        "tm,dm->td", inner_grad, mixin_full, preferred_element_type=jnp.float32
    )
    block_grad = out_cot.astype(jnp.float32) + root_back(normed_grad)[0]
    branch_grad = block_grad.astype(jnp.bfloat16)
    hidden_grad = jnp.dot(branch_grad, down_full, preferred_element_type=jnp.float32)
    up_grad_low = gelu_back(hidden_grad)[0].astype(jnp.bfloat16)
    mlp_in_grad = jnp.einsum("tf,df->td", up_grad_low, up_full, preferred_element_type=jnp.float32)
    context_grad_rows = jnp.dot(branch_grad, out_full, preferred_element_type=jnp.float32).astype(
        jnp.bfloat16
    )
    context_grad = jnp.transpose(context_grad_rows.reshape(seq_len, head_count, HD), (1, 0, 2))
    query_grad, key_grad, value_grad = attend_backward(
        queries, key_rows, value_rows, log_sum, context_grad
    )
    head_grads = jnp.stack(
        [
            rotate(query_grad, cos_table, -sin_table),
            rotate(key_grad, cos_table, -sin_table),
            value_grad,
        ]
    )
    proj_grad = (
        jnp.transpose(head_grads, (0, 2, 1, 3))
        .reshape(3, seq_len, head_count * HD)
        .astype(jnp.bfloat16)
    )
    attn_in_grad = jnp.einsum(
        "ste,sde->std", proj_grad, qkv_full, preferred_element_type=jnp.float32
    )
    attn_in_grad, mlp_in_grad = (
        lax.psum(attn_in_grad.astype(jnp.bfloat16), "tensor").astype(jnp.float32),
        lax.psum(mlp_in_grad.astype(jnp.bfloat16), "tensor").astype(jnp.float32),
    )
    streams_grad, gain_grad_attn, bias_grad_attn = attn_norm_back(attn_in_grad)
    residual_grad, gain_grad_mlp, bias_grad_mlp = mlp_norm_back(mlp_in_grad)
    stream_grad = jnp.concatenate([streams_grad, (residual_grad + block_grad)[None]], axis=0)
    grad_cols = jnp.transpose(stream_grad, (0, 2, 1))
    mix_parts = jnp.stack(
        [
            jnp.sum(grad_cols * hist_rows[source].astype(jnp.float32)[None], axis=1)
            for source in range(HIST)
        ],
        axis=2,
    )
    mix_grad = jnp.transpose(mix_parts, (1, 0, 2))
    hist_grad_cols = jnp.stack(
        [
            sum(
                (
                    mix_order[stream, source][None, :] * grad_cols[stream]
                    for stream in range(STREAMS)
                )
            )
            for source in range(HIST)
        ]
    ).astype(jnp.bfloat16)
    history_grad = lax.all_to_all(hist_grad_cols, "dp", split_axis=1, concat_axis=2, tiled=True)
    small_cols = jnp.stack([gain_grad_attn, gain_grad_mlp, bias_grad_attn, bias_grad_mlp], axis=1)
    qkv_grad = jnp.einsum("std,ste->sde", attn_in, proj_grad, preferred_element_type=jnp.float32)
    out_grad = jnp.einsum(
        "td,te->de", branch_grad, context_rows, preferred_element_type=jnp.float32
    )
    up_grad = jnp.einsum("td,tf->df", mlp_in, up_grad_low, preferred_element_type=jnp.float32)
    down_grad = jnp.einsum("td,tf->df", branch_grad, hidden, preferred_element_type=jnp.float32)
    mixin_grad = jnp.einsum("td,tm->dm", normed, inner_grad, preferred_element_type=jnp.float32)
    summed = (
        lax.psum_scatter(qkv_grad, "dp", scatter_dimension=1, tiled=True),
        lax.psum_scatter(out_grad, "dp", scatter_dimension=0, tiled=True),
        lax.psum_scatter(up_grad, "dp", scatter_dimension=0, tiled=True),
        lax.psum_scatter(down_grad, "dp", scatter_dimension=0, tiled=True),
        lax.psum_scatter(jnp.transpose(small_cols[:, 0:2]), "dp", scatter_dimension=1, tiled=True),
        lax.psum_scatter(jnp.transpose(small_cols[:, 2:4]), "dp", scatter_dimension=1, tiled=True),
        lax.psum_scatter(mixin_grad, "dp", scatter_dimension=0, tiled=True),
    )
    qkv_total, out_total, up_total, down_total, gain_total, bias_total, mixin_total = summed
    mixout_total, static_total = lax.psum((mixout_grad, static_grad), "dp")
    return (
        block_wide.astype(jnp.bfloat16),
        next_mix,
        history_grad,
        mix_grad,
        qkv_total,
        out_total,
        up_total,
        down_total,
        gain_total,
        bias_total,
        mixin_total,
        mixout_total,
        static_total,
    )


def solution(mesh):
    return jax.shard_map(
        per_device,
        mesh=mesh,
        in_specs=(
            P(None, "dp", None),
            P("dp", None, None),
            P(None, "dp", "tensor"),
            P("dp", "tensor"),
            P("dp", "tensor"),
            P("dp", "tensor"),
            P(None, "dp"),
            P(None, "dp"),
            P("dp", None),
            P(),
            P(),
            P("dp", None),
            P("dp", None, None),
        ),
        out_specs=(
            P("dp", None),
            P("dp", None, None),
            P(None, "dp", None),
            P("dp", None, None),
            P(None, "dp", "tensor"),
            P("dp", "tensor"),
            P("dp", "tensor"),
            P("dp", "tensor"),
            P(None, "dp"),
            P(None, "dp"),
            P("dp", None),
            P(),
            P(),
        ),
        check_vma=False,
    )
```

profile of v0, /device:TPU:7, one launch (start us, length us, event | category | flops | bytes accessed | tf_op | source)
XLA Modules:
  0.0 2453.2 jit_solution(9015686246957454978)
XLA Ops:
  9.4 23.2 copy.156
  41.0 559.8 %all_gather.27 = bf16[2,2048]{1,0:T(2,128)(2,1)S(1)} all-gather(bf16[2,128]{1,0:T(2,128)(2,1)S(1)} %copy-done.58), channel_id=1, replica_groups=mesh['dp'=16,'tensor'=2] {'dp'}, dimensions={1}, use_global_device_ids=true | all-gather | bytes 8704 | tf_op jit(solution)/shard_map/all_gather | solution.py:127
  600.8 19.0 all_gather.26
  620.5 22.5 copy.158
  698.0 10.4 convolution_bitcast_fusion
  714.0 19.8 multiply_convert_fusion
  733.8 10.2 fusion.61
  750.2 21.5 all_gather.32
  771.7 16.8 all-reduce.5.cloned.1.call-done
  813.7 14.9 add_convert_fusion.1
  828.6 11.9 convolution_convert_fusion.1
  840.5 10.3 convolution_convert_fusion
  851.3 107.9 %all-reduce.7.cloned.1.call-done = (bf16[256,2048]{1,0:T(8,128)(2,1)}, bf16[3,256,2048]{2,1,0:T(8,128)(2,1)}) async-done(((bf16[256,2048]{1,0:T(8,128)(2,1)}, bf16[3,256,2048]{2,1,0:T(8,128)(2,1)}), (bf16[256,2048]{1,0:T(8,128)(2,1)}, bf16[3,256,2048]{2,1,0:T(8,128)(2,1)})) %all-reduce.7.cloned.1.call-update) | async-done | bytes 4194320 | tf_op jit(solution)/shard_map/psum | solution.py:215
  982.1 16.0 fusion.47
  998.2 18.2 fusion.50
  1016.7 14.9 fusion.63
  1059.2 21.5 copy.187
  1110.2 396.4 %all-reduce = (f32[40,40]{1,0:T(8,128)}, f32[40]{0:T(128)}) all-reduce(f32[40,40]{1,0:T(8,128)S(1)} %fusion.64, f32[40]{0:T(128)S(1)} %reduce_sum.298), channel_id=1, replica_groups=mesh['dp'=16,'tensor'=2] {'dp'}, use_global_device_ids=true, to_apply=%region_36.37 | all-reduce | flops 1640 | bytes 13120 | tf_op jit(solution)/shard_map/psum | solution.py:259
  1506.6 10.8 multiply_reduce_fusion.1
  1520.5 12.9 copy.188
  1533.4 16.0 all_to_all.30
  1549.4 224.0 %reduce-scatter.12.cloned.1.call-done = f32[3,128,1024]{2,1,0:T(8,128)} async-done(((f32[3,2048,1024]{2,1,0:T(8,128)}), f32[3,128,1024]{2,1,0:T(8,128)}) %reduce-scatter.12.cloned.1.call-update) | async-done | bytes 1572880 | tf_op jit(solution)/shard_map/reduce_scatter | solution.py:250
  1773.4 336.4 %reduce-scatter.16.cloned.1.call-done = f32[128,4096]{1,0:T(8,128)} async-done(((f32[2048,4096]{1,0:T(8,128)}), f32[128,4096]{1,0:T(8,128)}) %reduce-scatter.16.cloned.1.call-update) | async-done | bytes 2097168 | tf_op jit(solution)/shard_map/reduce_scatter | solution.py:252
  2109.8 336.7 %reduce-scatter.18.cloned.1.call-done = f32[128,4096]{1,0:T(8,128)} async-done(((f32[2048,4096]{1,0:T(8,128)}), f32[128,4096]{1,0:T(8,128)}) %reduce-scatter.18.cloned.1.call-update) | async-done | bytes 2097168 | tf_op jit(solution)/shard_map/reduce_scatter | solution.py:253
  (292 shorter events, 186.1 us)
Async XLA Ops:
  7.2 784.1 %copy-start = (bf16[40,40]{1,0:T(8,128)(2,1)S(1)}, bf16[40,40]{1,0:T(8,128)(2,1)}, u32[]{:S(2)}) copy-start(bf16[40,40]{1,0:T(8,128)(2,1)} %param.22) | copy-start | bytes 9604
  7.2 690.8 %all-gather.5.cloned.1.call-start = ((), (), s32[]{:S(2)}) async-start(), calls=%async_computation.9 | async-start | bytes 13369344 | tf_op jit(solution)/shard_map/all_gather | solution.py:122
  7.9 706.0 %all-gather.9.cloned.1.call-start = ((), (), s32[]{:S(2)}) async-start(), calls=%async_computation.11 | async-start | bytes 17825792 | tf_op jit(solution)/shard_map/all_gather | solution.py:124
  8.7 725.1 %all-gather.11.cloned.1.call-start = ((), (), s32[]{:S(2)}) async-start(), calls=%async_computation.12 | async-start | bytes 17825792 | tf_op jit(solution)/shard_map/all_gather | solution.py:125
  32.6 568.2 %copy-start.59 = (bf16[2,128]{1,0:T(2,128)(2,1)S(1)}, bf16[2,128]{1,0:T(2,128)(2,1)}, u32[]{:S(2)}) copy-start(bf16[2,128]{1,0:T(2,128)(2,1)} %param.19) | copy-start | bytes 1540
  32.6 587.3 %copy-start.39 = (f32[256,4,9]{0,1,2:T(4,128)S(1)}, f32[256,4,9]{0,1,2:T(4,128)}, u32[]{:S(2)}) copy-start(f32[256,4,9]{0,1,2:T(4,128)} %param.14) | copy-start | bytes 110596
  32.6 587.9 %all-to-all-start = ((bf16[9,128,4096]{1,0,2:T(8,128)(2,1)}), bf16[9,128,4096]{1,0,2:T(8,128)(2,1)}, u32[]{:S(2)}, u32[]{:S(2)}) async-start(bf16[9,128,4096]{1,0,2:T(8,128)(2,1)} %copy.156), calls=%async_computation | async-start | bytes 33554432 | tf_op jit(solution)/shard_map/all_to_all | solution.py:120
  39.4 704.6 %all-gather.7.cloned.1.call-start = ((), (), s32[]{:S(2)}) async-start(), calls=%async_computation.10 | async-start | bytes 4456448 | tf_op jit(solution)/shard_map/all_gather | solution.py:123
  40.0 748.5 %all-reduce.5.cloned.1.call-start = ((), (), s32[]{:S(2)}) async-start(), calls=%async_computation.13 | async-start | bytes 2097152 | tf_op jit(solution)/shard_map/psum | solution.py:160
  697.9 10.5 copy-start.46
  713.9 30.1 %copy-start.36 = (bf16[8,256,128]{1,2,0:T(8,128)(2,1)}, bf16[8,256,128]{1,2,0:T(8,128)(2,1)S(1)}, u32[]{:S(2)}) copy-start(bf16[8,256,128]{1,2,0:T(8,128)(2,1)S(1)} %convolution_convert_fusion.3) | copy-start | bytes 1572868
  733.8 10.2 copy-start.35
  749.3 210.0 %all-reduce.7.cloned.1.call-start = ((), (), s32[]{:S(2)}) async-start(), calls=%async_computation.21 | async-start | bytes 8388608 | tf_op jit(solution)/shard_map/psum | solution.py:215
  750.1 41.2 %copy-start.41 = (bf16[256,40]{0,1:T(8,128)(2,1)}, bf16[256,40]{0,1:T(8,128)(2,1)S(1)}, u32[]{:S(2)}) copy-start(bf16[256,40]{0,1:T(8,128)(2,1)S(1)} %convert_element_type.302) | copy-start | bytes 61444
  850.9 111.1 %copy-start.55 = (f32[256]{0:T(256)S(1)}, f32[256]{0:T(256)}, u32[]{:S(2)}) copy-start(f32[256]{0:T(256)} %copy-done.54) | copy-start | bytes 3076
  850.9 666.6 %reduce-scatter.22.cloned.1.call-start = ((), (), s32[]{:S(2)}) async-start(), calls=%async_computation.19 | async-start | bytes 1114112
  973.8 545.2 %reduce-scatter.24.cloned.1.call-start = ((), (), s32[]{:S(2)}) async-start(), calls=%async_computation.20 | async-start | bytes 1114112
  975.2 574.2 %reduce-scatter.20.cloned.1.call-start = ((), (), s32[]{:S(2)}) async-start(), calls=%async_computation.18 | async-start | bytes 348160 | tf_op jit(solution)/shard_map/reduce_scatter | solution.py:256
  976.4 573.0 %reduce-scatter.14.cloned.1.call-start = ((), (), s32[]{:S(2)}) async-start(), calls=%async_computation.15 | async-start | bytes 8912896 | tf_op jit(solution)/shard_map/reduce_scatter | solution.py:251
  982.1 791.3 %reduce-scatter.12.cloned.1.call-start = ((), (), s32[]{:S(2)}) async-start(), calls=%async_computation.14 | async-start | bytes 26738688 | tf_op jit(solution)/shard_map/reduce_scatter | solution.py:250
  998.2 1111.6 %reduce-scatter.16.cloned.1.call-start = ((), (), s32[]{:S(2)}) async-start(), calls=%async_computation.16 | async-start | bytes 35651584 | tf_op jit(solution)/shard_map/reduce_scatter | solution.py:252
  1016.4 1430.0 %reduce-scatter.18.cloned.1.call-start = ((), (), s32[]{:S(2)}) async-start(), calls=%async_computation.17 | async-start | bytes 35651584 | tf_op jit(solution)/shard_map/reduce_scatter | solution.py:253
  1080.7 439.8 %all-to-all-start.1 = ((bf16[9,2048,256]{2,0,1:T(8,128)(2,1)}), bf16[9,2048,256]{2,0,1:T(8,128)(2,1)}, u32[]{:S(2)}, u32[]{:S(2)}) async-start(bf16[9,2048,256]{2,0,1:T(8,128)(2,1)} %copy.187), calls=%async_computation.1 | async-start | bytes 33554432 | tf_op jit(solution)/shard_map/all_to_all | solution.py:240
  1517.5 15.9 copy-start.60
  (56 other events, 159.0 us)
Sparse Core Ops, SparseCore 0:
  10.2 306.7 all-gather.4
  319.2 212.1 all-gather.8
  533.6 140.7 all-gather.10
  676.4 48.8 all-gather.6
  749.4 39.0 all-reduce.4
  851.0 108.2 all-reduce.6
  973.9 56.2 reduce-scatter.21
  1034.3 56.5 reduce-scatter.23
  1094.8 314.1 reduce-scatter.19
  1413.5 111.4 reduce-scatter.13
  1529.7 243.6 reduce-scatter.11
  1778.1 331.6 reduce-scatter.15
  2114.6 331.7 reduce-scatter.17
where the time goes:
time: 2460 us; the launch traced here: 2450 us
  waiting for transfers between devices  1020 us (41%)
  blocking collectives  997 us (41%)
  local copies, waits for them, and re-layouts  172 us (7%)
  matrix products  150 us (6%)
  other arithmetic  80.2 us (3%)
    all_gather x1, blocking collectives, per_device(): lax.all_gather(norm_bias, 'dp', axis=1, tiled=True)  560 us
    psum x1, blocking collectives, per_device(): mixout_total, static_total = lax.psum((mixout_grad, static_grad), 'dp')  396 us
    reduce_scatter x1, waiting for transfers between devices, per_device(): lax.psum_scatter(down_grad, 'dp', scatter_dimension=0, tiled=True)  337 us
    reduce_scatter x1, waiting for transfers between devices, per_device(): lax.psum_scatter(up_grad, 'dp', scatter_dimension=0, tiled=True)  336 us
    reduce_scatter x1, waiting for transfers between devices, per_device(): lax.psum_scatter(qkv_grad, 'dp', scatter_dimension=1, tiled=True)  224 us
    psum x1, waiting for transfers between devices, per_device(): lax.psum(mlp_in_grad.astype(jnp.bfloat16), 'tensor').astype(jnp.float32)  108 us
  transfers between devices with their start and end apart: 15, of which 5 were waited for; matrix products, arithmetic and copies ran while one was open for 12% of the time, Pallas kernels for 0%

commit v1 on v0

v1 whole, which is shorter than its diff:
```python
import functools
import math

import jax
import jax.numpy as jnp
from jax import lax
from jax.experimental import pallas as pl
from jax.experimental.pallas import tpu as pltpu
from jax.sharding import PartitionSpec as P

HD = 128
ROT = 32
HIST = 9
STREAMS = 4
NEXT = 10
MIXH = 40

NORM_EPS = 1e-05
ROOT_EPS = 1e-06
MASKED = -1e30

MESH = pl.DeviceIdType.MESH
ANY = pl.BlockSpec(memory_space=pl.ANY)
VM = pl.BlockSpec(memory_space=pltpu.VMEM)
DMA = pltpu.SemaphoreType.DMA
F32, BF16 = jnp.float32, jnp.bfloat16
CORE, SIDE, NEAR, HIGH = 1, 2, 4, 8
QUARTERS = 4


def bit(place, value):
    return lax.rem(lax.div(place, value), 2)


def flip(place, value):
    return place + value - 2 * value * bit(place, value)


def at(start, size, multiple=None):
    return pl.ds(pl.multiple_of(start, size if multiple is None else multiple), size)


def remote(src, dst, send, recv, **where):
    return pltpu.make_async_remote_copy(
        src_ref=src, dst_ref=dst, send_sem=send, recv_sem=recv, device_id=where, device_id_type=MESH
    )


def loop(lower, upper, step):
    def body(index, carry):
        step(index)
        return carry

    lax.fori_loop(lower, upper, body, 0)


def greet(targets):
    barrier = pltpu.get_barrier_semaphore()
    for target in targets:
        pl.semaphore_signal(barrier, inc=1, device_id=target, device_id_type=MESH)
    pl.semaphore_wait(barrier, len(targets))


def greet_all(n_dp, me, other_tensor):
    barrier = pltpu.get_barrier_semaphore()
    loop(
        1,
        n_dp,
        lambda step: pl.semaphore_signal(
            barrier, inc=1, device_id={"dp": lax.rem(me + step, n_dp)}, device_id_type=MESH
        ),
    )
    pl.semaphore_signal(barrier, inc=1, device_id={"tensor": other_tensor}, device_id_type=MESH)
    pl.semaphore_wait(barrier, n_dp)


class Place:
    def __init__(self):
        self.me = lax.axis_index("dp")
        self.tensor = lax.axis_index("tensor")
        self.other = 1 - self.tensor
        self.core = bit(self.me, CORE)
        self.side = bit(self.me, SIDE)
        self.near = bit(self.me, NEAR)
        self.high = lax.div(self.me, HIGH)
        self.quarter = self.near * 2 + self.core
        self.peers = (
            (flip(self.me, CORE), self.near * 2 + 1 - self.core),
            (flip(self.me, NEAR), (1 - self.near) * 2 + self.core),
            (flip(flip(self.me, NEAR), CORE), (1 - self.near) * 2 + 1 - self.core),
        )


def sum_rows(ref_at, depth, chunk, of):
    def body(index, total):
        return total + jnp.sum(of(ref_at(index)), axis=0, keepdims=True)

    return lax.fori_loop(0, depth // chunk, body, jnp.zeros((1, 128), F32))


def gather_kernel(
    n_dp, hist, mix, small, w_qkv, w_up, w_down, w_out,
    o_mix, o_small, o_streams, o_act, o_qkv, o_up, o_down, o_out,
    mix_all, small_all, hist_in, mixed, streams, act,
    early_s, early_r, hist_sem, a2a_s, a2a_r, reshard_s, reshard_r, high_s, high_r, side_s, side_r,
    act_s, act_r, act_local, own_sem, out_sem,
):
    here = Place()
    me, tensor = here.me, here.tensor
    rows = small.shape[0]
    depth = rows * n_dp
    half = hist.shape[2] // n_dp // 2
    high_bits = int(math.log2(n_dp // HIGH))
    weights = ((w_qkv, o_qkv), (w_up, o_up), (w_down, o_down), (w_out, o_out))
    greet_all(n_dp, me, here.other)

    def early(which, buf, phase):
        if phase < high_bits:
            span = 1 << phase
            block = buf.at[pl.ds(lax.div(here.high, span) * span, span), here.near, here.side, here.core]
            target = flip(me, HIGH << phase)
        elif phase == high_bits:
            block, target = buf.at[:, here.near, here.side, here.core], flip(me, NEAR)
        elif phase == high_bits + 1:
            block, target = buf.at[:, :, here.side, here.core], flip(me, SIDE)
        else:
            block, target = buf.at[:, :, :, here.core], flip(me, CORE)
        return remote(block, block, early_s.at[which, phase], early_r.at[which, phase], dp=target)

    own = [
        pltpu.make_async_copy(mix, mix_all.at[here.high, here.near, here.side, here.core], own_sem.at[0]),
        pltpu.make_async_copy(small, small_all.at[here.high, here.near, here.side, here.core], own_sem.at[1]),
    ]
    for copy in own:
        copy.start()
    for copy in own:
        copy.wait()
    early_pairs = ((0, mix_all), (1, small_all))
    early(0, mix_all, 0).start()
    early(1, small_all, 0).start()

    def cut(ref, quarter):
        width = ref.shape[-1] // QUARTERS
        columns = at(quarter * width, width)
        return ref.at[:, :, columns] if len(ref.shape) == 3 else ref.at[:, columns]

    def slot(ref):
        index = (here.high, here.near, here.side, pl.ds(pl.multiple_of(here.core * rows, rows), rows))
        return ref.at[(slice(None),) + index] if len(ref.shape) == 6 else ref.at[index]

    def keep(array):
        w, o = weights[array]
        return pltpu.make_async_copy(cut(w, here.quarter), slot(o), own_sem.at[2 + array])

    def reshard(array, peer):
        w, o = weights[array]
        target, quarter = here.peers[peer]
        return remote(cut(w, quarter), slot(o), reshard_s.at[array, peer], reshard_r.at[array, peer], dp=target)

    def high_hop(array, phase):
        o = weights[array][1]
        span = 1 << phase
        index = (pl.ds(lax.div(here.high, span) * span, span), slice(None), here.side)
        block = o.at[(slice(None),) + index] if len(o.shape) == 6 else o.at[index]
        return remote(block, block, high_s.at[array, phase], high_r.at[array, phase], dp=flip(me, HIGH << phase))

    def side_hop(array):
        o = weights[array][1]
        block = o.at[:, :, :, here.side] if len(o.shape) == 6 else o.at[:, :, here.side]
        return remote(block, block, side_s.at[array], side_r.at[array], dp=flip(me, SIDE))

    for phase in range(1, high_bits + 3):
        for which, buf in early_pairs:
            early(which, buf, phase - 1).wait()
            early(which, buf, phase).start()
        if phase == 1:
            for array in range(len(weights)):
                keep(array).start()
                for peer in range(3):
                    reshard(array, peer).start()
    early(0, mix_all, high_bits + 2).wait()

    def fetch(step, buf):
        target = lax.rem(me + step, n_dp)
        return pltpu.make_async_copy(
            hist.at[:, :, at(target * 2 * half + tensor * half, half)], hist_in.at[buf], hist_sem.at[buf]
        )

    def send(step):
        target = lax.rem(me + step, n_dp)
        return remote(
            mixed.at[step], streams.at[:, at(me * rows, rows), :], a2a_s.at[step], a2a_r.at[step], dp=target
        )

    fetch(0, 0).start()

    def mix_step(step):
        buf = lax.rem(step, 2)

        @pl.when(step + 1 < n_dp)
        def _():
            fetch(step + 1, 1 - buf).start()

        fetch(step, buf).wait()
        target = lax.rem(me + step, n_dp)
        weight = mix_all[lax.div(target, HIGH), bit(target, NEAR), bit(target, SIDE), bit(target, CORE)]
        for row in range(0, rows, 32):
            part = pl.ds(row, 32)
            sources = [hist_in[buf, source, part, :].astype(F32) for source in range(HIST)]
            for stream in range(STREAMS):
                total = sum(
                    sources[source] * weight[stream * HIST + source][None, :] for source in range(HIST)
                )
                mixed[step, stream, part, :] = total.astype(BF16)

        @pl.when(step > 0)
        def _():
            send(step).start()

    loop(0, n_dp, mix_step)
    streams[:, at(me * rows, rows), :] = mixed[0]
    for array in range(len(weights)):
        keep(array).wait()
        for peer in range(3):
            reshard(array, peer).wait()
        for phase in range(high_bits):
            if phase == 0:
                high_hop(array, 0).start()
    early(1, small_all, high_bits + 2).wait()
    loop(1, n_dp, lambda step: send(step).wait())

    chunk = min(256, depth)

    def lanes(near, core, half_at, count):
        return at(near * 4 * half + core * 2 * half + half_at * half, count * half, half)

    def act_keep(stream):
        return pltpu.make_async_copy(
            act.at[stream], o_act.at[stream, :, lanes(here.near, here.core, tensor, 1)], act_local.at[stream]
        )

    def act_near(stream):
        return remote(
            act.at[stream], o_act.at[stream, :, lanes(here.near, here.core, tensor, 1)],
            act_s.at[0, stream], act_r.at[0, stream], dp=flip(me, NEAR),
        )

    def act_tensor(stream, second):
        span = lanes(1 - here.near if second else here.near, here.core, tensor, 1)
        return remote(
            o_act.at[stream, :, span] if second else act.at[stream], o_act.at[stream, :, span],
            act_s.at[1 + second, stream], act_r.at[1 + second, stream], tensor=here.other,
        )

    def act_core(stream, near):
        span = lanes(near, here.core, 0, 2)
        return remote(
            o_act.at[stream, :, span], o_act.at[stream, :, span],
            act_s.at[3 + near, stream], act_r.at[3 + near, stream], dp=flip(me, CORE),
        )

    for stream in range(STREAMS):
        block = 0 if stream < 3 else 1

        def piece(index):
            return streams[stream, at(index * chunk, chunk), :].astype(F32)

        centre = sum_rows(piece, depth, chunk, lambda v: v) / depth
        spread = sum_rows(piece, depth, chunk, lambda v: (v - centre) * (v - centre)) / depth
        root = lax.rsqrt(spread + NORM_EPS)

        def normalise(index):
            span = chunk // rows
            first = index * span
            column = jnp.concatenate(
                [
                    small_all[
                        lax.div(first + k, HIGH), bit(first + k, NEAR), bit(first + k, SIDE), bit(first + k, CORE)
                    ]
                    for k in range(span)
                ],
                axis=0,
            ).astype(F32)
            gain = column[:, MIXH + block : MIXH + block + 1]
            bias = column[:, MIXH + 2 + block : MIXH + 3 + block]
            act[stream, at(index * chunk, chunk), :] = (
                (piece(index) - centre) * root * gain + bias
            ).astype(BF16)

        loop(0, depth // chunk, normalise)
        act_near(stream).start()
        act_tensor(stream, 0).start()
        act_keep(stream).start()

    finals = [
        pltpu.make_async_copy(mix_all, o_mix, out_sem.at[0]),
        pltpu.make_async_copy(small_all, o_small, out_sem.at[1]),
        pltpu.make_async_copy(streams, o_streams, out_sem.at[2]),
    ]
    for copy in finals:
        copy.start()
    for array in range(len(weights)):
        for phase in range(high_bits):
            high_hop(array, phase).wait()
            if phase + 1 < high_bits:
                high_hop(array, phase + 1).start()
        side_hop(array).start()
    for stream in range(STREAMS):
        act_near(stream).wait()
        act_tensor(stream, 1).start()
    for stream in range(STREAMS):
        act_keep(stream).wait()
        act_tensor(stream, 0).wait()
        act_tensor(stream, 1).wait()
        for near in range(2):
            act_core(stream, near).start()
    for array in range(len(weights)):
        side_hop(array).wait()
    for stream in range(STREAMS):
        for near in range(2):
            act_core(stream, near).wait()
    for copy in finals:
        copy.wait()


def gather(n_dp, hist, mix, small, w_qkv, w_up, w_down, w_out):
    rows = small.shape[0]
    depth = rows * n_dp
    half = hist.shape[2] // n_dp // 2
    high = n_dp // HIGH
    high_bits = int(math.log2(high))
    grid = (high, 2, 2, 2)

    def cut(width):
        return (high, 2, 2, 2 * rows, width // QUARTERS)

    shapes = [
        (grid + mix.shape, F32),
        (grid + (rows, 128), BF16),
        ((STREAMS, depth, half), BF16),
        ((STREAMS, depth, 8 * half), BF16),
        ((3,) + cut(w_qkv.shape[2]), BF16),
        (cut(w_up.shape[1]), BF16),
        (cut(w_down.shape[1]), BF16),
        (cut(w_out.shape[1]), BF16),
    ]
    return pl.pallas_call(
        functools.partial(gather_kernel, n_dp),
        out_shape=[jax.ShapeDtypeStruct(*shape) for shape in shapes],
        in_specs=[ANY] * 7,
        out_specs=[ANY] * 8,
        scratch_shapes=[
            pltpu.VMEM(grid + mix.shape, F32),
            pltpu.VMEM(grid + (rows, 128), BF16),
            pltpu.VMEM((2, HIST, rows, half), BF16),
            pltpu.VMEM((n_dp, STREAMS, rows, half), BF16),
            pltpu.VMEM((STREAMS, depth, half), BF16),
            pltpu.VMEM((STREAMS, depth, half), BF16),
            DMA((2, high_bits + 3)),
            DMA((2, high_bits + 3)),
            DMA((2,)),
            DMA((n_dp,)),
            DMA((n_dp,)),
            DMA((4, 3)),
            DMA((4, 3)),
            DMA((4, high_bits)),
            DMA((4, high_bits)),
            DMA((4,)),
            DMA((4,)),
            DMA((5, STREAMS)),
            DMA((5, STREAMS)),
            DMA((STREAMS,)),
            DMA((6,)),
            DMA((3,)),
        ],
        compiler_params=pltpu.CompilerParams(
            collective_id=1, has_side_effects=True, vmem_limit_bytes=40 * 1024 * 1024
        ),
        name="gather",
    )(hist, mix, small, w_qkv, w_up, w_down, w_out)


def lane_block(half, near, core, half_at, count):
    return at(near * 4 * half + core * 2 * half + half_at * half, count * half, half)


def gelu_parts(values):
    phi = 0.5 * (1.0 + lax.erf(values * (1.0 / math.sqrt(2.0))))
    density = jnp.exp(-0.5 * values * values) * (1.0 / math.sqrt(2.0 * math.pi))
    return values * phi, phi + values * density


def reduce_group(here, half, part, theirs, own, from_core, from_tensor, from_near, sems, local, pieces, piece):
    core_s, core_r, tensor_s, tensor_r, near_s, near_r = sems

    def load(span, near, half_at):
        return pltpu.make_async_copy(
            part.at[piece(span), lane_block(half, near, here.core, half_at, 1)],
            own.at[near, half_at, piece(span)], local.at[span, near * 2 + half_at],
        )

    def to_core(span, near, half_at):
        return remote(
            part.at[piece(span), lane_block(half, near, 1 - here.core, half_at, 1)],
            from_core.at[near, half_at, piece(span)],
            core_s.at[span, near * 2 + half_at], core_r.at[span, near * 2 + half_at], dp=flip(here.me, CORE),
        )

    def to_tensor(span, near):
        return remote(
            own.at[near, here.other, piece(span)], from_tensor.at[near, piece(span)],
            tensor_s.at[span, near], tensor_r.at[span, near], tensor=here.other,
        )

    def to_near(span):
        return remote(
            from_tensor.at[1 - here.near, piece(span)], from_near.at[piece(span)],
            near_s.at[span], near_r.at[span], dp=flip(here.me, NEAR),
        )

    def start(span):
        for near in range(2):
            for half_at in range(2):
                to_core(span, near, half_at).start()
                load(span, near, half_at).start()

    def after_core(span):
        for near in range(2):
            for half_at in range(2):
                load(span, near, half_at).wait()
                to_core(span, near, half_at).wait()
            own[near, here.other, piece(span)] += from_core[near, here.other, piece(span)]
            to_tensor(span, near).start()
        for near in range(2):
            own[near, here.tensor, piece(span)] += from_core[near, here.tensor, piece(span)]

    def after_tensor(span):
        for near in range(2):
            to_tensor(span, near).wait()
        far = 1 - here.near
        from_tensor[far, piece(span)] += own[far, here.tensor, piece(span)]
        to_near(span).start()
        from_tensor[here.near, piece(span)] += own[here.near, here.tensor, piece(span)]

    def after_near(span):
        to_near(span).wait()

    return start, after_core, after_tensor, after_near


def join_kernel(
    part, streams, cot, small, mix_in, mix_out, mix_back, static, next_cot,
    o_grad, o_wide, o_block, o_next, o_mixin, o_tiny,
    own, from_core, from_tensor, from_near, residual, wide, normed, block, back, low, next_rows, mixin, tiny,
    core_s, core_r, tensor_s, tensor_r, near_s, near_r, local, share_s, share_r, own_sem,
):
    here = Place()
    me, tensor = here.me, here.tensor
    depth, half = cot.shape
    spans = core_s.shape[0]
    size = depth // spans
    chunk = 256
    greet([{"dp": flip(me, CORE)}, {"dp": flip(me, NEAR)}, {"tensor": here.other}])

    def piece(span):
        return pl.ds(span * size, size)

    start, after_core, after_tensor, after_near = reduce_group(
        here, half, part, None, own, from_core, from_tensor, from_near,
        (core_s, core_r, tensor_s, tensor_r, near_s, near_r), local, spans, piece,
    )
    fetch = pltpu.make_async_copy(streams.at[3], residual, own_sem.at[0])
    fetch.start()
    for span in range(spans):
        start(span)
    for span in range(spans):
        after_core(span)
    for span in range(spans):
        after_tensor(span)
    fetch.wait()
    squares = jnp.zeros((1, half), F32)
    for span in range(spans):
        after_near(span)

        def widen(index, total):
            rows = at(span * size + index * chunk, chunk)
            branch = from_tensor[here.near, rows, :].astype(F32) + from_near[rows, :].astype(F32)
            value = residual[rows, :].astype(F32) + branch
            wide[rows, :] = value
            block[rows, :] = value.astype(BF16)
            return total + jnp.sum(value * value, axis=0, keepdims=True)

        squares = lax.fori_loop(0, size // chunk, widen, squares)
    root = lax.rsqrt(squares / depth + ROOT_EPS)

    def share_block(which):
        lanes = at(tensor * half, half)
        if which == 0:
            return pltpu.make_async_copy(block, o_block.at[:, lanes], own_sem.at[1])
        return remote(block, o_block.at[:, lanes], share_s.at[0], share_r.at[0], tensor=here.other)

    share_block(0).start()
    share_block(1).start()

    def norm(index):
        rows = at(index * chunk, chunk)
        normed[rows, :] = (wide[rows, :] * root).astype(BF16)

    loop(0, depth // chunk, norm)
    inner, slope = gelu_parts(jnp.dot(mix_in[...], normed[...], preferred_element_type=F32))
    inner_low = inner.astype(BF16)
    next_rows[...] = (jnp.dot(mix_out[...], inner_low, preferred_element_type=F32) + static[...])[:MIXH]
    next_low = next_cot[...].astype(BF16)

    def nt(left, right):
        return lax.dot_general(left, right, (((1,), (1,)), ((), ())), preferred_element_type=F32)

    tiny[:, :128] = nt(inner_low, next_low)
    tiny[:, 128:] = jnp.broadcast_to(jnp.sum(next_cot[...], axis=1, keepdims=True), (128, 128))
    inner_grad = (jnp.dot(mix_back[...], next_low, preferred_element_type=F32) * slope).astype(BF16)

    def pull(index, total):
        rows = at(index * chunk, chunk)
        value = jnp.dot(small[rows, :], inner_grad, preferred_element_type=F32)
        back[rows, :] = value
        return total + jnp.sum(value * wide[rows, :] * root, axis=0, keepdims=True)

    along = lax.fori_loop(0, depth // chunk, pull, jnp.zeros((1, half), F32)) / depth

    def finish(index):
        rows = at(index * chunk, chunk)
        value = cot[rows, :].astype(F32) + root * (back[rows, :] - wide[rows, :] * root * along)
        back[rows, :] = value
        low[rows, :] = value.astype(BF16)

    loop(0, depth // chunk, finish)

    def share(kind, index):
        if kind == 0:
            source, lanes, where = low, lane_block(half, here.near, here.core, tensor, 1), {"dp": flip(me, NEAR)}
        elif kind == 1:
            lanes = lane_block(half, 1 - here.near if index else here.near, here.core, tensor, 1)
            source, where = (o_grad.at[:, lanes] if index else low), {"tensor": here.other}
        else:
            lanes, where = lane_block(half, index, here.core, 0, 2), {"dp": flip(me, CORE)}
            source = o_grad.at[:, lanes]
        number = 1 + 2 * kind + index
        return remote(source, o_grad.at[:, lanes], share_s.at[number], share_r.at[number], **where)

    share(0, 0).start()
    share(1, 0).start()
    keep = pltpu.make_async_copy(
        low, o_grad.at[:, lane_block(half, here.near, here.core, tensor, 1)], own_sem.at[2]
    )
    keep.start()

    def mixin_rows(index):
        rows = at(index * chunk, chunk)
        mixin[rows, :] = nt(normed[rows, :], inner_grad)

    loop(0, depth // chunk, mixin_rows)
    share(0, 0).wait()
    share(1, 1).start()
    lanes = at(tensor * half, half)
    next_share = remote(next_rows, o_next.at[:, lanes], share_s.at[7], share_r.at[7], tensor=here.other)
    next_share.start()
    finals = [
        pltpu.make_async_copy(next_rows, o_next.at[:, lanes], own_sem.at[3]),
        pltpu.make_async_copy(back, o_wide, own_sem.at[4]),
        pltpu.make_async_copy(mixin, o_mixin, own_sem.at[5]),
        pltpu.make_async_copy(tiny, o_tiny, own_sem.at[6]),
    ]
    for copy in finals:
        copy.start()
    keep.wait()
    share(1, 0).wait()
    share(1, 1).wait()
    for near in range(2):
        share(2, near).start()
    for near in range(2):
        share(2, near).wait()
    share_block(0).wait()
    share_block(1).wait()
    next_share.wait()
    for copy in finals:
        copy.wait()


def join(part, streams, cot, small, mix_in, mix_out, mix_back, static, next_cot):
    depth, half = cot.shape
    spans = 4
    shapes = [
        ((depth, 8 * half), BF16),
        ((depth, half), F32),
        ((depth, 2 * half), BF16),
        ((MIXH, 2 * half), F32),
        ((depth, 128), F32),
        ((128, 256), F32),
    ]
    return pl.pallas_call(
        join_kernel,
        out_shape=[jax.ShapeDtypeStruct(*shape) for shape in shapes],
        in_specs=[ANY, ANY] + [VM] * 7,
        out_specs=[ANY] * 6,
        scratch_shapes=[
            pltpu.VMEM((2, 2, depth, half), BF16),
            pltpu.VMEM((2, 2, depth, half), BF16),
            pltpu.VMEM((2, depth, half), BF16),
            pltpu.VMEM((depth, half), BF16),
            pltpu.VMEM((depth, half), BF16),
            pltpu.VMEM((depth, half), F32),
            pltpu.VMEM((depth, half), BF16),
            pltpu.VMEM((depth, half), BF16),
            pltpu.VMEM((depth, half), F32),
            pltpu.VMEM((depth, half), BF16),
            pltpu.VMEM((MIXH, half), F32),
            pltpu.VMEM((depth, 128), F32),
            pltpu.VMEM((128, 256), F32),
            DMA((spans, 4)),
            DMA((spans, 4)),
            DMA((spans, 2)),
            DMA((spans, 2)),
            DMA((spans,)),
            DMA((spans,)),
            DMA((spans, 4)),
            DMA((8,)),
            DMA((8,)),
            DMA((7,)),
        ],
        compiler_params=pltpu.CompilerParams(
            collective_id=2, has_side_effects=True, vmem_limit_bytes=40 * 1024 * 1024
        ),
        name="join",
    )(part, streams, cot, small, mix_in, mix_out, mix_back, static, next_cot)


def scatter_kernel(
    n_dp, attn_grad, mlp_grad, streams, small, wide_grad, mixin_part, hist, g_qkv, g_up, g_down, g_out,
    o_stream, o_mix, o_small, o_qkv, o_up, o_down, o_out,
    own, from_core, from_tensor, from_near, rows_in, wide, stream_grad, gains, biases, tiny, tiny_in, tiny_out,
    hist_in, arrived, mix_part, mix_in, mix_sum, tiny_sum,
    side_qkv, side_up, side_down, side_out, mine_qkv, mine_up, mine_down, mine_out,
    high_qkv, high_up, high_down, high_out,
    core_s, core_r, tensor_s, tensor_r, near_s, near_r, local, in_sem,
    side_s, side_r, side_local, high_s, high_r, peer_s, peer_r, peer_local,
    a2a_s, a2a_r, keep_sem, pass_s, pass_r, tiny_s, tiny_r, mix_s, mix_r, hist_sem, last_s, last_r, last_local,
):
    here = Place()
    me, tensor = here.me, here.tensor
    depth, half = wide_grad.shape
    rows = depth // n_dp
    high_bits = int(math.log2(n_dp // HIGH))
    chunk = min(256, depth)
    greet_all(n_dp, me, here.other)
    weights = (
        (g_qkv, side_qkv, mine_qkv, high_qkv, o_qkv),
        (g_up, side_up, mine_up, high_up, o_up),
        (g_down, side_down, mine_down, high_down, o_down),
        (g_out, side_out, mine_out, high_out, o_out),
    )

    def pick(ref, *index):
        return ref.at[(slice(None),) + index] if ref.shape[0] == 3 and len(ref.shape) > len(index) + 2 else ref.at[index]

    def everything(_):
        return pl.ds(0, depth)

    steps = []
    for stream in range(STREAMS):
        part = attn_grad.at[stream] if stream < 3 else mlp_grad
        steps.append(
            reduce_group(
                here, half, part, None, own.at[stream], from_core.at[stream], from_tensor.at[stream],
                from_near.at[stream],
                tuple(
                    sem.at[pl.ds(stream, 1)]
                    for sem in (core_s, core_r, tensor_s, tensor_r, near_s, near_r)
                ),
                local.at[pl.ds(stream, 1)], 1, everything,
            )
        )
    for stream in range(STREAMS):
        steps[stream][0](0)
    loads = [
        pltpu.make_async_copy(streams, rows_in, in_sem.at[0]),
        pltpu.make_async_copy(wide_grad, wide, in_sem.at[1]),
    ]
    for copy in loads:
        copy.start()

    def is_qkv(array):
        return array == 0

    def index_of(array, *index):
        return ((slice(None),) if is_qkv(array) else ()) + index

    def side_hop(array):
        g, side, _, _, _ = weights[array]
        return remote(
            g.at[index_of(array, slice(None), slice(None), 1 - here.side)], side, side_s.at[array], side_r.at[array],
            dp=flip(me, SIDE),
        )

    def side_load(array):
        g, _, mine, _, _ = weights[array]
        return pltpu.make_async_copy(
            g.at[index_of(array, slice(None), slice(None), here.side)], mine, side_local.at[array]
        )

    def high_hop(array, phase):
        _, _, mine, high, _ = weights[array]
        span = 1 << phase
        base = lax.div(here.high, span)
        theirs = base + 1 - 2 * lax.rem(base, 2)
        return remote(
            mine.at[index_of(array, pl.ds(theirs * span, span))], high.at[index_of(array, pl.ds(span - 1, span))],
            high_s.at[array, phase], high_r.at[array, phase], dp=flip(me, HIGH << phase),
        )

    def add_blocks(array, into, other, first_into, first_other, count):
        shape = into.shape
        tall, width = shape[-2:]
        outer = 3 if is_qkv(array) else 1
        step = 32

        def add(flat):
            lead = lax.div(flat, count * 2)
            rest = lax.rem(flat, count * 2)
            high, near = lax.div(rest, 2), lax.rem(rest, 2)
            prefix = (lead,) if is_qkv(array) else ()

            def tile(index):
                span = at(index * step, step)
                into[prefix + (first_into + high, near, span)] += other[prefix + (first_other + high, near, span)]

            loop(0, tall // step, tile)

        loop(0, outer * count * 2, add)

    for array in range(4):
        side_hop(array).start()
        side_load(array).start()
    for copy in loads:
        copy.wait()
    stats = []
    for stream in range(STREAMS):

        def piece(index):
            return rows_in[stream, at(index * chunk, chunk), :].astype(F32)

        centre = sum_rows(piece, depth, chunk, lambda v: v) / depth
        spread = sum_rows(piece, depth, chunk, lambda v: (v - centre) * (v - centre)) / depth
        stats.append((centre, lax.rsqrt(spread + NORM_EPS)))
    for stream in range(STREAMS):
        steps[stream][1](0)
    for array in range(4):
        side_load(array).wait()
        side_hop(array).wait()
        _, side, mine, _, _ = weights[array]
        add_blocks(array, mine, side, 0, 0, n_dp // HIGH)
        high_hop(array, high_bits - 1).start()
    for stream in range(STREAMS):
        steps[stream][2](0)

    for stream in range(STREAMS):
        steps[stream][3](0)
        group = 0 if stream < 3 else 1
        centre, root = stats[stream]

        def parts(index):
            span = at(index * chunk, chunk)
            grad = from_tensor[stream, here.near, span].astype(F32) + from_near[stream, span].astype(F32)
            hat = (rows_in[stream, span, :].astype(F32) - centre) * root
            gain = small[span, MIXH + group : MIXH + group + 1].astype(F32)
            return span, grad, hat, grad * gain

        def sums(index, carry):
            span, grad, hat, scaled = parts(index)
            if stream in (0, 3):
                gains[group, span] = grad * hat
                biases[group, span] = grad
            else:
                gains[group, span] += grad * hat
                biases[group, span] += grad
            return (
                carry[0] + jnp.sum(scaled, axis=0, keepdims=True),
                carry[1] + jnp.sum(scaled * hat, axis=0, keepdims=True),
            )

        zero = jnp.zeros((1, half), F32)
        total, along = lax.fori_loop(0, depth // chunk, sums, (zero, zero))

        def finish(index):
            span, grad, hat, scaled = parts(index)
            value = root * (scaled - total / depth - hat * (along / depth))
            if stream == 3:
                value = value + wide[span, :]
            stream_grad[stream, span] = value.astype(BF16)

        loop(0, depth // chunk, finish)

    def send(step):
        target = lax.rem(me + step, n_dp)
        return remote(
            stream_grad.at[:, at(target * rows, rows), :], arrived.at[step], a2a_s.at[step], a2a_r.at[step], dp=target
        )

    loop(1, n_dp, lambda step: send(step).start())

    def fetch(step, buf):
        source = lax.rem(me - step + n_dp, n_dp)
        return pltpu.make_async_copy(
            hist.at[:, :, at(source * 2 * half + tensor * half, half)], hist_in.at[buf], hist_sem.at[buf]
        )

    fetch(0, 0).start()
    own_block = pltpu.make_async_copy(stream_grad.at[:, at(me * rows, rows), :], arrived.at[0], last_local.at[0])
    own_block.start()

    column = lax.broadcasted_iota(jnp.int32, (chunk, 128), 1)

    def gather_tiny(index):
        span = at(index * chunk, chunk)
        value = mixin_part[span, :]
        for group in range(2):
            gain = jnp.sum(gains[group, span], axis=1, keepdims=True)
            bias = jnp.sum(biases[group, span], axis=1, keepdims=True)
            value = jnp.where(column == MIXH + group, gain, value)
            value = jnp.where(column == MIXH + 2 + group, bias, value)
        tiny[span, :] = value.astype(BF16)

    loop(0, depth // chunk, gather_tiny)

    def tiny_send(step):
        target = lax.rem(me + step, n_dp)
        return remote(tiny.at[at(target * rows, rows), :], tiny_in.at[step], tiny_s.at[step], tiny_r.at[step], dp=target)

    loop(1, n_dp, lambda step: tiny_send(step).start())

    for array in range(4):
        _, _, mine, high, _ = weights[array]
        for phase in reversed(range(high_bits)):
            high_hop(array, phase).wait()
            span = 1 << phase
            add_blocks(array, mine, high, lax.div(here.high, span) * span, span - 1, span)
            if phase:
                high_hop(array, phase - 1).start()

    def peer_hop(array, peer):
        _, _, mine, _, out = weights[array]
        width = mine.shape[-1]
        target, _ = here.peers[peer]
        core = bit(target, CORE)
        return remote(
            mine.at[index_of(array, here.high, bit(target, NEAR), at(core * rows, rows))],
            out.at[index_of(array, slice(None), at(here.quarter * width, width))],
            peer_s.at[array, peer], peer_r.at[array, peer], dp=target,
        )

    def peer_keep(array):
        _, _, mine, _, out = weights[array]
        width = mine.shape[-1]
        return pltpu.make_async_copy(
            mine.at[index_of(array, here.high, here.near, at(here.core * rows, rows))],
            out.at[index_of(array, slice(None), at(here.quarter * width, width))], peer_local.at[array],
        )

    for array in range(4):
        peer_keep(array).start()
        for peer in range(3):
            peer_hop(array, peer).start()
    own_block.wait()

    def keep_lanes(step):
        source = lax.rem(me - step + n_dp, n_dp)
        return at(source * 2 * half + tensor * half, half)

    def keep(step):
        return pltpu.make_async_copy(arrived.at[step], o_stream.at[:, :, keep_lanes(step)], keep_sem.at[step])

    def pass_on(step):
        return remote(
            arrived.at[step], o_stream.at[:, :, keep_lanes(step)], pass_s.at[step], pass_r.at[step], tensor=here.other
        )

    def mix_send(step):
        return remote(
            mix_part.at[step], mix_in.at[step], mix_s.at[step], mix_r.at[step], dp=lax.rem(me - step + n_dp, n_dp)
        )

    def receive(step):
        buf = lax.rem(step, 2)

        @pl.when(step + 1 < n_dp)
        def _():
            fetch(step + 1, 1 - buf).start()

        @pl.when(step > 0)
        def _():
            send(step).wait()

        keep(step).start()
        pass_on(step).start()
        fetch(step, buf).wait()
        for stream in range(STREAMS):
            totals = [jnp.zeros((8, half), F32) for _ in range(HIST)]
            for row in range(0, rows, 16):
                span = pl.ds(row, 16)
                grad = arrived[step, stream, span, :].astype(F32)
                for source in range(HIST):
                    product = grad * hist_in[buf, source, span, :].astype(F32)
                    totals[source] = totals[source] + product[:8] + product[8:]
            for source in range(HIST):
                mix_part[step, pl.ds(stream * HIST + source, 1), :] = jnp.sum(totals[source], axis=0, keepdims=True)

        @pl.when(step > 0)
        def _():
            mix_send(step).start()

    mix_part[0] = jnp.zeros_like(mix_part[0])
    loop(0, n_dp, receive)

    mix_sum[...] = mix_part[0]

    def add_mix(step):
        mix_send(step).wait()
        mix_sum[...] += mix_in[step]

    loop(1, n_dp, add_mix)
    lanes = at(tensor * half, half)
    mix_share = remote(mix_sum, o_mix.at[:, lanes], last_s.at[0], last_r.at[0], tensor=here.other)
    mix_keep = pltpu.make_async_copy(mix_sum, o_mix.at[:, lanes], last_local.at[1])
    mix_share.start()
    mix_keep.start()
    tiny_sum[0] = tiny[at(me * rows, rows), :].astype(F32)

    def add_tiny(step):
        tiny_send(step).wait()
        tiny_sum[0] += tiny_in[step].astype(F32)

    loop(1, n_dp, add_tiny)
    tiny_share = remote(tiny_sum.at[0], tiny_sum.at[1], last_s.at[1], last_r.at[1], tensor=here.other)
    tiny_share.start()
    tiny_share.wait()
    tiny_out[...] = tiny_sum[0] + tiny_sum[1]
    tiny_keep = pltpu.make_async_copy(tiny_out, o_small, last_local.at[2])
    tiny_keep.start()
    for array in range(4):
        peer_keep(array).wait()
        for peer in range(3):
            peer_hop(array, peer).wait()

    def settle(step):
        keep(step).wait()
        pass_on(step).wait()

    loop(0, n_dp, settle)
    mix_share.wait()
    mix_keep.wait()
    tiny_keep.wait()


def scatter(n_dp, attn_grad, mlp_grad, streams, small, wide_grad, mixin_part, hist, g_qkv, g_up, g_down, g_out):
    depth, half = wide_grad.shape
    rows = depth // n_dp
    high = n_dp // HIGH
    high_bits = int(math.log2(high))
    grads = (g_qkv, g_up, g_down, g_out)

    def lead(g):
        return (3,) if g.ndim == 6 else ()

    def halved(g, highs):
        return lead(g) + (highs, 2) + g.shape[-2:]

    outs = [
        ((STREAMS, rows, 2 * half * n_dp), BF16),
        ((MIXH, 2 * half), F32),
        ((rows, 128), F32),
    ] + [(lead(g) + (rows, QUARTERS * g.shape[-1]), BF16) for g in grads]
    return pl.pallas_call(
        functools.partial(scatter_kernel, n_dp),
        out_shape=[jax.ShapeDtypeStruct(*shape) for shape in outs],
        in_specs=[ANY, ANY, ANY, VM, ANY, VM, ANY] + [ANY] * 4,
        out_specs=[ANY] * 7,
        scratch_shapes=[
            pltpu.VMEM((STREAMS, 2, 2, depth, half), BF16),
            pltpu.VMEM((STREAMS, 2, 2, depth, half), BF16),
            pltpu.VMEM((STREAMS, 2, depth, half), BF16),
            pltpu.VMEM((STREAMS, depth, half), BF16),
            pltpu.VMEM((STREAMS, depth, half), BF16),
            pltpu.VMEM((depth, half), F32),
            pltpu.VMEM((STREAMS, depth, half), BF16),
            pltpu.VMEM((2, depth, half), F32),
            pltpu.VMEM((2, depth, half), F32),
            pltpu.VMEM((depth, 128), BF16),
            pltpu.VMEM((n_dp, rows, 128), BF16),
            pltpu.VMEM((rows, 128), F32),
            pltpu.VMEM((2, HIST, rows, half), BF16),
            pltpu.VMEM((n_dp, STREAMS, rows, half), BF16),
            pltpu.VMEM((n_dp, MIXH, half), F32),
            pltpu.VMEM((n_dp, MIXH, half), F32),
            pltpu.VMEM((MIXH, half), F32),
            pltpu.VMEM((2, rows, 128), F32),
        ]
        + [pltpu.VMEM(halved(g, high), BF16) for g in grads]
        + [pltpu.VMEM(halved(g, high), BF16) for g in grads]
        + [pltpu.VMEM(halved(g, high - 1), BF16) for g in grads]
        + [
            DMA((STREAMS, 4)),
            DMA((STREAMS, 4)),
            DMA((STREAMS, 2)),
            DMA((STREAMS, 2)),
            DMA((STREAMS,)),
            DMA((STREAMS,)),
            DMA((STREAMS, 4)),
            DMA((2,)),
            DMA((4,)),
            DMA((4,)),
            DMA((4,)),
            DMA((4, high_bits)),
            DMA((4, high_bits)),
            DMA((4, 3)),
            DMA((4, 3)),
            DMA((4,)),
            DMA((n_dp,)),
            DMA((n_dp,)),
            DMA((n_dp,)),
            DMA((n_dp,)),
            DMA((n_dp,)),
            DMA((n_dp,)),
            DMA((n_dp,)),
            DMA((n_dp,)),
            DMA((n_dp,)),
            DMA((2,)),
            DMA((2,)),
            DMA((2,)),
            DMA((3,)),
        ],
        compiler_params=pltpu.CompilerParams(
            collective_id=3, has_side_effects=True, vmem_limit_bytes=60 * 1024 * 1024
        ),
        name="scatter",
    )(attn_grad, mlp_grad, streams, small, wide_grad, mixin_part, hist, *grads)


def exact_gelu(values):
    return jax.nn.gelu(values, approximate=False)


def rotary_tables(length, rotary, float_type):
    half_rot = rotary // 2
    places = jnp.arange(length).astype(float_type)
    frequency = jnp.exp(
        jnp.arange(half_rot).astype(float_type) * (-2.0 * math.log(10000.0) / rotary)
    )
    angles = places[:, None] * frequency[None, :]
    return (jnp.cos(angles), jnp.sin(angles))


def rotate(values, cos_table, sin_table):
    half_rot = cos_table.shape[-1]
    first_half = values[..., :half_rot]
    second = values[..., half_rot : 2 * half_rot]
    return jnp.concatenate(
        [
            first_half * cos_table - second * sin_table,
            second * cos_table + first_half * sin_table,
            values[..., 2 * half_rot :],
        ],
        axis=-1,
    )


def masked_scores(queries, key_rows):
    length = queries.shape[1]
    score_scale = 1.0 / math.sqrt(queries.shape[2])
    causal = lax.broadcasted_iota(jnp.int32, (length, length), 0) >= lax.broadcasted_iota(
        jnp.int32, (length, length), 1
    )
    scores = (
        jnp.einsum("hqd,hkd->hqk", queries, key_rows, preferred_element_type=jnp.float32)
        * score_scale
    )
    return (jnp.where(causal[None], scores, MASKED), score_scale)


def attend_forward(queries, key_rows, value_rows):
    scores, score_scale = masked_scores(queries, key_rows)
    row_peak = jnp.max(scores, axis=-1, keepdims=True)
    raised = jnp.exp(scores - row_peak)
    row_total = jnp.sum(raised, axis=-1, keepdims=True)
    prob_low = (raised / row_total).astype(jnp.bfloat16)
    context = jnp.einsum("hqk,hkd->hqd", prob_low, value_rows, preferred_element_type=jnp.float32)
    return (context.astype(jnp.bfloat16), row_peak + jnp.log(row_total))


def attend_backward(queries, key_rows, value_rows, log_sum, context_grad):
    scores, score_scale = masked_scores(queries, key_rows)
    attn_prob = jnp.exp(scores - log_sum)
    prob_low = attn_prob.astype(jnp.bfloat16)
    value_grad = jnp.einsum(
        "hqk,hqd->hkd", prob_low, context_grad, preferred_element_type=jnp.float32
    )
    prob_grad = jnp.einsum(
        "hqd,hkd->hqk", context_grad, value_rows, preferred_element_type=jnp.float32
    )
    inner_sum = jnp.sum(attn_prob * prob_grad, axis=-1, keepdims=True)
    score_grad = (attn_prob * (prob_grad - inner_sum)).astype(jnp.bfloat16)
    query_grad = (
        jnp.einsum("hqk,hkd->hqd", score_grad, key_rows, preferred_element_type=jnp.float32)
        * score_scale
    )
    key_grad = (
        jnp.einsum("hqk,hqd->hkd", score_grad, queries, preferred_element_type=jnp.float32)
        * score_scale
    )
    return (query_grad, key_grad, value_grad)


def per_device(
    n_dp, history, mix_weights, w_qkv, w_out, w_up, w_down, norm_gain, norm_bias, mix_in, mix_out, mix_static,
    out_cot, next_cot,
):
    tensor = lax.axis_index("tensor")
    seq_len = mix_weights.shape[0]
    half = seq_len // 2
    depth = mix_in.shape[0] * n_dp

    def own_half(rows):
        return lax.dynamic_slice_in_dim(rows, tensor * half, half, 0)

    mix_rows = jnp.pad(own_half(mix_weights.reshape(seq_len, -1)).T, ((0, MIXH - STREAMS * HIST), (0, 0)))
    small = jnp.concatenate([mix_in, norm_gain.T, norm_bias.T], axis=1)
    small = jnp.pad(small, ((0, 0), (0, 128 - small.shape[1])))
    mix_all, small_all, streams, act, qkv, up, down, out = gather(
        n_dp, history, mix_rows, small, w_qkv, w_up, w_down, w_out
    )
    small_all = small_all.reshape(depth, 128)
    qkv, up, down, out = (
        qkv.reshape(3, depth, -1), up.reshape(depth, -1), down.reshape(depth, -1), out.reshape(depth, -1)
    )
    tokens = act.shape[2]
    seqs = tokens // seq_len
    heads = qkv.shape[2] // HD
    projected = jnp.einsum("sdt,sde->ste", act[:3], qkv, preferred_element_type=F32)
    head_rows = jnp.transpose(projected.reshape(3, seqs, seq_len, heads, HD), (0, 1, 3, 2, 4)).reshape(
        3, seqs * heads, seq_len, HD
    )
    cos_table, sin_table = rotary_tables(seq_len, ROT, F32)
    queries = rotate(head_rows[0], cos_table, sin_table).astype(BF16)
    key_rows = rotate(head_rows[1], cos_table, sin_table).astype(BF16)
    value_rows = head_rows[2].astype(BF16)
    context, log_sum = attend_forward(queries, key_rows, value_rows)

    def join_heads(rows):
        return jnp.transpose(rows.reshape(seqs, heads, seq_len, HD), (0, 2, 1, 3)).reshape(tokens, heads * HD)

    context_rows = join_heads(context)
    up_pre = jnp.einsum("dt,df->tf", act[3], up, preferred_element_type=F32)
    hidden_wide, gelu_back = jax.vjp(exact_gelu, up_pre)
    hidden = hidden_wide.astype(BF16)
    part = (
        jnp.einsum("de,te->dt", out, context_rows, preferred_element_type=F32)
        + jnp.einsum("df,tf->dt", down, hidden, preferred_element_type=F32)
    ).astype(BF16)

    def square(values):
        return jnp.pad(values, ((0, 128 - values.shape[0]), (0, 128 - values.shape[1])))

    next_rows = own_half(next_cot.reshape(seq_len, -1)).T
    next_rows = jnp.pad(next_rows, ((0, 128 - next_rows.shape[0]), (0, 0)))
    mix_in_rows = jnp.pad(small_all[:, :MIXH].T, ((0, 128 - MIXH), (0, 0)))
    static = jnp.pad(mix_static[:, None], ((0, 128 - mix_static.shape[0]), (0, 0)))
    branch_grad, wide_grad, block, next_mix, mixin_part, tiny = join(
        part, streams, own_half(out_cot).T, small_all, mix_in_rows, square(mix_out.T), square(mix_out), static,
        next_rows,
    )
    mixout_total, static_total = lax.psum(
        (tiny[:MIXH, : STREAMS * NEXT], tiny[: STREAMS * NEXT, 128]), ("dp", "tensor")
    )
    hidden_grad = jnp.einsum("dt,df->tf", branch_grad, down, preferred_element_type=F32)
    up_grad_low = gelu_back(hidden_grad)[0].astype(BF16)
    mlp_in_grad = jnp.einsum("df,tf->dt", up, up_grad_low, preferred_element_type=F32).astype(BF16)
    context_grad_rows = jnp.einsum("dt,de->te", branch_grad, out, preferred_element_type=F32).astype(BF16)
    context_grad = jnp.transpose(context_grad_rows.reshape(seqs, seq_len, heads, HD), (0, 2, 1, 3)).reshape(
        seqs * heads, seq_len, HD
    )
    query_grad, key_grad, value_grad = attend_backward(queries, key_rows, value_rows, log_sum, context_grad)
    proj_grad = jnp.stack(
        [
            join_heads(rotate(query_grad, cos_table, -sin_table).astype(BF16)),
            join_heads(rotate(key_grad, cos_table, -sin_table).astype(BF16)),
            join_heads(value_grad.astype(BF16)),
        ]
    )
    attn_in_grad = jnp.einsum("sde,ste->sdt", qkv, proj_grad, preferred_element_type=F32).astype(BF16)
    g_qkv = jnp.einsum("sdt,ste->sde", act[:3], proj_grad, preferred_element_type=F32).astype(BF16)
    g_out = jnp.einsum("dt,te->de", branch_grad, context_rows, preferred_element_type=F32).astype(BF16)
    g_up = jnp.einsum("dt,tf->df", act[3], up_grad_low, preferred_element_type=F32).astype(BF16)
    g_down = jnp.einsum("dt,tf->df", branch_grad, hidden, preferred_element_type=F32).astype(BF16)
    grid = (n_dp // HIGH, 2, 2, 2 * mix_in.shape[0])
    stream_grad, mix_grad, small_total, qkv_total, up_total, down_total, out_total = scatter(
        n_dp, attn_in_grad, mlp_in_grad, streams, small_all, wide_grad, mixin_part, history,
        g_qkv.reshape((3,) + grid + (-1,)), g_up.reshape(grid + (-1,)), g_down.reshape(grid + (-1,)),
        g_out.reshape(grid + (-1,)),
    )
    mix_rows = mix_all.reshape(n_dp, MIXH, 1, half)
    mix_rows = lax.all_gather(mix_rows, "tensor", axis=2, tiled=True)
    mix_rows = jnp.transpose(mix_rows, (1, 0, 2, 3)).reshape(MIXH, n_dp * seq_len)
    history_grad = jnp.stack(
        [
            sum(
                mix_rows[stream * HIST + source][None, :] * stream_grad[stream].astype(F32)
                for stream in range(STREAMS)
            )
            for source in range(HIST)
        ]
    ).astype(BF16)
    return (
        block.T,
        next_mix.T.reshape(seq_len, STREAMS, NEXT),
        history_grad,
        mix_grad[: STREAMS * HIST].T.reshape(seq_len, STREAMS, HIST),
        qkv_total.astype(F32),
        out_total.astype(F32),
        up_total.astype(F32),
        down_total.astype(F32),
        small_total[:, MIXH : MIXH + 2].T,
        small_total[:, MIXH + 2 : MIXH + 4].T,
        small_total[:, :MIXH],
        mixout_total,
        static_total,
    )


def solution(mesh):
    return jax.shard_map(
        functools.partial(per_device, mesh.shape["dp"]),
        mesh=mesh,
        in_specs=(
            P(None, "dp", None),
            P("dp", None, None),
            P(None, "dp", "tensor"),
            P("dp", "tensor"),
            P("dp", "tensor"),
            P("dp", "tensor"),
            P(None, "dp"),
            P(None, "dp"),
            P("dp", None),
            P(),
            P(),
            P("dp", None),
            P("dp", None, None),
        ),
        out_specs=(
            P("dp", None),
            P("dp", None, None),
            P(None, "dp", None),
            P("dp", None, None),
            P(None, "dp", "tensor"),
            P("dp", "tensor"),
            P("dp", "tensor"),
            P("dp", "tensor"),
            P(None, "dp"),
            P(None, "dp"),
            P("dp", None),
            P(),
            P(),
        ),
        check_vma=False,
    )
```

time: 2460 us -> 900 us (0.37)
  waiting for transfers between devices: 1020 us -> 0 us
  blocking collectives: 997 us -> 49.3 us
  Pallas kernels: 0 us -> 662 us
  local copies, waits for them, and re-layouts: 172 us -> 58.5 us
  matrix products: 150 us -> 92.3 us
  other arithmetic: 80.2 us -> 22.5 us
    reduce_scatter x5 -> x0, waiting for transfers between devices: 897 us -> none  [the longest x1 337 us: per_device(): lax.psum_scatter(down_grad, 'dp', scatter_dimension=0, tiled=True)]
    pallas_call x0 -> x3, Pallas kernels: none -> 662 us  [the longest x1 304 us: scatter(): pl.pallas_call(functools.partial(scatter_kernel, n_dp), out_shape=[jax.Sh...]
    all_gather x3 -> x1, blocking collectives: 600 us -> 8.82 us  [per_device(): mix_rows = lax.all_gather(mix_rows, 'tensor', axis=2, tiled=True)]
    psum x1, blocking collectives: 396 us -> 40.5 us  [per_device(): lax.psum((tiny[:MIXH, :STREAMS * NEXT], tiny[:STREAMS * NEXT, 128]), ('dp...]
    psum x2 -> x0, waiting for transfers between devices: 125 us -> none  [the longest x1 108 us: per_device(): lax.psum(mlp_in_grad.astype(jnp.bfloat16), 'tensor').astype(jnp.float32)]
    dot_general x18 -> x12, matrix products: 143 us -> 86.8 us  [the longest x1 17.2 us: per_device(): up_pre = jnp.einsum('dt,df->tf', act[3], up, preferred_element_type=F32)]
    all_to_all x3 -> x0, local copies, waits for them, and re-layouts: 51.4 us -> none  [the longest x2 28.9 us: per_device(): lax.all_to_all(hist_grad_cols, 'dp', split_axis=1, concat_axis=2, tiled=T...]
    reduce_sum x11 -> x0, other arithmetic: 28.3 us -> none  [the longest x4 12.9 us: layer_norm(): return offset * lax.rsqrt(spread + NORM_EPS) * norm_weight + norm_shift]
  transfers between devices with their start and end apart: 15 -> 0, of which waited for: 5 -> 0; matrix products, arithmetic and copies ran while one was open for 12% -> 0% of each run, Pallas kernels for 0% -> 0%
where the time goes in v1:
time: 900 us; the launch traced here: 887 us
  Pallas kernels  662 us (74%)
  matrix products  92.3 us (10%)
  local copies, waits for them, and re-layouts  58.5 us (6%)
  blocking collectives  49.3 us (5%)
  other arithmetic  22.5 us (2%)
    pallas_call x1, Pallas kernels, scatter(): pl.pallas_call(functools.partial(scatter_kernel, n_dp), out_shape=[jax.Sh...  304 us
    pallas_call x1, Pallas kernels, gather(): pl.pallas_call(functools.partial(gather_kernel, n_dp), out_shape=[jax.Sha...  280 us
    pallas_call x1, Pallas kernels, join(): pl.pallas_call(join_kernel, out_shape=[jax.ShapeDtypeStruct(*shape) for s...  78.1 us
    psum x1, blocking collectives, per_device(): lax.psum((tiny[:MIXH, :STREAMS * NEXT], tiny[:STREAMS * NEXT, 128]), ('dp...  40.5 us
    unnamed x143, local copies, waits for them, and re-layouts  31.5 us

profile of v1, /device:TPU:7, one launch (start us, length us, event | category | flops | bytes accessed | tf_op | source)
XLA Modules:
  0.0 887.4 jit_solution(16426809544267875730)
XLA Ops:
  7.0 280.3 %gather.1 = (f32[2,2,2,2,40,128]{5,4,3,2,1,0:T(8,128)S(1)}, bf16[2,2,2,2,128,128]{5,4,3,2,1,0:T(8,128)(2,1)S(1)}, bf16[4,2048,128]{2,1,0:T(8,128)(2,1)S(1)}, bf1...) custom-call(bf16[9,128,4096]{2,1,0:T(8,128)(2,1)} %hist.3, ...), custom_call_target="tpu_custom_call" | custom-call | tf_op jit(solution)/shard_map/gather/pallas_call | solution.py:347
  289.1 2.0 copy-done.20
  292.8 10.9 %fusion.75 = f32[3,1024,256]{2,1,0:T(8,128)} fusion(bf16[4,2048,1024]{2,1,0:T(8,128)(2,1)} %get-tuple-element.35, bf16[3,2048,256]{2,1,0:T(8,128)(2,1)S(1)} %bitcast.138), kind=kOutput, calls=%fused_computation.170 | convolution fusion | flops 3221225472 | bytes 23068672 | tf_op jit(solution)/shard_map/sdt,sde->ste/dot_general | solution.py:1146
  303.8 5.2 reshape.510
  314.5 3.2 subtract_convert_fusion.3
  319.9 2.0 slice.458
  324.6 17.2 %multiply_convert_fusion = (bf16[1024,1024]{1,0:T(8,128)(2,1)S(1)}, f32[1024,1024]{1,0:T(8,128)}, f32[1024,1024]{1,0:T(8,128)}) fusion(bf16[2048,1024]{1,0:T(8,128)(2,1)S(1)} %bitcast.150, bf16[4,2048,1024]{2,1,0:T(8,128)(2,1)} %get-tuple-element.35), kind=kOutput, calls=%fused_computation.45 | convolution fusion | flops 4363124736 | bytes 18874368 | tf_op jit(solution)/shard_map/dt,df->tf/dot_general | solution.py:1160
  341.8 4.7 fusion.74
  346.6 3.2 add_convert_fusion.part
  350.6 1.9 copy.230
  358.8 78.1 %join.1 = (bf16[2048,1024]{1,0:T(8,128)(2,1)S(1)}, f32[2048,128]{1,0:T(8,128)S(1)}, bf16[2048,256]{1,0:T(8,128)(2,1)S(1)}, f32[40,256]{1,0:T(8,128)S(1)}, f32[20...) custom-call(bf16[2048,1024]{1,0:T(8,128)(2,1)} %add_convert_fusion.part, bf16[4,2048,128]{2,1,0:T(8,128)(2,1)S(1)} %get-tuple-element.39.streams, ...), custom_call_target="tpu_custom_call" | custom-call | tf_op jit(solution)/shard_map/join/pallas_call | solution.py:600
  437.0 2.3 convolution_convert_fusion.4
  441.9 5.8 add_convert_fusion.1
  447.8 9.1 %fusion.10 = bf16[2048,1024]{1,0:T(8,128)(2,1)} fusion(bf16[1024,1024]{1,0:T(8,128)(2,1)S(1)} %add_convert_fusion.1, bf16[4,2048,1024]{2,1,0:T(8,128)(2,1)} %get-tuple-element.35), kind=kOutput, calls=%fused_computation.59 | convolution fusion | flops 4297064448 | bytes 10485760 | tf_op jit(solution)/shard_map/dt,tf->df/dot_general | solution.py:1200
  456.9 6.3 convolution_convert_fusion.1
  468.3 2.2 stack_reshape.11
  482.7 9.9 %convolution_convert_fusion.3 = bf16[3,2048,256]{2,1,0:T(8,128)(2,1)} fusion(bf16[4,2048,1024]{2,1,0:T(8,128)(2,1)} %get-tuple-element.35, bf16[3,1024,256]{2,1,0:T(8,128)(2,1)S(1)} %constant_dynamic-update-slice_fusion), kind=kOutput, calls=%fused_computation.64 | convolution fusion | flops 3222798336 | bytes 21495808 | tf_op jit(solution)/shard_map/sdt,ste->sde/dot_general | solution.py:1198
  492.6 9.5 %convolution_convert_fusion.2.mlp_grad = bf16[2048,1024]{1,0:T(8,128)(2,1)} fusion(bf16[2048,1024]{1,0:T(8,128)(2,1)} %bitcast.149, bf16[1024,1024]{1,0:T(8,128)(2,1)} %copy-done.62), kind=kOutput, calls=%fused_computation.61 | convolution fusion | flops 4297064448 | bytes 10485760 | tf_op jit(solution)/shard_map/df,tf->dt/dot_general | solution.py:1184
  502.1 6.5 convolution_convert_fusion.attn_grad
  508.7 304.1 %scatter.1 = (bf16[4,128,4096]{2,1,0:T(8,128)(2,1)}, f32[40,256]{1,0:T(8,128)}, f32[128,128]{1,0:T(8,128)}, bf16[3,128,1024]{2,1,0:T(8,128)(2,1)}, bf16[128,4096...) custom-call(bf16[3,2048,1024]{2,1,0:T(8,128)(2,1)} %convolution_convert_fusion.attn_grad, ...), custom_call_target="tpu_custom_call" | custom-call | tf_op jit(solution)/shard_map/scatter/pallas_call | solution.py:981
  812.8 8.8 all_gather.3
  822.0 3.2 fusion.62
  832.5 3.7 copy-done.51
  836.4 40.5 %all-reduce.7 = (f32[40,40]{1,0:T(8,128)}, f32[40]{0:T(128)}) all-reduce(f32[40,40]{1,0:T(8,128)S(1)} %slice.332, f32[40]{0:T(128)S(1)} %slice_reduce_fusion), channel_id=1, replica_groups=mesh['dp'=16,'tensor'=2] {'dp','tensor'}, use_global_device_ids=true, to_apply=%region_3.4 | all-reduce | flops 1640 | bytes 13120 | tf_op jit(solution)/shard_map/psum | solution.py:1179
  (249 shorter events, 64.4 us)
Async XLA Ops:
  0.6 353.6 %copy-start = (bf16[256,2048]{1,0:T(8,128)(2,1)S(1)}, bf16[256,2048]{1,0:T(8,128)(2,1)}, u32[]{:S(2)}) copy-start(bf16[256,2048]{1,0:T(8,128)(2,1)} %param.24) | copy-start | bytes 3145732
  291.1 65.6 %copy-start.2 = (bf16[4,2048,128]{2,1,0:T(8,128)(2,1)}, bf16[4,2048,128]{2,1,0:T(8,128)(2,1)S(1)}, u32[]{:S(2)}) copy-start(bf16[4,2048,128]{2,1,0:T(8,128)(2,1)S(1)} %get-tuple-element.39.streams) | copy-start | bytes 6291460
  323.4 23.1 %copy-start.39 = (bf16[4,2,256,128]{3,1,2,0:T(2,128)(2,1)}, bf16[4,2,256,128]{3,1,2,0:T(2,128)(2,1)S(1)}, u32[]{:S(2)}) copy-start(bf16[4,2,256,128]{3,1,2,0:T(2,128)(2,1)S(1)} %copy.162) | copy-start | bytes 1572868
  324.6 17.2 %copy-start.58 = (bf16[2,2,2,256,1024]{4,3,2,1,0:T(8,128)(2,1)S(1)}, bf16[2,2,2,256,1024]{4,3,2,1,0:T(8,128)(2,1)}, u32[]{:S(2)}) copy-start(bf16[2,2,2,256,1024]{4,3,2,1,0:T(8,128)(2,1)} %get-tuple-element.37) | copy-start | bytes 12582916
  341.8 4.7 copy-start.63
  341.8 4.7 copy-start.12
  349.8 6.6 copy-start.52
  349.8 6.7 copy-start.57
  349.8 6.8 copy-start.54
  358.8 78.1 %copy-start.40 = (bf16[4,2,256,128]{3,1,2,0:T(2,128)(2,1)S(1)}, bf16[4,2,256,128]{3,1,2,0:T(2,128)(2,1)}, u32[]{:S(2)}) copy-start(bf16[4,2,256,128]{3,1,2,0:T(2,128)(2,1)} %copy-done.39) | copy-start | bytes 1572868
  358.8 80.4 %copy-start.61 = (f32[1024,1024]{1,0:T(8,128)S(1)}, f32[1024,1024]{1,0:T(8,128)}, u32[]{:S(2)}) copy-start(f32[1024,1024]{1,0:T(8,128)} %get-tuple-element.166) | copy-start | bytes 12582916
  437.0 3.7 copy-start.59
  437.0 4.9 copy-start.60
  447.8 9.1 %copy-start.62 = (bf16[1024,1024]{1,0:T(8,128)(2,1)}, bf16[1024,1024]{1,0:T(8,128)(2,1)S(1)}, u32[]{:S(2)}) copy-start(bf16[1024,1024]{1,0:T(8,128)(2,1)S(1)} %add_convert_fusion.1) | copy-start | bytes 6291460
  447.8 9.1 %copy-start.64 = (bf16[1024,1024]{1,0:T(8,128)(2,1)S(1)}, bf16[1024,1024]{1,0:T(8,128)(2,1)}, u32[]{:S(2)}) copy-start(bf16[1024,1024]{1,0:T(8,128)(2,1)} %copy-done.63) | copy-start | bytes 6291460
  456.9 6.3 copy-start.13
  492.6 9.5 %copy-start.4 = (bf16[3,2,2,2,256,256]{5,4,3,2,1,0:T(8,128)(2,1)S(1)}, bf16[3,2,2,2,256,256]{5,4,3,2,1,0:T(8,128)(2,1)}, u32[]{:S(2)}) copy-start(bf16[3,2,2,2,256,256]{5,4,3,2,1,0:T(8,128)(2,1)} %copy-done.3) | copy-start | bytes 9437188
  831.6 45.2 %copy-start.47 = (bf16[128,4096]{1,0:T(8,128)(2,1)S(1)}, bf16[128,4096]{1,0:T(8,128)(2,1)}, u32[]{:S(2)}) copy-start(bf16[128,4096]{1,0:T(8,128)(2,1)} %get-tuple-element.51) | copy-start | bytes 3145732
  831.7 46.7 %copy-start.46 = (bf16[128,4096]{1,0:T(8,128)(2,1)S(1)}, bf16[128,4096]{1,0:T(8,128)(2,1)}, u32[]{:S(2)}) copy-start(bf16[128,4096]{1,0:T(8,128)(2,1)} %get-tuple-element.52) | copy-start | bytes 3145732
  832.5 3.7 copy-start.51
  878.4 3.7 copy-start.53
  878.4 4.4 copy-start.49
  878.4 6.4 copy-start.17
  878.4 8.5 copy-start.1
  (41 other events, 82.6 us)

commit v2 on v1

--- a/solution.py
+++ b/solution.py
@@ -26,6 +26,7 @@
 F32, BF16 = jnp.float32, jnp.bfloat16
 CORE, SIDE, NEAR, HIGH = 1, 2, 4, 8
 QUARTERS = 4
+UNIT = 256
 
 
 def bit(place, value):
@@ -103,7 +104,7 @@
     o_mix, o_small, o_streams, o_act, o_qkv, o_up, o_down, o_out,
     mix_all, small_all, hist_in, mixed, streams, act,
     early_s, early_r, hist_sem, a2a_s, a2a_r, reshard_s, reshard_r, high_s, high_r, side_s, side_r,
-    act_s, act_r, act_local, own_sem, out_sem,
+    act_s, act_r, act_local, own_sem, out_sem, share_s, share_r,
 ):
     here = Place()
     me, tensor = here.me, here.tensor
@@ -115,12 +116,12 @@
     greet_all(n_dp, me, here.other)
 
     def early(which, buf, phase):
-        if phase < high_bits:
-            span = 1 << phase
-            block = buf.at[pl.ds(lax.div(here.high, span) * span, span), here.near, here.side, here.core]
-            target = flip(me, HIGH << phase)
-        elif phase == high_bits:
-            block, target = buf.at[:, here.near, here.side, here.core], flip(me, NEAR)
+        if phase == 0:
+            block, target = buf.at[here.high, here.near, here.side, here.core], flip(me, NEAR)
+        elif phase <= high_bits:
+            span = 1 << (phase - 1)
+            block = buf.at[pl.ds(lax.div(here.high, span) * span, span), :, here.side, here.core]
+            target = flip(me, HIGH << (phase - 1))
         elif phase == high_bits + 1:
             block, target = buf.at[:, :, here.side, here.core], flip(me, SIDE)
         else:
@@ -131,54 +132,39 @@
         pltpu.make_async_copy(mix, mix_all.at[here.high, here.near, here.side, here.core], own_sem.at[0]),
         pltpu.make_async_copy(small, small_all.at[here.high, here.near, here.side, here.core], own_sem.at[1]),
     ]
-    for copy in own:
-        copy.start()
-    for copy in own:
-        copy.wait()
-    early_pairs = ((0, mix_all), (1, small_all))
-    early(0, mix_all, 0).start()
-    early(1, small_all, 0).start()
-
-    def cut(ref, quarter):
-        width = ref.shape[-1] // QUARTERS
-        columns = at(quarter * width, width)
-        return ref.at[:, :, columns] if len(ref.shape) == 3 else ref.at[:, columns]
-
-    def slot(ref):
-        index = (here.high, here.near, here.side, pl.ds(pl.multiple_of(here.core * rows, rows), rows))
-        return ref.at[(slice(None),) + index] if len(ref.shape) == 6 else ref.at[index]
-
-    def keep(array):
-        w, o = weights[array]
-        return pltpu.make_async_copy(cut(w, here.quarter), slot(o), own_sem.at[2 + array])
-
-    def reshard(array, peer):
-        w, o = weights[array]
+    units = []
+    for w, o in weights:
+        if len(w.shape) == 3:
+            units += [(w.at[part], o.at[part], 0) for part in range(w.shape[0])]
+        else:
+            units += [(w, o, first) for first in range(0, o.shape[-1], UNIT)]
+
+    def cut(unit, quarter):
+        w, o, first = units[unit]
+        return w.at[:, at(quarter * o.shape[-1] + first, UNIT)]
+
+    def slot(unit):
+        _, o, first = units[unit]
+        mine = pl.ds(pl.multiple_of(here.core * rows, rows), rows)
+        return o.at[here.high, here.near, here.side, mine, pl.ds(first, UNIT)]
+
+    def keep(unit):
+        return pltpu.make_async_copy(cut(unit, here.quarter), slot(unit), own_sem.at[2 + unit])
+
+    def reshard(unit, peer):
         target, quarter = here.peers[peer]
-        return remote(cut(w, quarter), slot(o), reshard_s.at[array, peer], reshard_r.at[array, peer], dp=target)
-
-    def high_hop(array, phase):
-        o = weights[array][1]
+        return remote(cut(unit, quarter), slot(unit), reshard_s.at[unit, peer], reshard_r.at[unit, peer], dp=target)
+
+    def high_hop(unit, phase):
+        _, o, first = units[unit]
         span = 1 << phase
-        index = (pl.ds(lax.div(here.high, span) * span, span), slice(None), here.side)
-        block = o.at[(slice(None),) + index] if len(o.shape) == 6 else o.at[index]
-        return remote(block, block, high_s.at[array, phase], high_r.at[array, phase], dp=flip(me, HIGH << phase))
-
-    def side_hop(array):
-        o = weights[array][1]
-        block = o.at[:, :, :, here.side] if len(o.shape) == 6 else o.at[:, :, here.side]
-        return remote(block, block, side_s.at[array], side_r.at[array], dp=flip(me, SIDE))
-
-    for phase in range(1, high_bits + 3):
-        for which, buf in early_pairs:
-            early(which, buf, phase - 1).wait()
-            early(which, buf, phase).start()
-        if phase == 1:
-            for array in range(len(weights)):
-                keep(array).start()
-                for peer in range(3):
-                    reshard(array, peer).start()
-    early(0, mix_all, high_bits + 2).wait()
+        block = o.at[pl.ds(lax.div(here.high, span) * span, span), :, here.side, :, pl.ds(first, UNIT)]
+        return remote(block, block, high_s.at[unit, phase], high_r.at[unit, phase], dp=flip(me, HIGH << phase))
+
+    def side_hop(unit):
+        _, o, first = units[unit]
+        block = o.at[:, :, here.side, :, pl.ds(first, UNIT)]
+        return remote(block, block, side_s.at[unit], side_r.at[unit], dp=flip(me, SIDE))
 
     def fetch(step, buf):
         target = lax.rem(me + step, n_dp)
@@ -217,18 +203,6 @@
         def _():
             send(step).start()
 
-    loop(0, n_dp, mix_step)
-    streams[:, at(me * rows, rows), :] = mixed[0]
-    for array in range(len(weights)):
-        keep(array).wait()
-        for peer in range(3):
-            reshard(array, peer).wait()
-        for phase in range(high_bits):
-            if phase == 0:
-                high_hop(array, 0).start()
-    early(1, small_all, high_bits + 2).wait()
-    loop(1, n_dp, lambda step: send(step).wait())
-
     chunk = min(256, depth)
 
     def lanes(near, core, half_at, count):
@@ -259,7 +233,7 @@
             act_s.at[3 + near, stream], act_r.at[3 + near, stream], dp=flip(me, CORE),
         )
 
-    for stream in range(STREAMS):
+    def normalise_stream(stream):
         block = 0 if stream < 3 else 1
 
         def piece(index):
@@ -288,39 +262,112 @@
             ).astype(BF16)
 
         loop(0, depth // chunk, normalise)
-        act_near(stream).start()
-        act_tensor(stream, 0).start()
         act_keep(stream).start()
 
     finals = [
-        pltpu.make_async_copy(mix_all, o_mix, out_sem.at[0]),
         pltpu.make_async_copy(small_all, o_small, out_sem.at[1]),
         pltpu.make_async_copy(streams, o_streams, out_sem.at[2]),
     ]
-    for copy in finals:
-        copy.start()
-    for array in range(len(weights)):
+    early_pairs = ((0, mix_all), (1, small_all))
+    last = high_bits + 2
+
+    def first(array):
+        keep(array).start()
+        for peer in range(3):
+            reshard(array, peer).start()
+
+    def second(array):
+        keep(array).wait()
+        for peer in range(3):
+            reshard(array, peer).wait()
+        high_hop(array, 0).start()
+
+    def third(array):
         for phase in range(high_bits):
             high_hop(array, phase).wait()
             if phase + 1 < high_bits:
                 high_hop(array, phase + 1).start()
         side_hop(array).start()
-    for stream in range(STREAMS):
+
+    def act_first(stream):
         act_near(stream).wait()
         act_tensor(stream, 1).start()
-    for stream in range(STREAMS):
+        if stream + 1 < STREAMS:
+            act_near(stream + 1).start()
+        if stream and stream + 1 < STREAMS:
+            act_tensor(stream + 1, 0).start()
+
+    def act_second(stream):
         act_keep(stream).wait()
         act_tensor(stream, 0).wait()
         act_tensor(stream, 1).wait()
         for near in range(2):
             act_core(stream, near).start()
-    for array in range(len(weights)):
-        side_hop(array).wait()
+
+    for copy in own:
+        copy.start()
+    for copy in own:
+        copy.wait()
+    for which, buf in early_pairs:
+        early(which, buf, 0).start()
+    total = len(units)
+
+    def tick(unit):
+        third(unit)
+        if unit + 3 < total:
+            first(unit + 3)
+        if unit + 1 < total:
+            second(unit + 1)
+
+    for unit in range(min(3, total)):
+        first(unit)
+    for phase in range(1, last + 1):
+        for which, buf in early_pairs:
+            early(which, buf, phase - 1).wait()
+            early(which, buf, phase).start()
+    early(0, mix_all, last).wait()
+    mix_copy = pltpu.make_async_copy(mix_all, o_mix.at[tensor], out_sem.at[0])
+    mix_share = remote(mix_all, o_mix.at[tensor], share_s.at[0], share_r.at[0], tensor=here.other)
+    mix_copy.start()
+    mix_share.start()
+    second(0)
+    loop(0, n_dp, mix_step)
+    streams[:, at(me * rows, rows), :] = mixed[0]
+    early(1, small_all, last).wait()
+    done = 0
+
+    def ticks(count):
+        nonlocal done
+        for unit in range(done, min(done + count, total)):
+            tick(unit)
+        done = min(done + count, total)
+
+    ticks(3)
+    loop(1, n_dp, lambda step: send(step).wait())
+    for stream in range(STREAMS):
+        normalise_stream(stream)
+        if stream == 0:
+            act_near(0).start()
+        if stream < 2:
+            act_tensor(stream, 0).start()
+    for copy in finals:
+        copy.start()
+    for stream in range(STREAMS):
+        ticks(2)
+        act_first(stream)
+    for stream in range(STREAMS):
+        ticks(1)
+        act_second(stream)
+    ticks(total)
+    for unit in range(total):
+        side_hop(unit).wait()
     for stream in range(STREAMS):
         for near in range(2):
             act_core(stream, near).wait()
     for copy in finals:
         copy.wait()
+    mix_copy.wait()
+    mix_share.wait()
 
 
 def gather(n_dp, hist, mix, small, w_qkv, w_up, w_down, w_out):
@@ -330,12 +377,13 @@
     high = n_dp // HIGH
     high_bits = int(math.log2(high))
     grid = (high, 2, 2, 2)
+    units = sum(w.size // w.shape[-2] for w in (w_qkv, w_up, w_down, w_out)) // QUARTERS // UNIT
 
     def cut(width):
         return (high, 2, 2, 2 * rows, width // QUARTERS)
 
     shapes = [
-        (grid + mix.shape, F32),
+        ((2,) + grid + mix.shape, F32),
         (grid + (rows, 128), BF16),
         ((STREAMS, depth, half), BF16),
         ((STREAMS, depth, 8 * half), BF16),
@@ -361,17 +409,19 @@
             DMA((2,)),
             DMA((n_dp,)),
             DMA((n_dp,)),
-            DMA((4, 3)),
-            DMA((4, 3)),
-            DMA((4, high_bits)),
-            DMA((4, high_bits)),
-            DMA((4,)),
-            DMA((4,)),
+            DMA((units, 3)),
+            DMA((units, 3)),
+            DMA((units, high_bits)),
+            DMA((units, high_bits)),
+            DMA((units,)),
+            DMA((units,)),
             DMA((5, STREAMS)),
             DMA((5, STREAMS)),
             DMA((STREAMS,)),
-            DMA((6,)),
+            DMA((2 + units,)),
             DMA((3,)),
+            DMA((1,)),
+            DMA((1,)),
         ],
         compiler_params=pltpu.CompilerParams(
             collective_id=1, has_side_effects=True, vmem_limit_bytes=40 * 1024 * 1024
@@ -1270,3 +1320,968 @@
         ),
         check_vma=False,
     )
+
+
+def lane_block(half, near, core, half_at, count):
+    return at(near * 4 * half + core * 2 * half + half_at * half, count * half, half)
+
+
+def gelu_parts(values):
+    phi = 0.5 * (1.0 + lax.erf(values * (1.0 / math.sqrt(2.0))))
+    density = jnp.exp(-0.5 * values * values) * (1.0 / math.sqrt(2.0 * math.pi))
+    return values * phi, phi + values * density
+
+
+def reduce_group(here, half, part, theirs, own, from_core, from_tensor, from_near, sems, local, pieces, piece):
+    core_s, core_r, tensor_s, tensor_r, near_s, near_r = sems
+
+    def load(span, near, half_at):
+        return pltpu.make_async_copy(
+            part.at[piece(span), lane_block(half, near, here.core, half_at, 1)],
+            own.at[near, half_at, piece(span)], local.at[span, near * 2 + half_at],
+        )
+
+    def to_core(span, near, half_at):
+        return remote(
+            part.at[piece(span), lane_block(half, near, 1 - here.core, half_at, 1)],
+            from_core.at[near, half_at, piece(span)],
+            core_s.at[span, near * 2 + half_at], core_r.at[span, near * 2 + half_at], dp=flip(here.me, CORE),
+        )
+
+    def to_tensor(span, near):
+        return remote(
+            own.at[near, here.other, piece(span)], from_tensor.at[near, piece(span)],
+            tensor_s.at[span, near], tensor_r.at[span, near], tensor=here.other,
+        )
+
+    def to_near(span):
+        return remote(
+            from_tensor.at[1 - here.near, piece(span)], from_near.at[piece(span)],
+            near_s.at[span], near_r.at[span], dp=flip(here.me, NEAR),
+        )
+
+    def start(span):
+        for near in range(2):
+            for half_at in range(2):
+                to_core(span, near, half_at).start()
+                load(span, near, half_at).start()
+
+    def after_core(span):
+        for near in range(2):
+            for half_at in range(2):
+                load(span, near, half_at).wait()
+                to_core(span, near, half_at).wait()
+            own[near, here.other, piece(span)] += from_core[near, here.other, piece(span)]
+            to_tensor(span, near).start()
+        for near in range(2):
+            own[near, here.tensor, piece(span)] += from_core[near, here.tensor, piece(span)]
+
+    def after_tensor(span):
+        for near in range(2):
+            to_tensor(span, near).wait()
+        far = 1 - here.near
+        from_tensor[far, piece(span)] += own[far, here.tensor, piece(span)]
+        to_near(span).start()
+        from_tensor[here.near, piece(span)] += own[here.near, here.tensor, piece(span)]
+
+    def after_near(span):
+        to_near(span).wait()
+
+    return start, after_core, after_tensor, after_near
+
+
+def join_kernel(
+    part, streams, cot, small, mix_in, mix_out, mix_back, static, next_cot,
+    o_grad, o_wide, o_block, o_next, o_mixin, o_tiny,
+    own, from_core, from_tensor, from_near, residual, wide, normed, block, back, low, next_rows, mixin, tiny,
+    core_s, core_r, tensor_s, tensor_r, near_s, near_r, local, share_s, share_r, own_sem,
+):
+    here = Place()
+    me, tensor = here.me, here.tensor
+    depth, half = cot.shape
+    spans = core_s.shape[0]
+    size = depth // spans
+    chunk = 256
+    greet([{"dp": flip(me, CORE)}, {"dp": flip(me, NEAR)}, {"tensor": here.other}])
+
+    def piece(span):
+        return pl.ds(span * size, size)
+
+    start, after_core, after_tensor, after_near = reduce_group(
+        here, half, part, None, own, from_core, from_tensor, from_near,
+        (core_s, core_r, tensor_s, tensor_r, near_s, near_r), local, spans, piece,
+    )
+    fetch = pltpu.make_async_copy(streams.at[3], residual, own_sem.at[0])
+    fetch.start()
+    for span in range(spans):
+        start(span)
+    for span in range(spans):
+        after_core(span)
+    for span in range(spans):
+        after_tensor(span)
+    fetch.wait()
+    squares = jnp.zeros((1, half), F32)
+    for span in range(spans):
+        after_near(span)
+
+        def widen(index, total):
+            rows = at(span * size + index * chunk, chunk)
+            branch = from_tensor[here.near, rows, :].astype(F32) + from_near[rows, :].astype(F32)
+            value = residual[rows, :].astype(F32) + branch
+            wide[rows, :] = value
+            block[rows, :] = value.astype(BF16)
+            return total + jnp.sum(value * value, axis=0, keepdims=True)
+
+        squares = lax.fori_loop(0, size // chunk, widen, squares)
+    root = lax.rsqrt(squares / depth + ROOT_EPS)
+
+    def share_block(which):
+        lanes = at(tensor * half, half)
+        if which == 0:
+            return pltpu.make_async_copy(block, o_block.at[:, lanes], own_sem.at[1])
+        return remote(block, o_block.at[:, lanes], share_s.at[0], share_r.at[0], tensor=here.other)
+
+    share_block(0).start()
+    share_block(1).start()
+
+    def norm(index):
+        rows = at(index * chunk, chunk)
+        normed[rows, :] = (wide[rows, :] * root).astype(BF16)
+
+    loop(0, depth // chunk, norm)
+    inner, slope = gelu_parts(jnp.dot(mix_in[...], normed[...], preferred_element_type=F32))
+    inner_low = inner.astype(BF16)
+    next_rows[...] = (jnp.dot(mix_out[...], inner_low, preferred_element_type=F32) + static[...])[:MIXH]
+    next_low = next_cot[...].astype(BF16)
+
+    def nt(left, right):
+        return lax.dot_general(left, right, (((1,), (1,)), ((), ())), preferred_element_type=F32)
+
+    column = lax.broadcasted_iota(jnp.int32, (128, 128), 1)
+    static_grad = jnp.sum(next_cot[...], axis=1, keepdims=True)
+    tiny[...] = jnp.where(column == MIXH, static_grad, nt(inner_low, next_low))[:MIXH]
+    inner_grad = (jnp.dot(mix_back[...], next_low, preferred_element_type=F32) * slope).astype(BF16)
+
+    def pull(index, total):
+        rows = at(index * chunk, chunk)
+        value = jnp.dot(small[rows, :], inner_grad, preferred_element_type=F32)
+        back[rows, :] = value
+        return total + jnp.sum(value * wide[rows, :] * root, axis=0, keepdims=True)
+
+    along = lax.fori_loop(0, depth // chunk, pull, jnp.zeros((1, half), F32)) / depth
+
+    def finish(index):
+        rows = at(index * chunk, chunk)
+        value = cot[rows, :].astype(F32) + root * (back[rows, :] - wide[rows, :] * root * along)
+        back[rows, :] = value
+        low[rows, :] = value.astype(BF16)
+
+    loop(0, depth // chunk, finish)
+
+    def share(kind, index):
+        if kind == 0:
+            source, lanes, where = low, lane_block(half, here.near, here.core, tensor, 1), {"dp": flip(me, NEAR)}
+        elif kind == 1:
+            lanes = lane_block(half, 1 - here.near if index else here.near, here.core, tensor, 1)
+            source, where = (o_grad.at[:, lanes] if index else low), {"tensor": here.other}
+        else:
+            lanes, where = lane_block(half, index, here.core, 0, 2), {"dp": flip(me, CORE)}
+            source = o_grad.at[:, lanes]
+        number = 1 + 2 * kind + index
+        return remote(source, o_grad.at[:, lanes], share_s.at[number], share_r.at[number], **where)
+
+    share(0, 0).start()
+    share(1, 0).start()
+    keep = pltpu.make_async_copy(
+        low, o_grad.at[:, lane_block(half, here.near, here.core, tensor, 1)], own_sem.at[2]
+    )
+    keep.start()
+
+    def mixin_rows(index):
+        rows = at(index * chunk, chunk)
+        mixin[rows, :] = nt(normed[rows, :], inner_grad)
+
+    loop(0, depth // chunk, mixin_rows)
+    share(0, 0).wait()
+    share(1, 1).start()
+    lanes = at(tensor * half, half)
+    next_share = remote(next_rows, o_next.at[:, lanes], share_s.at[7], share_r.at[7], tensor=here.other)
+    next_share.start()
+    finals = [
+        pltpu.make_async_copy(next_rows, o_next.at[:, lanes], own_sem.at[3]),
+        pltpu.make_async_copy(back, o_wide, own_sem.at[4]),
+        pltpu.make_async_copy(mixin, o_mixin, own_sem.at[5]),
+        pltpu.make_async_copy(tiny, o_tiny, own_sem.at[6]),
+    ]
+    for copy in finals:
+        copy.start()
+    keep.wait()
+    share(1, 0).wait()
+    share(1, 1).wait()
+    for near in range(2):
+        share(2, near).start()
+    for near in range(2):
+        share(2, near).wait()
+    share_block(0).wait()
+    share_block(1).wait()
+    next_share.wait()
+    for copy in finals:
+        copy.wait()
+
+
+def join(part, streams, cot, small, mix_in, mix_out, mix_back, static, next_cot):
+    depth, half = cot.shape
+    spans = 4
+    shapes = [
+        ((depth, 8 * half), BF16),
+        ((depth, half), F32),
+        ((depth, 2 * half), BF16),
+        ((MIXH, 2 * half), F32),
+        ((depth, 128), F32),
+        ((MIXH, 128), F32),
+    ]
+    return pl.pallas_call(
+        join_kernel,
+        out_shape=[jax.ShapeDtypeStruct(*shape) for shape in shapes],
+        in_specs=[ANY, ANY] + [VM] * 7,
+        out_specs=[ANY] * 6,
+        scratch_shapes=[
+            pltpu.VMEM((2, 2, depth, half), BF16),
+            pltpu.VMEM((2, 2, depth, half), BF16),
+            pltpu.VMEM((2, depth, half), BF16),
+            pltpu.VMEM((depth, half), BF16),
+            pltpu.VMEM((depth, half), BF16),
+            pltpu.VMEM((depth, half), F32),
+            pltpu.VMEM((depth, half), BF16),
+            pltpu.VMEM((depth, half), BF16),
+            pltpu.VMEM((depth, half), F32),
+            pltpu.VMEM((depth, half), BF16),
+            pltpu.VMEM((MIXH, half), F32),
+            pltpu.VMEM((depth, 128), F32),
+            pltpu.VMEM((MIXH, 128), F32),
+            DMA((spans, 4)),
+            DMA((spans, 4)),
+            DMA((spans, 2)),
+            DMA((spans, 2)),
+            DMA((spans,)),
+            DMA((spans,)),
+            DMA((spans, 4)),
+            DMA((8,)),
+            DMA((8,)),
+            DMA((7,)),
+        ],
+        compiler_params=pltpu.CompilerParams(
+            collective_id=2, has_side_effects=True, vmem_limit_bytes=40 * 1024 * 1024
+        ),
+        name="join",
+    )(part, streams, cot, small, mix_in, mix_out, mix_back, static, next_cot)
+
+
+def scatter_kernel(
+    n_dp, attn_grad, mlp_grad, streams, small, wide_grad, mixin_part, mix_tiny, hist, g_qkv, g_up, g_down, g_out,
+    o_stream, o_mix, o_small, o_tiny, o_qkv, o_up, o_down, o_out,
+    own, from_core, from_tensor, from_near, rows_in, wide, stream_grad, gains, biases, tiny, tiny_in, tiny_out,
+    hist_in, arrived, mix_part, mix_in, mix_sum, tiny_sum, ring, side_in, mine, high_in,
+    core_s, core_r, tensor_s, tensor_r, near_s, near_r, local, in_sem,
+    side_s, side_r, side_local, high_s, high_r, peer_s, peer_r, peer_local,
+    a2a_s, a2a_r, a2a_own, keep_sem, pass_s, pass_r, tiny_s, tiny_r, mix_s, mix_r, hist_sem,
+    ring_s, ring_r, last_s, last_r, last_local,
+):
+    here = Place()
+    me, tensor = here.me, here.tensor
+    depth, half = wide_grad.shape
+    rows = depth // n_dp
+    high_bits = int(math.log2(n_dp // HIGH))
+    chunk = min(256, depth)
+    greet_all(n_dp, me, here.other)
+
+    units = []
+    for g, o in ((g_qkv, o_qkv), (g_up, o_up), (g_down, o_down), (g_out, o_out)):
+        if len(o.shape) == 3:
+            units += [(g.at[part], o.at[part], 0) for part in range(o.shape[0])]
+        else:
+            units += [(g, o, first) for first in range(0, g.shape[-1], UNIT)]
+    total = len(units)
+
+    def side_hop(unit):
+        g, _, first = units[unit]
+        return remote(
+            g.at[:, :, 1 - here.side, :, pl.ds(first, UNIT)], side_in.at[unit], side_s.at[unit], side_r.at[unit],
+            dp=flip(me, SIDE),
+        )
+
+    def side_load(unit):
+        g, _, first = units[unit]
+        return pltpu.make_async_copy(
+            g.at[:, :, here.side, :, pl.ds(first, UNIT)], mine.at[unit], side_local.at[unit]
+        )
+
+    def high_hop(unit, phase):
+        span = 1 << phase
+        base = lax.div(here.high, span)
+        theirs = base + 1 - 2 * lax.rem(base, 2)
+        return remote(
+            mine.at[unit, pl.ds(theirs * span, span)], high_in.at[unit, pl.ds(span - 1, span)],
+            high_s.at[unit, phase], high_r.at[unit, phase], dp=flip(me, HIGH << phase),
+        )
+
+    def peer_hop(unit, peer):
+        _, o, first = units[unit]
+        target, _ = here.peers[peer]
+        return remote(
+            mine.at[unit, here.high, bit(target, NEAR), at(bit(target, CORE) * rows, rows)],
+            o.at[:, at(here.quarter * (o.shape[-1] // QUARTERS) + first, UNIT)],
+            peer_s.at[unit, peer], peer_r.at[unit, peer], dp=target,
+        )
+
+    def peer_keep(unit):
+        _, o, first = units[unit]
+        return pltpu.make_async_copy(
+            mine.at[unit, here.high, here.near, at(here.core * rows, rows)],
+            o.at[:, at(here.quarter * (o.shape[-1] // QUARTERS) + first, UNIT)], peer_local.at[unit],
+        )
+
+    def add_blocks(unit, other, first_mine, first_other, count):
+        tall = 2 * rows
+        step = min(64, tall)
+
+        def add(flat):
+            high, rest = lax.div(flat, 2 * (tall // step)), lax.rem(flat, 2 * (tall // step))
+            near, span = lax.div(rest, tall // step), at(lax.rem(rest, tall // step) * step, step)
+            mine[unit, first_mine + high, near, span] += other[unit, first_other + high, near, span]
+
+        loop(0, count * 2 * (tall // step), add)
+
+    def side_start(unit):
+        side_hop(unit).start()
+        side_load(unit).start()
+
+    def finish_high(unit):
+        for phase in reversed(range(high_bits)):
+            high_hop(unit, phase).wait()
+            span = 1 << phase
+            add_blocks(unit, high_in, lax.div(here.high, span) * span, span - 1, span)
+            if phase:
+                high_hop(unit, phase - 1).start()
+        peer_keep(unit).start()
+        for peer in range(3):
+            peer_hop(unit, peer).start()
+
+    def tick(unit):
+        side_load(unit).wait()
+        side_hop(unit).wait()
+        if unit + 2 < total:
+            side_start(unit + 2)
+        add_blocks(unit, side_in, 0, 0, n_dp // HIGH)
+        if unit:
+            finish_high(unit - 1)
+        high_hop(unit, high_bits - 1).start()
+
+    done = 0
+
+    def ticks(count):
+        nonlocal done
+        for unit in range(done, min(done + count, total)):
+            tick(unit)
+        done = min(done + count, total)
+
+    def load(stream, near, half_at):
+        part = attn_grad.at[stream] if stream < 3 else mlp_grad
+        return pltpu.make_async_copy(
+            part.at[:, lane_block(half, near, here.core, half_at, 1)], own.at[stream, near, half_at],
+            local.at[stream, near * 2 + half_at],
+        )
+
+    def to_core(stream, near, half_at):
+        part = attn_grad.at[stream] if stream < 3 else mlp_grad
+        return remote(
+            part.at[:, lane_block(half, near, 1 - here.core, half_at, 1)], from_core.at[stream, near, half_at],
+            core_s.at[stream, near * 2 + half_at], core_r.at[stream, near * 2 + half_at], dp=flip(me, CORE),
+        )
+
+    def to_tensor(stream, near):
+        return remote(
+            own.at[stream, near, here.other], from_tensor.at[stream, near],
+            tensor_s.at[stream, near], tensor_r.at[stream, near], tensor=here.other,
+        )
+
+    def to_near(stream):
+        return remote(
+            from_tensor.at[stream, 1 - here.near], from_near.at[stream], near_s.at[stream], near_r.at[stream],
+            dp=flip(me, NEAR),
+        )
+
+    def after_core(stream):
+        for near in range(2):
+            for half_at in range(2):
+                load(stream, near, half_at).wait()
+                to_core(stream, near, half_at).wait()
+
+        def add(index):
+            span = at(index * chunk, chunk)
+            for near in range(2):
+                for half_at in range(2):
+                    own[stream, near, half_at, span] += from_core[stream, near, half_at, span]
+
+        loop(0, depth // chunk, add)
+
+    def after_tensor(stream):
+        for near in range(2):
+            to_tensor(stream, near).wait()
+
+        def add(index):
+            span = at(index * chunk, chunk)
+            for near in range(2):
+                from_tensor[stream, near, span] += own[stream, near, tensor, span]
+
+        loop(0, depth // chunk, add)
+        to_near(stream).start()
+
+    stats = []
+
+    def measure(stream):
+        def piece(index):
+            return rows_in[stream, at(index * chunk, chunk), :].astype(F32)
+
+        centre = sum_rows(piece, depth, chunk, lambda v: v) / depth
+        spread = sum_rows(piece, depth, chunk, lambda v: (v - centre) * (v - centre)) / depth
+        stats.append((centre, lax.rsqrt(spread + NORM_EPS)))
+
+    def back_norm(stream):
+        to_near(stream).wait()
+        group = 0 if stream < 3 else 1
+        centre, root = stats[stream]
+
+        def parts(index):
+            span = at(index * chunk, chunk)
+            grad = from_tensor[stream, here.near, span].astype(F32) + from_near[stream, span].astype(F32)
+            hat = (rows_in[stream, span, :].astype(F32) - centre) * root
+            gain = small[span, MIXH + group : MIXH + group + 1].astype(F32)
+            return span, grad, hat, grad * gain
+
+        def sums(index, carry):
+            span, grad, hat, scaled = parts(index)
+            if stream in (0, 3):
+                gains[group, span] = grad * hat
+                biases[group, span] = grad
+            else:
+                gains[group, span] += grad * hat
+                biases[group, span] += grad
+            return (
+                carry[0] + jnp.sum(scaled, axis=0, keepdims=True),
+                carry[1] + jnp.sum(scaled * hat, axis=0, keepdims=True),
+            )
+
+        zero = jnp.zeros((1, half), F32)
+        whole, along = lax.fori_loop(0, depth // chunk, sums, (zero, zero))
+
+        def finish(index):
+            span, _, hat, scaled = parts(index)
+            value = root * (scaled - whole / depth - hat * (along / depth))
+            if stream == 3:
+                value = value + wide[span, :]
+            stream_grad[stream, span] = value.astype(BF16)
+
+        loop(0, depth // chunk, finish)
+        loop(1, n_dp, lambda step: send(stream, step).start())
+        send_own(stream).start()
+
+    def send(stream, step):
+        target = lax.rem(me + step, n_dp)
+        return remote(
+            stream_grad.at[stream, at(target * rows, rows), :], arrived.at[stream, step],
+            a2a_s.at[stream, step], a2a_r.at[stream, step], dp=target,
+        )
+
+    def send_own(stream):
+        return pltpu.make_async_copy(
+            stream_grad.at[stream, at(me * rows, rows), :], arrived.at[stream, 0], a2a_own.at[stream]
+        )
+
+    def source_of(step):
+        return lax.rem(me - step + n_dp, n_dp)
+
+    def lanes_of(step):
+        return at(source_of(step) * 2 * half + tensor * half, half)
+
+    def fetch(step):
+        return pltpu.make_async_copy(hist.at[:, :, lanes_of(step)], hist_in.at[step], hist_sem.at[step])
+
+    def keep(stream, step):
+        return pltpu.make_async_copy(
+            arrived.at[stream, step], o_stream.at[stream, :, lanes_of(step)], keep_sem.at[stream, step]
+        )
+
+    def pass_on(stream, step):
+        return remote(
+            arrived.at[stream, step], o_stream.at[stream, :, lanes_of(step)],
+            pass_s.at[stream, step], pass_r.at[stream, step], tensor=here.other,
+        )
+
+    def mix_send(step):
+        return remote(mix_part.at[step], mix_in.at[step], mix_s.at[step], mix_r.at[step], dp=source_of(step))
+
+    def receive(stream):
+        send_own(stream).wait()
+
+        def one(step):
+            @pl.when(step > 0)
+            def _():
+                send(stream, step).wait()
+
+            keep(stream, step).start()
+            pass_on(stream, step).start()
+            if stream == 0:
+                fetch(step).wait()
+            totals = [jnp.zeros((8, half), F32) for _ in range(HIST)]
+            for row in range(0, rows, 16):
+                span = pl.ds(row, 16)
+                grad = arrived[stream, step, span, :].astype(F32)
+                for source in range(HIST):
+                    product = grad * hist_in[step, source, span, :].astype(F32)
+                    totals[source] = totals[source] + product[:8] + product[8:]
+            for source in range(HIST):
+                mix_part[step, pl.ds(stream * HIST + source, 1), :] = jnp.sum(totals[source], axis=0, keepdims=True)
+            if stream == STREAMS - 1:
+
+                @pl.when(step > 0)
+                def _():
+                    mix_send(step).start()
+
+        loop(0, n_dp, one)
+
+    ring_targets = [{"dp": flip(me, value)} for value in (CORE, SIDE, NEAR)]
+    ring_targets += [{"dp": flip(me, HIGH << phase)} for phase in range(high_bits)]
+    ring_targets.append({"tensor": here.other})
+    hops = len(ring_targets)
+
+    def ring_hop(hop):
+        return remote(ring.at[hop, 0], ring.at[hop, 1], ring_s.at[hop], ring_r.at[hop], **ring_targets[hop])
+
+    def ring_step(hop):
+        ring_hop(hop).wait()
+        ring[hop + 1, 0] = ring[hop, 0] + ring[hop, 1]
+        if hop + 1 < hops:
+            ring_hop(hop + 1).start()
+
+    side_start(0)
+    for stream in range(STREAMS):
+        for near in range(2):
+            for half_at in range(2):
+                to_core(stream, near, half_at).start()
+                load(stream, near, half_at).start()
+        if stream == 0:
+            side_start(1)
+    loads = [
+        pltpu.make_async_copy(streams, rows_in, in_sem.at[0]),
+        pltpu.make_async_copy(wide_grad, wide, in_sem.at[1]),
+        pltpu.make_async_copy(mix_tiny, ring.at[0, 0], in_sem.at[2]),
+    ]
+    for copy in loads:
+        copy.start()
+    after_core(0)
+    for near in range(2):
+        to_tensor(0, near).start()
+    for copy in loads:
+        copy.wait()
+    ring_hop(0).start()
+    loop(0, n_dp, lambda step: fetch(step).start())
+    mix_part[...] = jnp.zeros_like(mix_part)
+    for stream in range(STREAMS):
+        measure(stream)
+    for stream in range(1, STREAMS):
+        after_core(stream)
+    ring_step(0)
+    for stream in range(STREAMS):
+        ticks(2)
+        after_tensor(stream)
+        if stream + 1 < STREAMS:
+            for near in range(2):
+                to_tensor(stream + 1, near).start()
+            if stream + 1 < hops:
+                ring_step(stream + 1)
+        if stream > 0:
+            back_norm(stream - 1)
+        if stream > 1:
+            receive(stream - 2)
+    back_norm(STREAMS - 1)
+
+    column = lax.broadcasted_iota(jnp.int32, (chunk, 128), 1)
+    pltpu.make_async_copy(mixin_part, wide, in_sem.at[0]).start()
+    pltpu.make_async_copy(mixin_part, wide, in_sem.at[0]).wait()
+
+    def gather_tiny(index):
+        span = at(index * chunk, chunk)
+        value = wide[span, :]
+        for group in range(2):
+            gain = jnp.sum(gains[group, span], axis=1, keepdims=True)
+            bias = jnp.sum(biases[group, span], axis=1, keepdims=True)
+            value = jnp.where(column == MIXH + group, gain, value)
+            value = jnp.where(column == MIXH + 2 + group, bias, value)
+        tiny[span, :] = value.astype(BF16)
+
+    loop(0, depth // chunk, gather_tiny)
+
+    def tiny_send(step):
+        target = lax.rem(me + step, n_dp)
+        return remote(tiny.at[at(target * rows, rows), :], tiny_in.at[step], tiny_s.at[step], tiny_r.at[step], dp=target)
+
+    loop(1, n_dp, lambda step: tiny_send(step).start())
+    receive(2)
+    ticks(2)
+    receive(3)
+    for hop in range(STREAMS, hops):
+        ring_step(hop)
+    tiny_final = pltpu.make_async_copy(ring.at[hops, 0], o_tiny, last_local.at[0])
+    tiny_final.start()
+    ticks(total)
+
+    tiny_sum[0] = tiny[at(me * rows, rows), :].astype(F32)
+
+    def add_tiny(step):
+        tiny_send(step).wait()
+        tiny_sum[0] += tiny_in[step].astype(F32)
+
+    loop(1, n_dp, add_tiny)
+    tiny_share = remote(tiny_sum.at[0], tiny_sum.at[1], last_s.at[1], last_r.at[1], tensor=here.other)
+    tiny_share.start()
+    mix_sum[...] = mix_part[0]
+
+    def add_mix(step):
+        mix_send(step).wait()
+        mix_sum[...] += mix_in[step]
+
+    loop(1, n_dp, add_mix)
+    lanes = at(tensor * half, half)
+    mix_share = remote(mix_sum, o_mix.at[:, lanes], last_s.at[0], last_r.at[0], tensor=here.other)
+    mix_keep = pltpu.make_async_copy(mix_sum, o_mix.at[:, lanes], last_local.at[1])
+    mix_share.start()
+    mix_keep.start()
+    finish_high(total - 1)
+    tiny_share.wait()
+    tiny_out[...] = tiny_sum[0] + tiny_sum[1]
+    tiny_keep = pltpu.make_async_copy(tiny_out, o_small, last_local.at[2])
+    tiny_keep.start()
+    for unit in range(total):
+        peer_keep(unit).wait()
+        for peer in range(3):
+            peer_hop(unit, peer).wait()
+
+    def settle(step):
+        for stream in range(STREAMS):
+            keep(stream, step).wait()
+            pass_on(stream, step).wait()
+
+    loop(0, n_dp, settle)
+    mix_share.wait()
+    mix_keep.wait()
+    tiny_keep.wait()
+    tiny_final.wait()
+
+
+def scatter(
+    n_dp, attn_grad, mlp_grad, streams, small, wide_grad, mixin_part, mix_tiny, hist, g_qkv, g_up, g_down, g_out
+):
+    depth, half = wide_grad.shape
+    rows = depth // n_dp
+    high = n_dp // HIGH
+    high_bits = int(math.log2(high))
+    grads = (g_qkv, g_up, g_down, g_out)
+    units = sum(g.size for g in grads) // depth // UNIT
+    hops = high_bits + 4
+
+    outs = [
+        ((STREAMS, rows, 2 * half * n_dp), BF16),
+        ((MIXH, 2 * half), F32),
+        ((rows, 128), F32),
+        (mix_tiny.shape, F32),
+    ] + [((3,) * (g.ndim == 6) + (rows, QUARTERS * g.shape[-1]), BF16) for g in grads]
+    return pl.pallas_call(
+        functools.partial(scatter_kernel, n_dp),
+        out_shape=[jax.ShapeDtypeStruct(*shape) for shape in outs],
+        in_specs=[ANY, ANY, ANY, VM, ANY, ANY, ANY, ANY] + [ANY] * 4,
+        out_specs=[ANY] * 8,
+        scratch_shapes=[
+            pltpu.VMEM((STREAMS, 2, 2, depth, half), BF16),
+            pltpu.VMEM((STREAMS, 2, 2, depth, half), BF16),
+            pltpu.VMEM((STREAMS, 2, depth, half), BF16),
+            pltpu.VMEM((STREAMS, depth, half), BF16),
+            pltpu.VMEM((STREAMS, depth, half), BF16),
+            pltpu.VMEM((depth, half), F32),
+            pltpu.VMEM((STREAMS, depth, half), BF16),
+            pltpu.VMEM((2, depth, half), F32),
+            pltpu.VMEM((2, depth, half), F32),
+            pltpu.VMEM((depth, 128), BF16),
+            pltpu.VMEM((n_dp, rows, 128), BF16),
+            pltpu.VMEM((rows, 128), F32),
+            pltpu.VMEM((n_dp, HIST, rows, half), BF16),
+            pltpu.VMEM((STREAMS, n_dp, rows, half), BF16),
+            pltpu.VMEM((n_dp, MIXH, half), F32),
+            pltpu.VMEM((n_dp, MIXH, half), F32),
+            pltpu.VMEM((MIXH, half), F32),
+            pltpu.VMEM((2, rows, 128), F32),
+            pltpu.VMEM((hops + 1, 2) + mix_tiny.shape, F32),
+            pltpu.VMEM((units, high, 2, 2 * rows, UNIT), BF16),
+            pltpu.VMEM((units, high, 2, 2 * rows, UNIT), BF16),
+            pltpu.VMEM((units, high - 1, 2, 2 * rows, UNIT), BF16),
+            DMA((STREAMS, 4)),
+            DMA((STREAMS, 4)),
+            DMA((STREAMS, 2)),
+            DMA((STREAMS, 2)),
+            DMA((STREAMS,)),
+            DMA((STREAMS,)),
+            DMA((STREAMS, 4)),
+            DMA((3,)),
+            DMA((units,)),
+            DMA((units,)),
+            DMA((units,)),
+            DMA((units, high_bits)),
+            DMA((units, high_bits)),
+            DMA((units, 3)),
+            DMA((units, 3)),
+            DMA((units,)),
+            DMA((STREAMS, n_dp)),
+            DMA((STREAMS, n_dp)),
+            DMA((STREAMS,)),
+            DMA((STREAMS, n_dp)),
+            DMA((STREAMS, n_dp)),
+            DMA((STREAMS, n_dp)),
+            DMA((n_dp,)),
+            DMA((n_dp,)),
+            DMA((n_dp,)),
+            DMA((n_dp,)),
+            DMA((n_dp,)),
+            DMA((hops,)),
+            DMA((hops,)),
+            DMA((2,)),
+            DMA((2,)),
+            DMA((3,)),
+        ],
+        compiler_params=pltpu.CompilerParams(
+            collective_id=3, has_side_effects=True, vmem_limit_bytes=62 * 1024 * 1024
+        ),
+        name="scatter",
+    )(attn_grad, mlp_grad, streams, small, wide_grad, mixin_part, mix_tiny, hist, *grads)
+
+
+def exact_gelu(values):
+    return jax.nn.gelu(values, approximate=False)
+
+
+def rotary_tables(length, rotary, float_type):
+    half_rot = rotary // 2
+    places = jnp.arange(length).astype(float_type)
+    frequency = jnp.exp(
+        jnp.arange(half_rot).astype(float_type) * (-2.0 * math.log(10000.0) / rotary)
+    )
+    angles = places[:, None] * frequency[None, :]
+    return (jnp.cos(angles), jnp.sin(angles))
+
+
+def rotate(values, cos_table, sin_table):
+    half_rot = cos_table.shape[-1]
+    first_half = values[..., :half_rot]
+    second = values[..., half_rot : 2 * half_rot]
+    return jnp.concatenate(
+        [
+            first_half * cos_table - second * sin_table,
+            second * cos_table + first_half * sin_table,
+            values[..., 2 * half_rot :],
+        ],
+        axis=-1,
+    )
+
+
+def masked_scores(queries, key_rows):
+    length = queries.shape[1]
+    score_scale = 1.0 / math.sqrt(queries.shape[2])
+    causal = lax.broadcasted_iota(jnp.int32, (length, length), 0) >= lax.broadcasted_iota(
+        jnp.int32, (length, length), 1
+    )
+    scores = (
+        jnp.einsum("hqd,hkd->hqk", queries, key_rows, preferred_element_type=jnp.float32)
+        * score_scale
+    )
+    return (jnp.where(causal[None], scores, MASKED), score_scale)
+
+
+def attend_forward(queries, key_rows, value_rows):
+    scores, score_scale = masked_scores(queries, key_rows)
+    row_peak = jnp.max(scores, axis=-1, keepdims=True)
+    raised = jnp.exp(scores - row_peak)
+    row_total = jnp.sum(raised, axis=-1, keepdims=True)
+    prob_low = (raised / row_total).astype(jnp.bfloat16)
+    context = jnp.einsum("hqk,hkd->hqd", prob_low, value_rows, preferred_element_type=jnp.float32)
+    return (context.astype(jnp.bfloat16), row_peak + jnp.log(row_total))
+
+
+def attend_backward(queries, key_rows, value_rows, log_sum, context_grad):
+    scores, score_scale = masked_scores(queries, key_rows)
+    attn_prob = jnp.exp(scores - log_sum)
+    prob_low = attn_prob.astype(jnp.bfloat16)
+    value_grad = jnp.einsum(
+        "hqk,hqd->hkd", prob_low, context_grad, preferred_element_type=jnp.float32
+    )
+    prob_grad = jnp.einsum(
+        "hqd,hkd->hqk", context_grad, value_rows, preferred_element_type=jnp.float32
+    )
+    inner_sum = jnp.sum(attn_prob * prob_grad, axis=-1, keepdims=True)
+    score_grad = (attn_prob * (prob_grad - inner_sum)).astype(jnp.bfloat16)
+    query_grad = (
+        jnp.einsum("hqk,hkd->hqd", score_grad, key_rows, preferred_element_type=jnp.float32)
+        * score_scale
+    )
+    key_grad = (
+        jnp.einsum("hqk,hqd->hkd", score_grad, queries, preferred_element_type=jnp.float32)
+        * score_scale
+    )
+    return (query_grad, key_grad, value_grad)
+
+
+def per_device(
+    n_dp, history, mix_weights, w_qkv, w_out, w_up, w_down, norm_gain, norm_bias, mix_in, mix_out, mix_static,
+    out_cot, next_cot,
+):
+    tensor = lax.axis_index("tensor")
+    seq_len = mix_weights.shape[0]
+    half = seq_len // 2
+    depth = mix_in.shape[0] * n_dp
+
+    def own_half(rows):
+        return lax.dynamic_slice_in_dim(rows, tensor * half, half, 0)
+
+    mix_rows = jnp.pad(own_half(mix_weights.reshape(seq_len, -1)).T, ((0, MIXH - STREAMS * HIST), (0, 0)))
+    small = jnp.concatenate([mix_in, norm_gain.T, norm_bias.T], axis=1)
+    small = jnp.pad(small, ((0, 0), (0, 128 - small.shape[1])))
+    mix_all, small_all, streams, act, qkv, up, down, out = gather(
+        n_dp, history, mix_rows, small, w_qkv, w_up, w_down, w_out
+    )
+    small_all = small_all.reshape(depth, 128)
+    qkv, up, down, out = (
+        qkv.reshape(3, depth, -1), up.reshape(depth, -1), down.reshape(depth, -1), out.reshape(depth, -1)
+    )
+    tokens = act.shape[2]
+    seqs = tokens // seq_len
+    heads = qkv.shape[2] // HD
+    projected = jnp.einsum("sdt,sde->ste", act[:3], qkv, preferred_element_type=F32)
+    head_rows = jnp.transpose(projected.reshape(3, seqs, seq_len, heads, HD), (0, 1, 3, 2, 4)).reshape(
+        3, seqs * heads, seq_len, HD
+    )
+    cos_table, sin_table = rotary_tables(seq_len, ROT, F32)
+    queries = rotate(head_rows[0], cos_table, sin_table).astype(BF16)
+    key_rows = rotate(head_rows[1], cos_table, sin_table).astype(BF16)
+    value_rows = head_rows[2].astype(BF16)
+    context, log_sum = attend_forward(queries, key_rows, value_rows)
+
+    def join_heads(rows):
+        return jnp.transpose(rows.reshape(seqs, heads, seq_len, HD), (0, 2, 1, 3)).reshape(tokens, heads * HD)
+
+    context_rows = join_heads(context)
+    up_pre = jnp.einsum("dt,df->tf", act[3], up, preferred_element_type=F32)
+    hidden_wide, gelu_back = jax.vjp(exact_gelu, up_pre)
+    hidden = hidden_wide.astype(BF16)
+    part = (
+        jnp.einsum("de,te->dt", out, context_rows, preferred_element_type=F32)
+        + jnp.einsum("df,tf->dt", down, hidden, preferred_element_type=F32)
+    ).astype(BF16)
+
+    def square(values):
+        return jnp.pad(values, ((0, 128 - values.shape[0]), (0, 128 - values.shape[1])))
+
+    next_rows = own_half(next_cot.reshape(seq_len, -1)).T
+    next_rows = jnp.pad(next_rows, ((0, 128 - next_rows.shape[0]), (0, 0)))
+    mix_in_rows = jnp.pad(small_all[:, :MIXH].T, ((0, 128 - MIXH), (0, 0)))
+    static = jnp.pad(mix_static[:, None], ((0, 128 - mix_static.shape[0]), (0, 0)))
+    branch_grad, wide_grad, block, next_mix, mixin_part, tiny = join(
+        part, streams, own_half(out_cot).T, small_all, mix_in_rows, square(mix_out.T), square(mix_out), static,
+        next_rows,
+    )
+    hidden_grad = jnp.einsum("dt,df->tf", branch_grad, down, preferred_element_type=F32)
+    up_grad_low = gelu_back(hidden_grad)[0].astype(BF16)
+    mlp_in_grad = jnp.einsum("df,tf->dt", up, up_grad_low, preferred_element_type=F32).astype(BF16)
+    context_grad_rows = jnp.einsum("dt,de->te", branch_grad, out, preferred_element_type=F32).astype(BF16)
+    context_grad = jnp.transpose(context_grad_rows.reshape(seqs, seq_len, heads, HD), (0, 2, 1, 3)).reshape(
+        seqs * heads, seq_len, HD
+    )
+    query_grad, key_grad, value_grad = attend_backward(queries, key_rows, value_rows, log_sum, context_grad)
+    proj_grad = jnp.stack(
+        [
+            join_heads(rotate(query_grad, cos_table, -sin_table).astype(BF16)),
+            join_heads(rotate(key_grad, cos_table, -sin_table).astype(BF16)),
+            join_heads(value_grad.astype(BF16)),
+        ]
+    )
+    attn_in_grad = jnp.einsum("sde,ste->sdt", qkv, proj_grad, preferred_element_type=F32).astype(BF16)
+    g_qkv = jnp.einsum("sdt,ste->sde", act[:3], proj_grad, preferred_element_type=F32).astype(BF16)
+    g_out = jnp.einsum("dt,te->de", branch_grad, context_rows, preferred_element_type=F32).astype(BF16)
+    g_up = jnp.einsum("dt,tf->df", act[3], up_grad_low, preferred_element_type=F32).astype(BF16)
+    g_down = jnp.einsum("dt,tf->df", branch_grad, hidden, preferred_element_type=F32).astype(BF16)
+    grid = (n_dp // HIGH, 2, 2, 2 * mix_in.shape[0])
+    stream_grad, mix_grad, small_total, tiny, qkv_total, up_total, down_total, out_total = scatter(
+        n_dp, attn_in_grad, mlp_in_grad, streams, small_all, wide_grad, mixin_part, tiny, history,
+        g_qkv.reshape((3,) + grid + (-1,)), g_up.reshape(grid + (-1,)), g_down.reshape(grid + (-1,)),
+        g_out.reshape(grid + (-1,)),
+    )
+    mix_rows = jnp.transpose(mix_all.reshape(2, n_dp, MIXH, half), (2, 1, 0, 3)).reshape(MIXH, n_dp * seq_len)
+    history_grad = jnp.stack(
+        [
+            sum(
+                mix_rows[stream * HIST + source][None, :] * stream_grad[stream].astype(F32)
+                for stream in range(STREAMS)
+            )
+            for source in range(HIST)
+        ]
+    ).astype(BF16)
+    return (
+        block.T,
+        next_mix.T.reshape(seq_len, STREAMS, NEXT),
+        history_grad,
+        mix_grad[: STREAMS * HIST].T.reshape(seq_len, STREAMS, HIST),
+        qkv_total.astype(F32),
+        out_total.astype(F32),
+        up_total.astype(F32),
+        down_total.astype(F32),
+        small_total[:, MIXH : MIXH + 2].T,
+        small_total[:, MIXH + 2 : MIXH + 4].T,
+        small_total[:, :MIXH],
+        tiny[:, : STREAMS * NEXT],
+        tiny[: STREAMS * NEXT, MIXH],
+    )
+
+
+def solution(mesh):
+    return jax.shard_map(
+        functools.partial(per_device, mesh.shape["dp"]),
+        mesh=mesh,
+        in_specs=(
+            P(None, "dp", None),
+            P("dp", None, None),
+            P(None, "dp", "tensor"),
+            P("dp", "tensor"),
+            P("dp", "tensor"),
+            P("dp", "tensor"),
+            P(None, "dp"),
+            P(None, "dp"),
+            P("dp", None),
+            P(),
+            P(),
+            P("dp", None),
+            P("dp", None, None),
+        ),
+        out_specs=(
+            P("dp", None),
+            P("dp", None, None),
+            P(None, "dp", None),
+            P("dp", None, None),
+            P(None, "dp", "tensor"),
+            P("dp", "tensor"),
+            P("dp", "tensor"),
+            P("dp", "tensor"),
+            P(None, "dp"),
+            P(None, "dp"),
+            P("dp", None),
+            P(),
+            P(),
+        ),
+        check_vma=False,
+    )

time: 900 us -> 736 us (0.82)
  Pallas kernels: 662 us -> 565 us
  blocking collectives: 49.3 us -> 0 us
  local copies, waits for them, and re-layouts: 58.5 us -> 47.5 us
    pallas_call x1, Pallas kernels: 304 us -> 252 us  [scatter(): pl.pallas_call(functools.partial(scatter_kernel, n_dp), out_shape=[jax.Sh...]
    psum x1 -> x0, blocking collectives: 40.5 us -> none  [per_device(): lax.psum((tiny[:MIXH, :STREAMS * NEXT], tiny[:STREAMS * NEXT, 128]), ('dp...]
    pallas_call x1, Pallas kernels: 280 us -> 241 us  [gather(): pl.pallas_call(functools.partial(gather_kernel, n_dp), out_shape=[jax.Sha...]
    unnamed x143 -> x134, local copies, waits for them, and re-layouts: 31.5 us -> 23.6 us
where the time goes in v2:
time: 736 us; the launch traced here: 728 us
  Pallas kernels  565 us (77%)
  matrix products  92.1 us (13%)
  local copies, waits for them, and re-layouts  47.5 us (6%)
  other arithmetic  21.3 us (3%)
    pallas_call x1, Pallas kernels, scatter(): pl.pallas_call(functools.partial(scatter_kernel, n_dp), out_shape=[jax.Sh...  252 us
    pallas_call x1, Pallas kernels, gather(): pl.pallas_call(functools.partial(gather_kernel, n_dp), out_shape=[jax.Sha...  241 us
    pallas_call x1, Pallas kernels, join(): pl.pallas_call(join_kernel, out_shape=[jax.ShapeDtypeStruct(*shape) for s...  71.5 us
    unnamed x134, local copies, waits for them, and re-layouts  23.6 us
    dot_general x1, matrix products, per_device(): up_pre = jnp.einsum('dt,df->tf', act[3], up, preferred_element_type=F32)  17.3 us

profile of v2, /device:TPU:7, one launch (start us, length us, event | category | flops | bytes accessed | tf_op | source)
XLA Modules:
  0.0 728.1 jit_solution(7310835787875515766)
XLA Ops:
  7.0 241.2 %gather.1 = (f32[2,2,2,2,2,40,128]{6,5,4,3,2,1,0:T(8,128)S(1)}, bf16[2,2,2,2,128,128]{5,4,3,2,1,0:T(8,128)(2,1)S(1)}, bf16[4,2048,128]{2,1,0:T(8,128)(2,1)S(1)},...) custom-call(bf16[9,128,4096]{2,1,0:T(8,128)(2,1)} %hist.3, ...), custom_call_target="tpu_custom_call" | custom-call | tf_op jit(solution)/shard_map/gather/pallas_call | solution.py:395
  250.3 1.7 copy-done.4
  252.1 10.7 %fusion.75 = f32[3,1024,256]{2,1,0:T(8,128)} fusion(bf16[4,2048,1024]{2,1,0:T(8,128)(2,1)} %get-tuple-element.36, bf16[3,2048,256]{2,1,0:T(8,128)(2,1)S(1)} %bitcast.141), kind=kOutput, calls=%fused_computation.171 | convolution fusion | flops 3221225472 | bytes 23068672 | tf_op jit(solution)/shard_map/sdt,sde->ste/dot_general | solution.py:2166
  262.7 5.4 reshape.510
  268.2 1.7 fusion.70
  272.3 3.1 subtract_convert_fusion.3
  277.8 2.0 slice.458
  282.2 17.3 %multiply_convert_fusion = (bf16[1024,1024]{1,0:T(8,128)(2,1)S(1)}, f32[1024,1024]{1,0:T(8,128)}, f32[1024,1024]{1,0:T(8,128)}) fusion(bf16[2048,1024]{1,0:T(8,128)(2,1)S(1)} %bitcast.222, bf16[4,2048,1024]{2,1,0:T(8,128)(2,1)} %get-tuple-element.36), kind=kOutput, calls=%fused_computation.45 | convolution fusion | flops 4363124736 | bytes 18874368 | tf_op jit(solution)/shard_map/dt,df->tf/dot_general | solution.py:2180
  299.6 4.6 fusion.74
  304.2 3.4 add_convert_fusion.part
  308.7 1.6 copy-done.3
  310.3 71.5 %join.1 = (bf16[2048,1024]{1,0:T(8,128)(2,1)S(1)}, f32[2048,128]{1,0:T(8,128)S(1)}, bf16[2048,256]{1,0:T(8,128)(2,1)S(1)}, f32[40,256]{1,0:T(8,128)S(1)}, f32[20...) custom-call(bf16[2048,1024]{1,0:T(8,128)(2,1)} %add_convert_fusion.part, bf16[4,2048,128]{2,1,0:T(8,128)(2,1)S(1)} %copy-done.3, ...), custom_call_target="tpu_custom_call" | custom-call | tf_op jit(solution)/shard_map/join/pallas_call | solution.py:1543
  381.8 2.3 convolution_convert_fusion.4
  386.8 5.9 add_convert_fusion.1
  392.7 9.1 %fusion.10 = bf16[2048,1024]{1,0:T(8,128)(2,1)} fusion(bf16[1024,1024]{1,0:T(8,128)(2,1)S(1)} %add_convert_fusion.1, bf16[4,2048,1024]{2,1,0:T(8,128)(2,1)} %get-tuple-element.36), kind=kOutput, calls=%fused_computation.59 | convolution fusion | flops 4297064448 | bytes 10485760 | tf_op jit(solution)/shard_map/dt,tf->df/dot_general | solution.py:2217
  401.8 6.3 convolution_convert_fusion.1
  408.1 2.1 convolution_convert_fusion.7
  410.2 2.0 reshape.519
  415.2 2.2 stack_reshape.11
  426.4 9.9 %convolution_convert_fusion.3 = bf16[3,2048,256]{2,1,0:T(8,128)(2,1)} fusion(bf16[4,2048,1024]{2,1,0:T(8,128)(2,1)} %get-tuple-element.36, bf16[3,1024,256]{2,1,0:T(8,128)(2,1)S(1)} %constant_dynamic-update-slice_fusion), kind=kOutput, calls=%fused_computation.64 | convolution fusion | flops 3222798336 | bytes 21495808 | tf_op jit(solution)/shard_map/sdt,ste->sde/dot_general | solution.py:2215
  436.3 9.6 %convolution_convert_fusion.2.mlp_grad = bf16[2048,1024]{1,0:T(8,128)(2,1)} fusion(bf16[2048,1024]{1,0:T(8,128)(2,1)} %bitcast.221, bf16[1024,1024]{1,0:T(8,128)(2,1)} %copy-done.57), kind=kOutput, calls=%fused_computation.61 | convolution fusion | flops 4297064448 | bytes 10485760 | tf_op jit(solution)/shard_map/df,tf->dt/dot_general | solution.py:2201
  445.9 6.5 convolution_convert_fusion.attn_grad
  452.4 252.4 %scatter.1 = (bf16[4,128,4096]{2,1,0:T(8,128)(2,1)}, f32[40,256]{1,0:T(8,128)}, f32[128,128]{1,0:T(8,128)}, f32[40,128]{1,0:T(8,128)}, bf16[3,128,1024]{2,1,0:T(...) custom-call(bf16[3,2048,1024]{2,1,0:T(8,128)(2,1)} %convolution_convert_fusion.attn_gra, ...), custom_call_target="tpu_custom_call" | custom-call | tf_op jit(solution)/shard_map/scatter/pallas_call | solution.py:1999
  705.4 3.2 fusion.62
  (202 shorter events, 50.5 us)
Async XLA Ops:
  0.6 307.2 %copy-start = (bf16[256,2048]{1,0:T(8,128)(2,1)S(1)}, bf16[256,2048]{1,0:T(8,128)(2,1)}, u32[]{:S(2)}) copy-start(bf16[256,2048]{1,0:T(8,128)(2,1)} %param.24) | copy-start | bytes 3145732
  250.3 53.8 %copy-start.9 = (bf16[2,2,2,256,256]{4,3,2,1,0:T(8,128)(2,1)}, bf16[2,2,2,256,256]{4,3,2,1,0:T(8,128)(2,1)S(1)}, u32[]{:S(2)}) copy-start(bf16[2,2,2,256,256]{4,3,2,1,0:T(8,128)(2,1)S(1)} %get-tuple-element.35) | copy-start | bytes 3145732
  250.3 58.3 %copy-start.6 = (bf16[2,2,2,2,128,128]{5,4,3,2,1,0:T(8,128)(2,1)}, bf16[2,2,2,2,128,128]{5,4,3,2,1,0:T(8,128)(2,1)S(1)}, u32[]{:S(2)}) copy-start(bf16[2,2,2,2,128,128]{5,4,3,2,1,0:T(8,128)(2,1)S(1)} %get-tuple-element.41) | copy-start | bytes 1572868
  272.3 3.2 copy-start.24
  272.3 3.4 copy-start.23
  282.2 17.3 %copy-start.53 = (bf16[2,2,2,256,1024]{4,3,2,1,0:T(8,128)(2,1)S(1)}, bf16[2,2,2,256,1024]{4,3,2,1,0:T(8,128)(2,1)}, u32[]{:S(2)}) copy-start(bf16[2,2,2,256,1024]{4,3,2,1,0:T(8,128)(2,1)} %get-tuple-element.38) | copy-start | bytes 12582916
  299.6 4.6 copy-start.58
  310.3 73.9 %copy-start.56 = (f32[1024,1024]{1,0:T(8,128)S(1)}, f32[1024,1024]{1,0:T(8,128)}, u32[]{:S(2)}) copy-start(f32[1024,1024]{1,0:T(8,128)} %get-tuple-element.166) | copy-start | bytes 12582916
  381.8 3.7 copy-start.54
  381.8 4.9 copy-start.55
  392.7 9.1 %copy-start.57 = (bf16[1024,1024]{1,0:T(8,128)(2,1)}, bf16[1024,1024]{1,0:T(8,128)(2,1)S(1)}, u32[]{:S(2)}) copy-start(bf16[1024,1024]{1,0:T(8,128)(2,1)S(1)} %add_convert_fusion.1) | copy-start | bytes 6291460
  392.7 9.1 %copy-start.59 = (bf16[1024,1024]{1,0:T(8,128)(2,1)S(1)}, bf16[1024,1024]{1,0:T(8,128)(2,1)}, u32[]{:S(2)}) copy-start(bf16[1024,1024]{1,0:T(8,128)(2,1)} %copy-done.58) | copy-start | bytes 6291460
  401.8 6.3 copy-start.10
  408.1 5.3 copy-start.22
  412.2 5.2 copy-start.38
  436.3 9.6 %copy-start.5 = (bf16[3,2,2,2,256,256]{5,4,3,2,1,0:T(8,128)(2,1)S(1)}, bf16[3,2,2,2,256,256]{5,4,3,2,1,0:T(8,128)(2,1)}, u32[]{:S(2)}) copy-start(bf16[3,2,2,2,256,256]{5,4,3,2,1,0:T(8,128)(2,1)} %copy-done.4) | copy-start | bytes 9437188
  452.4 252.4 %copy-start.17 = (f32[2,2,2,2,2,40,128]{6,5,4,3,2,1,0:T(8,128)S(1)}, f32[2,2,2,2,2,40,128]{6,5,4,3,2,1,0:T(8,128)}, u32[]{:S(2)}) copy-start(f32[2,2,2,2,2,40,128]{6,5,4,3,2,1,0:T(8,128)} %copy-done.16) | copy-start | bytes 1966084
  705.4 3.5 copy-start.20
  715.3 6.3 copy-start.46
  717.2 4.3 copy-start.49
  717.3 5.0 copy-start.44
  717.3 7.0 copy-start.47
  717.3 7.7 %copy-start.12 = (bf16[2048,256]{1,0:T(8,128)(2,1)S(1)}, bf16[2048,256]{1,0:T(8,128)(2,1)}, u32[]{:S(2)}) copy-start(bf16[2048,256]{1,0:T(8,128)(2,1)} %copy-done.11) | copy-start | bytes 3145732
  718.8 8.9 %copy-start.1 = (bf16[256,2048]{1,0:T(8,128)(2,1)S(1)}, bf16[256,2048]{1,0:T(8,128)(2,1)}, u32[]{:S(2)}) copy-start(bf16[256,2048]{1,0:T(8,128)(2,1)} %param.24) | copy-start | bytes 3145732
  (36 other events, 59.3 us)

commit v3 on v2

--- a/solution.py
+++ b/solution.py
@@ -20,13 +20,17 @@
 MASKED = -1e30
 
 MESH = pl.DeviceIdType.MESH
-ANY = pl.BlockSpec(memory_space=pl.ANY)
+ANY = pl.BlockSpec(memory_space=pltpu.HBM)
 VM = pl.BlockSpec(memory_space=pltpu.VMEM)
 DMA = pltpu.SemaphoreType.DMA
 F32, BF16 = jnp.float32, jnp.bfloat16
 CORE, SIDE, NEAR, HIGH = 1, 2, 4, 8
 QUARTERS = 4
 UNIT = 256
+PLAN = (
+    "T", "T", "n0", "T", "T", "n1", "T", "T", "n2", "s0", "T", "n3", "t0", "s1", "w0", "p0", "T", "t1", "s2", "p1",
+    "T", "t2", "s3", "p2", "t3", "a0", "u0",
+)
 
 
 def bit(place, value):
@@ -99,12 +103,52 @@
     return lax.fori_loop(0, depth // chunk, body, jnp.zeros((1, 128), F32))
 
 
+def gelu_parts(values):
+    phi = 0.5 * (1.0 + lax.erf(values * (1.0 / math.sqrt(2.0))))
+    density = jnp.exp(-0.5 * values * values) * (1.0 / math.sqrt(2.0 * math.pi))
+    return values * phi, phi + values * density
+
+
+def tn(left, right):
+    return lax.dot_general(left, right, (((0,), (0,)), ((), ())), preferred_element_type=F32)
+
+
+def nt(left, right):
+    return lax.dot_general(left, right, (((1,), (1,)), ((), ())), preferred_element_type=F32)
+
+
+def nn(left, right):
+    return jnp.dot(left, right, preferred_element_type=F32)
+
+
+def turned(values, cos, sin):
+    pieces = []
+    half_rot = ROT // 2
+    repeats = values.shape[1] // cos.shape[1]
+    cos, sin = (jnp.concatenate([table] * repeats, axis=1) for table in (cos, sin))
+    for head in range(values.shape[0] // HD):
+        rows = values[head * HD : (head + 1) * HD]
+        first, second = rows[:half_rot], rows[half_rot:ROT]
+        pieces += [first * cos - second * sin, second * cos + first * sin, rows[ROT:]]
+    return jnp.concatenate(pieces, axis=0)
+
+
+def causal_scores(keys, queries):
+    scores = tn(keys, queries) * (1.0 / math.sqrt(HD))
+    length = scores.shape[0]
+    key = lax.broadcasted_iota(jnp.int32, (length, length), 0)
+    query = lax.broadcasted_iota(jnp.int32, (length, length), 1)
+    return jnp.where(query >= key, scores, MASKED)
+
+
 def gather_kernel(
-    n_dp, hist, mix, small, w_qkv, w_up, w_down, w_out,
-    o_mix, o_small, o_streams, o_act, o_qkv, o_up, o_down, o_out,
+    n_dp, hist, mix, small, w_qkv, w_out, w_up, w_down, cos, sin,
+    o_mix, o_small, o_streams, o_act, o_qkv, o_out, o_up, o_down,
+    o_rows, o_context, o_sums, o_hidden, o_slope, o_part,
     mix_all, small_all, hist_in, mixed, streams, act,
     early_s, early_r, hist_sem, a2a_s, a2a_r, reshard_s, reshard_r, high_s, high_r, side_s, side_r,
-    act_s, act_r, act_local, own_sem, out_sem, share_s, share_r,
+    act_s, act_r, act_local, own_sem, out_sem, share_s, share_r, share_l,
+    act_in, qkv_in, out_in, up_in, down_in, rows_out, context, sums, hidden, slope, part, load_sem, save_sem,
 ):
     here = Place()
     me, tensor = here.me, here.tensor
@@ -112,7 +156,7 @@
     depth = rows * n_dp
     half = hist.shape[2] // n_dp // 2
     high_bits = int(math.log2(n_dp // HIGH))
-    weights = ((w_qkv, o_qkv), (w_up, o_up), (w_down, o_down), (w_out, o_out))
+    weights = ((w_qkv, o_qkv), (w_out, o_out), (w_up, o_up), (w_down, o_down))
     greet_all(n_dp, me, here.other)
 
     def early(which, buf, phase):
@@ -325,12 +369,27 @@
         for which, buf in early_pairs:
             early(which, buf, phase - 1).wait()
             early(which, buf, phase).start()
+        if phase == 2:
+            second(0)
     early(0, mix_all, last).wait()
-    mix_copy = pltpu.make_async_copy(mix_all, o_mix.at[tensor], out_sem.at[0])
-    mix_share = remote(mix_all, o_mix.at[tensor], share_s.at[0], share_r.at[0], tensor=here.other)
-    mix_copy.start()
-    mix_share.start()
-    second(0)
+    def mix_lanes(index):
+        return mix_all.at[lax.div(index, HIGH), bit(index, NEAR), bit(index, SIDE), bit(index, CORE)], o_mix.at[
+            :, at(index * 2 * half + tensor * half, half)
+        ]
+
+    def mix_copy(index):
+        source, target = mix_lanes(index)
+        return pltpu.make_async_copy(source, target, share_l.at[index])
+
+    def mix_share(index):
+        source, target = mix_lanes(index)
+        return remote(source, target, share_s.at[index], share_r.at[index], tensor=here.other)
+
+    def mix_out(index):
+        mix_copy(index).start()
+        mix_share(index).start()
+
+    loop(0, n_dp, mix_out)
     loop(0, n_dp, mix_step)
     streams[:, at(me * rows, rows), :] = mixed[0]
     early(1, small_all, last).wait()
@@ -352,51 +411,150 @@
             act_tensor(stream, 0).start()
     for copy in finals:
         copy.start()
-    for stream in range(STREAMS):
-        ticks(2)
-        act_first(stream)
-    for stream in range(STREAMS):
-        ticks(1)
-        act_second(stream)
-    ticks(total)
-    for unit in range(total):
-        side_hop(unit).wait()
-    for stream in range(STREAMS):
+    depth, tokens = act_in.shape[1:]
+    seq_len = 2 * half
+    heads = context.shape[0] // HD
+    tile = 256
+
+    def act_load(stream):
+        return pltpu.make_async_copy(o_act.at[stream], act_in.at[stream], load_sem.at[stream])
+
+    def act_third(stream):
         for near in range(2):
             act_core(stream, near).wait()
-    for copy in finals:
+        act_load(stream).start()
+
+    loads = {
+        "qkv": pltpu.make_async_copy(o_qkv.reshape(3, depth, qkv_in.shape[2]), qkv_in, load_sem.at[4]),
+        "out": pltpu.make_async_copy(o_out.reshape(depth, out_in.shape[1]), out_in, load_sem.at[5]),
+        "up": pltpu.make_async_copy(o_up.reshape(depth, up_in.shape[1]), up_in, load_sem.at[6]),
+        "down": pltpu.make_async_copy(o_down.reshape(depth, down_in.shape[1]), down_in, load_sem.at[7]),
+    }
+    held = 0
+
+    def arrive(count):
+        nonlocal held
+        ticks(max(held + count - done, 0))
+        for unit in range(held, held + count):
+            side_hop(unit).wait()
+        held += count
+
+    def project(stream):
+        act_load(stream).wait()
+        values = tn(qkv_in[stream], act_in[stream])
+        if stream < 2:
+            values = turned(values, cos[...], sin[...])
+        rows_out[stream] = values.astype(BF16)
+
+    def attend(seq):
+        span = at(seq * seq_len, seq_len)
+        for head in range(heads):
+            lane = pl.ds(head * HD, HD)
+            scores = causal_scores(rows_out[1, lane, span], rows_out[0, lane, span])
+            peak = jnp.max(scores, axis=0, keepdims=True)
+            raised = jnp.exp(scores - peak)
+            total_weight = jnp.sum(raised, axis=0, keepdims=True)
+            prob = (raised / total_weight).astype(BF16)
+            context[lane, span] = nn(rows_out[2, lane, span], prob).astype(BF16)
+            sums[pl.ds(seq * heads + head, 1), :] = peak + jnp.log(total_weight)
+
+    def raise_up(index):
+        span = at(index * tile, tile)
+        value, derivative = gelu_parts(tn(up_in[:, span], act_in[3]))
+        hidden[span, :] = value.astype(BF16)
+        slope[span, :] = derivative
+
+    def lower(index):
+        span = at(index * tile, tile)
+        part[span, :] = (nn(out_in[span, :], context[...]) + nn(down_in[span, :], hidden[...])).astype(BF16)
+
+    saves = []
+
+    def save(*pairs):
+        for source, target in pairs:
+            copy = pltpu.make_async_copy(source, target, save_sem.at[len(saves)])
+            copy.start()
+            saves.append(copy)
+
+    def rows_arrive(_):
+        arrive(4)
+        loads["qkv"].start()
+        loads["out"].start()
+        loads["qkv"].wait()
+
+    def attend_all(_):
+        loop(0, tokens // seq_len, attend)
+        save((rows_out, o_rows), (context, o_context), (sums, o_sums))
+
+    def raise_all(_):
+        arrive(up_in.shape[1] // UNIT)
+        loads["up"].start()
+        act_load(3).wait()
+        loads["up"].wait()
+        loop(0, hidden.shape[0] // tile, raise_up)
+        save((hidden, o_hidden), (slope, o_slope))
+
+    actions = {
+        "n": act_first, "s": act_second, "t": act_third, "w": rows_arrive, "p": project, "a": attend_all, "u": raise_all
+    }
+    for action in PLAN:
+        if action == "T":
+            ticks(1)
+        else:
+            actions[action[0]](int(action[1]))
+    arrive(total - held)
+    loads["down"].start()
+    loads["out"].wait()
+    loads["down"].wait()
+    loop(0, depth // tile, lower)
+    save((part, o_part))
+    for copy in finals + saves:
         copy.wait()
-    mix_copy.wait()
-    mix_share.wait()
-
-
-def gather(n_dp, hist, mix, small, w_qkv, w_up, w_down, w_out):
+
+    def settle(index):
+        mix_copy(index).wait()
+        mix_share(index).wait()
+
+    loop(0, n_dp, settle)
+
+
+def gather(n_dp, hist, mix, small, w_qkv, w_out, w_up, w_down, cos, sin):
     rows = small.shape[0]
     depth = rows * n_dp
     half = hist.shape[2] // n_dp // 2
     high = n_dp // HIGH
     high_bits = int(math.log2(high))
     grid = (high, 2, 2, 2)
-    units = sum(w.size // w.shape[-2] for w in (w_qkv, w_up, w_down, w_out)) // QUARTERS // UNIT
+    units = sum(w.size // w.shape[-2] for w in (w_qkv, w_out, w_up, w_down)) // QUARTERS // UNIT
 
     def cut(width):
         return (high, 2, 2, 2 * rows, width // QUARTERS)
 
+    tokens = 8 * half
+    narrow, width = w_qkv.shape[2] // QUARTERS, w_up.shape[1] // QUARTERS
+    results = [
+        ((3, narrow, tokens), BF16),
+        ((narrow, tokens), BF16),
+        ((tokens // (2 * half) * (narrow // HD), 2 * half), F32),
+        ((width, tokens), BF16),
+        ((width, tokens), F32),
+        ((depth, tokens), BF16),
+    ]
     shapes = [
-        ((2,) + grid + mix.shape, F32),
+        ((mix.shape[0], n_dp * 2 * half), F32),
         (grid + (rows, 128), BF16),
         ((STREAMS, depth, half), BF16),
-        ((STREAMS, depth, 8 * half), BF16),
+        ((STREAMS, depth, tokens), BF16),
         ((3,) + cut(w_qkv.shape[2]), BF16),
+        (cut(w_out.shape[1]), BF16),
         (cut(w_up.shape[1]), BF16),
         (cut(w_down.shape[1]), BF16),
-        (cut(w_out.shape[1]), BF16),
-    ]
+    ] + results
     return pl.pallas_call(
         functools.partial(gather_kernel, n_dp),
         out_shape=[jax.ShapeDtypeStruct(*shape) for shape in shapes],
-        in_specs=[ANY] * 7,
-        out_specs=[ANY] * 8,
+        in_specs=[ANY] * 7 + [VM] * 2,
+        out_specs=[ANY] * 14,
         scratch_shapes=[
             pltpu.VMEM(grid + mix.shape, F32),
             pltpu.VMEM(grid + (rows, 128), BF16),
@@ -420,14 +578,22 @@
             DMA((STREAMS,)),
             DMA((2 + units,)),
             DMA((3,)),
-            DMA((1,)),
-            DMA((1,)),
-        ],
+            DMA((n_dp,)),
+            DMA((n_dp,)),
+            DMA((n_dp,)),
+            pltpu.VMEM((STREAMS, depth, tokens), BF16),
+            pltpu.VMEM((3, depth, narrow), BF16),
+            pltpu.VMEM((depth, narrow), BF16),
+            pltpu.VMEM((depth, width), BF16),
+            pltpu.VMEM((depth, width), BF16),
+        ]
+        + [pltpu.VMEM(*shape) for shape in results]
+        + [DMA((8,)), DMA((6,))],
         compiler_params=pltpu.CompilerParams(
-            collective_id=1, has_side_effects=True, vmem_limit_bytes=40 * 1024 * 1024
+            collective_id=1, has_side_effects=True, vmem_limit_bytes=61 * 1024 * 1024
         ),
         name="gather",
-    )(hist, mix, small, w_qkv, w_up, w_down, w_out)
+    )(hist, mix, small, w_qkv, w_out, w_up, w_down, cos, sin)
 
 
 def lane_block(half, near, core, half_at, count):
@@ -1326,12 +1492,6 @@
     return at(near * 4 * half + core * 2 * half + half_at * half, count * half, half)
 
 
-def gelu_parts(values):
-    phi = 0.5 * (1.0 + lax.erf(values * (1.0 / math.sqrt(2.0))))
-    density = jnp.exp(-0.5 * values * values) * (1.0 / math.sqrt(2.0 * math.pi))
-    return values * phi, phi + values * density
-
-
 def reduce_group(here, half, part, theirs, own, from_core, from_tensor, from_near, sems, local, pieces, piece):
     core_s, core_r, tensor_s, tensor_r, near_s, near_r = sems
 
@@ -1391,9 +1551,9 @@
 
 
 def join_kernel(
-    part, streams, cot, small, mix_in, mix_out, mix_back, static, next_cot,
+    part, streams, out_cot, small, mix_out, next_cot,
     o_grad, o_wide, o_block, o_next, o_mixin, o_tiny,
-    own, from_core, from_tensor, from_near, residual, wide, normed, block, back, low, next_rows, mixin, tiny,
+    own, from_core, from_tensor, from_near, residual, wide, normed, block, cot, cot_in, back, low, next_rows, mixin, tiny,
     core_s, core_r, tensor_s, tensor_r, near_s, near_r, local, share_s, share_r, own_sem,
 ):
     here = Place()
@@ -1413,6 +1573,8 @@
     )
     fetch = pltpu.make_async_copy(streams.at[3], residual, own_sem.at[0])
     fetch.start()
+    cot_fetch = pltpu.make_async_copy(out_cot.at[at(tensor * half, half), :], cot_in, own_sem.at[7])
+    cot_fetch.start()
     for span in range(spans):
         start(span)
     for span in range(spans):
@@ -1420,6 +1582,13 @@
     for span in range(spans):
         after_tensor(span)
     fetch.wait()
+    cot_fetch.wait()
+
+    def turn(index):
+        rows = at(index * chunk, chunk)
+        cot[rows, :] = cot_in[:, rows].T
+
+    loop(0, depth // chunk, turn)
     squares = jnp.zeros((1, half), F32)
     for span in range(spans):
         after_near(span)
@@ -1429,17 +1598,17 @@
             branch = from_tensor[here.near, rows, :].astype(F32) + from_near[rows, :].astype(F32)
             value = residual[rows, :].astype(F32) + branch
             wide[rows, :] = value
-            block[rows, :] = value.astype(BF16)
+            block[:, rows] = value.T.astype(BF16)
             return total + jnp.sum(value * value, axis=0, keepdims=True)
 
         squares = lax.fori_loop(0, size // chunk, widen, squares)
     root = lax.rsqrt(squares / depth + ROOT_EPS)
 
     def share_block(which):
-        lanes = at(tensor * half, half)
+        mine = o_block.at[at(tensor * half, half), :]
         if which == 0:
-            return pltpu.make_async_copy(block, o_block.at[:, lanes], own_sem.at[1])
-        return remote(block, o_block.at[:, lanes], share_s.at[0], share_r.at[0], tensor=here.other)
+            return pltpu.make_async_copy(block, mine, own_sem.at[1])
+        return remote(block, mine, share_s.at[0], share_r.at[0], tensor=here.other)
 
     share_block(0).start()
     share_block(1).start()
@@ -1449,18 +1618,15 @@
         normed[rows, :] = (wide[rows, :] * root).astype(BF16)
 
     loop(0, depth // chunk, norm)
-    inner, slope = gelu_parts(jnp.dot(mix_in[...], normed[...], preferred_element_type=F32))
+    inner, slope = gelu_parts(tn(small[...], normed[...]))
     inner_low = inner.astype(BF16)
-    next_rows[...] = (jnp.dot(mix_out[...], inner_low, preferred_element_type=F32) + static[...])[:MIXH]
+    next_rows[...] = tn(mix_out[...], inner_low)[:MIXH]
     next_low = next_cot[...].astype(BF16)
-
-    def nt(left, right):
-        return lax.dot_general(left, right, (((1,), (1,)), ((), ())), preferred_element_type=F32)
 
     column = lax.broadcasted_iota(jnp.int32, (128, 128), 1)
     static_grad = jnp.sum(next_cot[...], axis=1, keepdims=True)
     tiny[...] = jnp.where(column == MIXH, static_grad, nt(inner_low, next_low))[:MIXH]
-    inner_grad = (jnp.dot(mix_back[...], next_low, preferred_element_type=F32) * slope).astype(BF16)
+    inner_grad = (nn(mix_out[...], next_low) * slope).astype(BF16)
 
     def pull(index, total):
         rows = at(index * chunk, chunk)
@@ -1529,13 +1695,13 @@
         copy.wait()
 
 
-def join(part, streams, cot, small, mix_in, mix_out, mix_back, static, next_cot):
-    depth, half = cot.shape
+def join(part, streams, out_cot, small, mix_out, next_cot):
+    depth, half = streams.shape[1:]
     spans = 4
     shapes = [
         ((depth, 8 * half), BF16),
         ((depth, half), F32),
-        ((depth, 2 * half), BF16),
+        ((2 * half, depth), BF16),
         ((MIXH, 2 * half), F32),
         ((depth, 128), F32),
         ((MIXH, 128), F32),
@@ -1543,7 +1709,7 @@
     return pl.pallas_call(
         join_kernel,
         out_shape=[jax.ShapeDtypeStruct(*shape) for shape in shapes],
-        in_specs=[ANY, ANY] + [VM] * 7,
+        in_specs=[ANY] * 3 + [VM] * 3,
         out_specs=[ANY] * 6,
         scratch_shapes=[
             pltpu.VMEM((2, 2, depth, half), BF16),
@@ -1553,7 +1719,9 @@
             pltpu.VMEM((depth, half), BF16),
             pltpu.VMEM((depth, half), F32),
             pltpu.VMEM((depth, half), BF16),
+            pltpu.VMEM((half, depth), BF16),
             pltpu.VMEM((depth, half), BF16),
+            pltpu.VMEM((half, depth), BF16),
             pltpu.VMEM((depth, half), F32),
             pltpu.VMEM((depth, half), BF16),
             pltpu.VMEM((MIXH, half), F32),
@@ -1568,13 +1736,144 @@
             DMA((spans, 4)),
             DMA((8,)),
             DMA((8,)),
-            DMA((7,)),
+            DMA((8,)),
         ],
         compiler_params=pltpu.CompilerParams(
-            collective_id=2, has_side_effects=True, vmem_limit_bytes=40 * 1024 * 1024
+            collective_id=2, has_side_effects=True, vmem_limit_bytes=56 * 1024 * 1024
         ),
         name="join",
-    )(part, streams, cot, small, mix_in, mix_out, mix_back, static, next_cot)
+    )(part, streams, out_cot, small, mix_out, next_cot)
+
+
+def back_kernel(
+    grad, act, w_qkv, w_out, w_up, w_down, rows, context, sums, hidden, slope, cos, sin,
+    o_attn, o_mlp, o_qkv, o_out, o_up, o_down,
+    grad_in, act_in, qkv_in, out_in, up_in, down_in, rows_in, context_in, sums_in, hidden_in, slope_in,
+    up_grad, context_grad, row_grad, tall, wide, load_sem, tall_sem, wide_sem,
+):
+    depth, tokens = grad.shape
+    seq_len = sums.shape[1]
+    heads = context.shape[0] // HD
+    tile = 256
+    loads = {}
+    pairs = (
+        ("grad", grad, grad_in), ("down", w_down, down_in), ("slope", slope, slope_in), ("hidden", hidden, hidden_in),
+        ("up", w_up, up_in), ("out", w_out, out_in), ("rows", rows, rows_in), ("sums", sums, sums_in),
+        ("context", context, context_in), ("qkv", w_qkv, qkv_in), ("act3", act.at[3], act_in.at[0]),
+    )
+    for number, (name, source, target) in enumerate(pairs):
+        loads[name] = pltpu.make_async_copy(source, target, load_sem.at[number])
+        loads[name].start()
+
+    def act_load(stream):
+        slot = (stream + 1) % 2
+        return pltpu.make_async_copy(act.at[stream], act_in.at[slot], load_sem.at[len(pairs) + slot])
+
+    act_load(0).start()
+
+    pending = {}
+
+    def write(kind, turn, out, width, compute):
+        buf, sem = (tall, tall_sem) if kind == "tall" else (wide, wide_sem)
+        slots = buf.shape[1]
+        if (kind, turn) in pending:
+            pending.pop((kind, turn))()
+
+        def copy(index):
+            slot = lax.rem(index, slots)
+            target = out.at[at(index * tile, tile), :]
+            return pltpu.make_async_copy(buf.at[turn, slot, :, pl.ds(0, width)], target, sem.at[turn, slot])
+
+        def body(index):
+            @pl.when(index >= slots)
+            def _():
+                copy(index - slots).wait()
+
+            buf[turn, lax.rem(index, slots), :, :width] = compute(at(index * tile, tile)).astype(BF16)
+            copy(index).start()
+
+        steps = depth // tile
+        loop(0, steps, body)
+        pending[kind, turn] = lambda: loop(steps - slots, steps, lambda index: copy(index).wait())
+
+    for name in ("grad", "down", "slope"):
+        loads[name].wait()
+
+    def lift(index):
+        span = at(index * tile, tile)
+        up_grad[span, :] = (tn(down_in[:, span], grad_in[...]) * slope_in[span, :]).astype(BF16)
+
+    loop(0, hidden.shape[0] // tile, lift)
+    loads["up"].wait()
+    write("tall", 1, o_mlp, tokens, lambda span: nn(up_in[span, :], up_grad[...]))
+    for name in ("out", "rows", "sums", "context"):
+        loads[name].wait()
+    context_grad[...] = tn(out_in[...], grad_in[...]).astype(BF16)
+
+    def attend(seq):
+        span = at(seq * seq_len, seq_len)
+        for head in range(heads):
+            lane = pl.ds(head * HD, HD)
+            queries, keys, values = (rows_in[s, lane, span] for s in range(3))
+            prob = jnp.exp(causal_scores(keys, queries) - sums_in[pl.ds(seq * heads + head, 1), :])
+            outer = context_grad[lane, span]
+            value_grad = nt(outer, prob.astype(BF16))
+            prob_grad = tn(values, outer)
+            inner = jnp.sum(prob * prob_grad, axis=0, keepdims=True)
+            score_grad = (prob * (prob_grad - inner)).astype(BF16)
+            query_grad = nn(keys, score_grad) * (1.0 / math.sqrt(HD))
+            key_grad = nt(queries, score_grad) * (1.0 / math.sqrt(HD))
+            row_grad[0, lane, span] = turned(query_grad, cos[...], -sin[...]).astype(BF16)
+            row_grad[1, lane, span] = turned(key_grad, cos[...], -sin[...]).astype(BF16)
+            row_grad[2, lane, span] = value_grad.astype(BF16)
+
+    loop(0, tokens // seq_len, attend)
+    loads["qkv"].wait()
+    for stream in range(3):
+        write("tall", stream % 2, o_attn.at[stream], tokens, lambda span: nn(qkv_in[stream, span, :], row_grad[stream]))
+    loads["hidden"].wait()
+    width, narrow = hidden.shape[0], context.shape[0]
+    write("wide", 0, o_down, width, lambda span: nt(grad_in[span, :], hidden_in[...]))
+    write("wide", 1, o_out, narrow, lambda span: nt(grad_in[span, :], context_in[...]))
+    loads["act3"].wait()
+    write("wide", 0, o_up, width, lambda span: nt(act_in[0, span, :], up_grad[...]))
+    for stream in range(3):
+        slot = (stream + 1) % 2
+        act_load(stream).wait()
+        if stream < 2:
+            act_load(stream + 1).start()
+        write(
+            "wide", (stream + 1) % 2, o_qkv.at[stream], narrow,
+            lambda span: nt(act_in[slot, span, :], row_grad[stream]),
+        )
+    for drain in pending.values():
+        drain()
+
+
+def back(grad, act, w_qkv, w_out, w_up, w_down, rows, context, sums, hidden, slope, cos, sin):
+    depth, tokens = grad.shape
+    weights = (w_qkv, w_out, w_up, w_down)
+    shapes = [(3, depth, tokens), (depth, tokens)] + [w.shape for w in weights]
+    return pl.pallas_call(
+        back_kernel,
+        out_shape=[jax.ShapeDtypeStruct(shape, BF16) for shape in shapes],
+        in_specs=[ANY] * 11 + [VM] * 2,
+        out_specs=[ANY] * 6,
+        scratch_shapes=[pltpu.VMEM((depth, tokens), BF16), pltpu.VMEM((2, depth, tokens), BF16)]
+        + [pltpu.VMEM(v.shape, v.dtype) for v in weights + (rows, context, sums, hidden, slope)]
+        + [
+            pltpu.VMEM(hidden.shape, BF16),
+            pltpu.VMEM(context.shape, BF16),
+            pltpu.VMEM(rows.shape, BF16),
+            pltpu.VMEM((2, 4, 256, tokens), BF16),
+            pltpu.VMEM((2, 4, 256, hidden.shape[0]), BF16),
+            DMA((13,)),
+            DMA((2, 4)),
+            DMA((2, 4)),
+        ],
+        compiler_params=pltpu.CompilerParams(vmem_limit_bytes=56 * 1024 * 1024),
+        name="back",
+    )(grad, act, w_qkv, w_out, w_up, w_down, rows, context, sums, hidden, slope, cos, sin)
 
 
 def scatter_kernel(
@@ -2064,10 +2363,6 @@
     )(attn_grad, mlp_grad, streams, small, wide_grad, mixin_part, mix_tiny, hist, *grads)
 
 
-def exact_gelu(values):
-    return jax.nn.gelu(values, approximate=False)
-
-
 def rotary_tables(length, rotary, float_type):
     half_rot = rotary // 2
     places = jnp.arange(length).astype(float_type)
@@ -2076,66 +2371,6 @@
     )
     angles = places[:, None] * frequency[None, :]
     return (jnp.cos(angles), jnp.sin(angles))
-
-
-def rotate(values, cos_table, sin_table):
-    half_rot = cos_table.shape[-1]
-    first_half = values[..., :half_rot]
-    second = values[..., half_rot : 2 * half_rot]
-    return jnp.concatenate(
-        [
-            first_half * cos_table - second * sin_table,
-            second * cos_table + first_half * sin_table,
-            values[..., 2 * half_rot :],
-        ],
-        axis=-1,
-    )
-
-
-def masked_scores(queries, key_rows):
-    length = queries.shape[1]
-    score_scale = 1.0 / math.sqrt(queries.shape[2])
-    causal = lax.broadcasted_iota(jnp.int32, (length, length), 0) >= lax.broadcasted_iota(
-        jnp.int32, (length, length), 1
-    )
-    scores = (
-        jnp.einsum("hqd,hkd->hqk", queries, key_rows, preferred_element_type=jnp.float32)
-        * score_scale
-    )
-    return (jnp.where(causal[None], scores, MASKED), score_scale)
-
-
-def attend_forward(queries, key_rows, value_rows):
-    scores, score_scale = masked_scores(queries, key_rows)
-    row_peak = jnp.max(scores, axis=-1, keepdims=True)
-    raised = jnp.exp(scores - row_peak)
-    row_total = jnp.sum(raised, axis=-1, keepdims=True)
-    prob_low = (raised / row_total).astype(jnp.bfloat16)
-    context = jnp.einsum("hqk,hkd->hqd", prob_low, value_rows, preferred_element_type=jnp.float32)
-    return (context.astype(jnp.bfloat16), row_peak + jnp.log(row_total))
-
-
-def attend_backward(queries, key_rows, value_rows, log_sum, context_grad):
-    scores, score_scale = masked_scores(queries, key_rows)
-    attn_prob = jnp.exp(scores - log_sum)
-    prob_low = attn_prob.astype(jnp.bfloat16)
-    value_grad = jnp.einsum(
-        "hqk,hqd->hkd", prob_low, context_grad, preferred_element_type=jnp.float32
-    )
-    prob_grad = jnp.einsum(
-        "hqd,hkd->hqk", context_grad, value_rows, preferred_element_type=jnp.float32
-    )
-    inner_sum = jnp.sum(attn_prob * prob_grad, axis=-1, keepdims=True)
-    score_grad = (attn_prob * (prob_grad - inner_sum)).astype(jnp.bfloat16)
-    query_grad = (
-        jnp.einsum("hqk,hkd->hqd", score_grad, key_rows, preferred_element_type=jnp.float32)
-        * score_scale
-    )
-    key_grad = (
-        jnp.einsum("hqk,hqd->hkd", score_grad, queries, preferred_element_type=jnp.float32)
-        * score_scale
-    )
-    return (query_grad, key_grad, value_grad)
 
 
 def per_device(
@@ -2150,79 +2385,35 @@
     def own_half(rows):
         return lax.dynamic_slice_in_dim(rows, tensor * half, half, 0)
 
-    mix_rows = jnp.pad(own_half(mix_weights.reshape(seq_len, -1)).T, ((0, MIXH - STREAMS * HIST), (0, 0)))
-    small = jnp.concatenate([mix_in, norm_gain.T, norm_bias.T], axis=1)
-    small = jnp.pad(small, ((0, 0), (0, 128 - small.shape[1])))
-    mix_all, small_all, streams, act, qkv, up, down, out = gather(
-        n_dp, history, mix_rows, small, w_qkv, w_up, w_down, w_out
+    mix_rows = own_half(mix_weights.reshape(seq_len, -1)).T
+    small = jnp.concatenate(
+        [mix_in, norm_gain.T, norm_bias.T, jnp.zeros((mix_in.shape[0], 128 - MIXH - 4), BF16)], axis=1
+    )
+    cos, sin = (table.T for table in rotary_tables(seq_len, ROT, F32))
+    mix_rows, small_all, streams, act, qkv, out, up, down, rows, context, sums, hidden, slope, part = gather(
+        n_dp, history, mix_rows, small, w_qkv, w_out, w_up, w_down, cos, sin
     )
     small_all = small_all.reshape(depth, 128)
     qkv, up, down, out = (
         qkv.reshape(3, depth, -1), up.reshape(depth, -1), down.reshape(depth, -1), out.reshape(depth, -1)
     )
-    tokens = act.shape[2]
-    seqs = tokens // seq_len
-    heads = qkv.shape[2] // HD
-    projected = jnp.einsum("sdt,sde->ste", act[:3], qkv, preferred_element_type=F32)
-    head_rows = jnp.transpose(projected.reshape(3, seqs, seq_len, heads, HD), (0, 1, 3, 2, 4)).reshape(
-        3, seqs * heads, seq_len, HD
-    )
-    cos_table, sin_table = rotary_tables(seq_len, ROT, F32)
-    queries = rotate(head_rows[0], cos_table, sin_table).astype(BF16)
-    key_rows = rotate(head_rows[1], cos_table, sin_table).astype(BF16)
-    value_rows = head_rows[2].astype(BF16)
-    context, log_sum = attend_forward(queries, key_rows, value_rows)
-
-    def join_heads(rows):
-        return jnp.transpose(rows.reshape(seqs, heads, seq_len, HD), (0, 2, 1, 3)).reshape(tokens, heads * HD)
-
-    context_rows = join_heads(context)
-    up_pre = jnp.einsum("dt,df->tf", act[3], up, preferred_element_type=F32)
-    hidden_wide, gelu_back = jax.vjp(exact_gelu, up_pre)
-    hidden = hidden_wide.astype(BF16)
-    part = (
-        jnp.einsum("de,te->dt", out, context_rows, preferred_element_type=F32)
-        + jnp.einsum("df,tf->dt", down, hidden, preferred_element_type=F32)
-    ).astype(BF16)
 
     def square(values):
         return jnp.pad(values, ((0, 128 - values.shape[0]), (0, 128 - values.shape[1])))
 
-    next_rows = own_half(next_cot.reshape(seq_len, -1)).T
-    next_rows = jnp.pad(next_rows, ((0, 128 - next_rows.shape[0]), (0, 0)))
-    mix_in_rows = jnp.pad(small_all[:, :MIXH].T, ((0, 128 - MIXH), (0, 0)))
-    static = jnp.pad(mix_static[:, None], ((0, 128 - mix_static.shape[0]), (0, 0)))
+    next_rows = jnp.pad(own_half(next_cot.reshape(seq_len, -1)).T, ((0, 128 - STREAMS * NEXT), (0, 0)))
     branch_grad, wide_grad, block, next_mix, mixin_part, tiny = join(
-        part, streams, own_half(out_cot).T, small_all, mix_in_rows, square(mix_out.T), square(mix_out), static,
-        next_rows,
-    )
-    hidden_grad = jnp.einsum("dt,df->tf", branch_grad, down, preferred_element_type=F32)
-    up_grad_low = gelu_back(hidden_grad)[0].astype(BF16)
-    mlp_in_grad = jnp.einsum("df,tf->dt", up, up_grad_low, preferred_element_type=F32).astype(BF16)
-    context_grad_rows = jnp.einsum("dt,de->te", branch_grad, out, preferred_element_type=F32).astype(BF16)
-    context_grad = jnp.transpose(context_grad_rows.reshape(seqs, seq_len, heads, HD), (0, 2, 1, 3)).reshape(
-        seqs * heads, seq_len, HD
-    )
-    query_grad, key_grad, value_grad = attend_backward(queries, key_rows, value_rows, log_sum, context_grad)
-    proj_grad = jnp.stack(
-        [
-            join_heads(rotate(query_grad, cos_table, -sin_table).astype(BF16)),
-            join_heads(rotate(key_grad, cos_table, -sin_table).astype(BF16)),
-            join_heads(value_grad.astype(BF16)),
-        ]
-    )
-    attn_in_grad = jnp.einsum("sde,ste->sdt", qkv, proj_grad, preferred_element_type=F32).astype(BF16)
-    g_qkv = jnp.einsum("sdt,ste->sde", act[:3], proj_grad, preferred_element_type=F32).astype(BF16)
-    g_out = jnp.einsum("dt,te->de", branch_grad, context_rows, preferred_element_type=F32).astype(BF16)
-    g_up = jnp.einsum("dt,tf->df", act[3], up_grad_low, preferred_element_type=F32).astype(BF16)
-    g_down = jnp.einsum("dt,tf->df", branch_grad, hidden, preferred_element_type=F32).astype(BF16)
+        part, streams, out_cot, small_all, square(mix_out), next_rows
+    )
+    attn_in_grad, mlp_in_grad, g_qkv, g_out, g_up, g_down = back(
+        branch_grad, act, qkv, out, up, down, rows, context, sums, hidden, slope, cos, sin
+    )
     grid = (n_dp // HIGH, 2, 2, 2 * mix_in.shape[0])
     stream_grad, mix_grad, small_total, tiny, qkv_total, up_total, down_total, out_total = scatter(
         n_dp, attn_in_grad, mlp_in_grad, streams, small_all, wide_grad, mixin_part, tiny, history,
         g_qkv.reshape((3,) + grid + (-1,)), g_up.reshape(grid + (-1,)), g_down.reshape(grid + (-1,)),
         g_out.reshape(grid + (-1,)),
     )
-    mix_rows = jnp.transpose(mix_all.reshape(2, n_dp, MIXH, half), (2, 1, 0, 3)).reshape(MIXH, n_dp * seq_len)
     history_grad = jnp.stack(
         [
             sum(
@@ -2233,8 +2424,8 @@
         ]
     ).astype(BF16)
     return (
-        block.T,
-        next_mix.T.reshape(seq_len, STREAMS, NEXT),
+        block,
+        (next_mix.T + mix_static).reshape(seq_len, STREAMS, NEXT),
         history_grad,
         mix_grad[: STREAMS * HIST].T.reshape(seq_len, STREAMS, HIST),
         qkv_total.astype(F32),

time: 736 us -> 679 us (0.923)
  matrix products: 92.1 us -> 0 us
  Pallas kernels: 565 us -> 638 us
  local copies, waits for them, and re-layouts: 47.5 us -> 23.3 us
    dot_general x18 -> x0, matrix products: 92.1 us -> none  [the longest x1 17.3 us: per_device(): up_pre = jnp.einsum('dt,df->tf', act[3], up, preferred_element_type=F32)]
    pallas_call x0 -> x1, Pallas kernels: none -> 52.6 us  [back(): pl.pallas_call(back_kernel, out_shape=[jax.ShapeDtypeStruct(shape, BF16)...]
    pallas_call x1, Pallas kernels: 241 us -> 256 us  [gather(): pl.pallas_call(functools.partial(gather_kernel, n_dp), out_shape=[jax.Sha...]
    unnamed x134 -> x30, local copies, waits for them, and re-layouts: 23.6 us -> 13.1 us
    reshape x7 -> x3, local copies, waits for them, and re-layouts: 8.45 us -> 0.03 us  [the longest x1 0.01 us: per_device(): (next_mix.T + mix_static).reshape(seq_len, STREAMS, NEXT)]
where the time goes in v3:
time: 679 us; the launch traced here: 678 us
  Pallas kernels  638 us (94%)
  local copies, waits for them, and re-layouts  23.3 us (3%)
  other arithmetic  15.1 us (2%)
    pallas_call x1, Pallas kernels, gather(): pl.pallas_call(functools.partial(gather_kernel, n_dp), out_shape=[jax.Sha...  256 us
    pallas_call x1, Pallas kernels, scatter(): pl.pallas_call(functools.partial(scatter_kernel, n_dp), out_shape=[jax.Sh...  256 us
    pallas_call x1, Pallas kernels, join(): pl.pallas_call(join_kernel, out_shape=[jax.ShapeDtypeStruct(*shape) for s...  73.3 us
    pallas_call x1, Pallas kernels, back(): pl.pallas_call(back_kernel, out_shape=[jax.ShapeDtypeStruct(shape, BF16)...  52.6 us

profile of v3, /device:TPU:7, one launch (start us, length us, event | category | flops | bytes accessed | tf_op | source)
XLA Modules:
  0.0 677.7 jit_solution(9079876105434817668)
XLA Ops:
  3.1 0.8 copy.39
  4.6 1.3 pad.8.mix_out
  8.8 256.4 %gather.1 = (f32[36,4096]{1,0:T(8,128)}, bf16[2,2,2,2,128,128]{5,4,3,2,1,0:T(8,128)(2,1)}, bf16[4,2048,128]{2,1,0:T(8,128)(2,1)}, bf16[4,2048,1024]{2,1,0:T(8,12...) custom-call(bf16[9,128,4096]{2,1,0:T(8,128)(2,1)} %hist.3, ...), custom_call_target="tpu_custom_call" | custom-call | tf_op jit(solution)/shard_map/gather/pallas_call | solution.py:553
  265.2 2.1 fusion.46
  267.3 2.1 fusion.45
  269.4 73.3 %join.1 = (bf16[2048,1024]{1,0:T(8,128)(2,1)}, f32[2048,128]{1,0:T(8,128)}, bf16[256,2048]{1,0:T(8,128)(2,1)}, f32[40,256]{1,0:T(8,128)}, f32[2048,128]{1,0:T(8,128)}, /*index=5*/f32[40,128]{1,0:T(8,128)}) custom-call(bf16[2048,1024]{1,0:T(8,128)(2,1)} %get-tuple-element.47.part, bf16[4,2048,128]{2,1,0:T(8,128)(2,1)} %get-tuple-element.48.streams, ...), custom_call_target="tpu_custom_call" | custom-call | tf_op jit(solution)/shard_map/join/pallas_call | solution.py:1709
  342.7 52.6 %back.1 = (bf16[3,2048,1024]{2,1,0:T(8,128)(2,1)}, bf16[2048,1024]{1,0:T(8,128)(2,1)}, bf16[3,2048,256]{2,1,0:T(8,128)(2,1)}, bf16[2048,256]{1,0:T(8,128)(2,1)},...) custom-call(bf16[2048,1024]{1,0:T(8,128)(2,1)} %get-tuple-element.53.grad, ...), custom_call_target="tpu_custom_call" | custom-call | tf_op jit(solution)/shard_map/back/pallas_call | solution.py:1857
  395.3 256.2 %scatter.1 = (bf16[4,128,4096]{2,1,0:T(8,128)(2,1)}, f32[40,256]{1,0:T(8,128)}, f32[128,128]{1,0:T(8,128)}, f32[40,128]{1,0:T(8,128)}, bf16[3,128,1024]{2,1,0:T(...) custom-call(bf16[3,2048,1024]{2,1,0:T(8,128)(2,1)} %get-tuple-element.64.attn_grad, ...), custom_call_target="tpu_custom_call" | custom-call | tf_op jit(solution)/shard_map/scatter/pallas_call | solution.py:2298
  651.5 0.9 slice_bitcast_fusion.2
  652.4 1.5 slice_reduce_fusion
  653.9 1.5 copy.45
  656.8 1.0 slice_bitcast_fusion
  659.1 1.8 convert_element_type.130
  660.9 1.3 convert_element_type.129
  662.2 1.5 convert_element_type.131
  663.7 1.5 convert_element_type.132
  665.8 0.9 fusion.44
  666.7 0.8 fusion.43
  669.1 0.8 fusion.40
  669.9 0.8 fusion.39
  671.6 0.8 fusion.37
  672.4 0.8 fusion.36
  673.6 1.0 copy.56
  675.2 2.5 copy-done.5
  (43 shorter events, 12.6 us)
Async XLA Ops:
  395.2 260.8 %copy-start.7 = (f32[40,256]{1,0:T(8,128)S(1)}, f32[40,256]{1,0:T(8,128)}, u32[]{:S(2)}) copy-start(f32[40,256]{1,0:T(8,128)} %get-tuple-element.51) | copy-start | bytes 122884
  395.2 260.8 %copy-start.8 = (f32[40]{0:T(128)S(1)}, f32[40]{0:T(128)}, u32[]{:S(2)}) copy-start(f32[40]{0:T(128)} %param.23) | copy-start | bytes 484
  651.5 9.4 %copy-start.4 = (bf16[3,128,1024]{2,1,0:T(8,128)(2,1)S(1)}, bf16[3,128,1024]{2,1,0:T(8,128)(2,1)}, u32[]{:S(2)}) copy-start(bf16[3,128,1024]{2,1,0:T(8,128)(2,1)} %get-tuple-element.75) | copy-start | bytes 2359300
  652.4 9.8 %copy-start.2 = (bf16[128,4096]{1,0:T(8,128)(2,1)S(1)}, bf16[128,4096]{1,0:T(8,128)(2,1)}, u32[]{:S(2)}) copy-start(bf16[128,4096]{1,0:T(8,128)(2,1)} %get-tuple-element.77) | copy-start | bytes 3145732
  660.9 2.9 copy-start.1
  662.2 3.6 copy-start
  672.4 1.2 copy-start.3
  673.6 4.1 copy-start.5
  673.6 1.0 copy-start.6

commit v4 on v3

--- a/solution.py
+++ b/solution.py
@@ -152,7 +152,7 @@
 ):
     here = Place()
     me, tensor = here.me, here.tensor
-    rows = small.shape[0]
+    rows = small.shape[1]
     depth = rows * n_dp
     half = hist.shape[2] // n_dp // 2
     high_bits = int(math.log2(n_dp // HIGH))
@@ -172,10 +172,7 @@
             block, target = buf.at[:, :, :, here.core], flip(me, CORE)
         return remote(block, block, early_s.at[which, phase], early_r.at[which, phase], dp=target)
 
-    own = [
-        pltpu.make_async_copy(mix, mix_all.at[here.high, here.near, here.side, here.core], own_sem.at[0]),
-        pltpu.make_async_copy(small, small_all.at[here.high, here.near, here.side, here.core], own_sem.at[1]),
-    ]
+    own_mix = pltpu.make_async_copy(mix, mix_all.at[here.high, here.near, here.side, here.core], own_sem.at[0])
     units = []
     for w, o in weights:
         if len(w.shape) == 3:
@@ -348,10 +345,9 @@
         for near in range(2):
             act_core(stream, near).start()
 
-    for copy in own:
-        copy.start()
-    for copy in own:
-        copy.wait()
+    own_mix.start()
+    small_all[here.high, here.near, here.side, here.core] = small[...].T
+    own_mix.wait()
     for which, buf in early_pairs:
         early(which, buf, 0).start()
     total = len(units)
@@ -519,7 +515,7 @@
 
 
 def gather(n_dp, hist, mix, small, w_qkv, w_out, w_up, w_down, cos, sin):
-    rows = small.shape[0]
+    rows = small.shape[1]
     depth = rows * n_dp
     half = hist.shape[2] // n_dp // 2
     high = n_dp // HIGH
@@ -553,7 +549,7 @@
     return pl.pallas_call(
         functools.partial(gather_kernel, n_dp),
         out_shape=[jax.ShapeDtypeStruct(*shape) for shape in shapes],
-        in_specs=[ANY] * 7 + [VM] * 2,
+        in_specs=[ANY, ANY, VM] + [ANY] * 4 + [VM] * 2,
         out_specs=[ANY] * 14,
         scratch_shapes=[
             pltpu.VMEM(grid + mix.shape, F32),
@@ -1492,69 +1488,11 @@
     return at(near * 4 * half + core * 2 * half + half_at * half, count * half, half)
 
 
-def reduce_group(here, half, part, theirs, own, from_core, from_tensor, from_near, sems, local, pieces, piece):
-    core_s, core_r, tensor_s, tensor_r, near_s, near_r = sems
-
-    def load(span, near, half_at):
-        return pltpu.make_async_copy(
-            part.at[piece(span), lane_block(half, near, here.core, half_at, 1)],
-            own.at[near, half_at, piece(span)], local.at[span, near * 2 + half_at],
-        )
-
-    def to_core(span, near, half_at):
-        return remote(
-            part.at[piece(span), lane_block(half, near, 1 - here.core, half_at, 1)],
-            from_core.at[near, half_at, piece(span)],
-            core_s.at[span, near * 2 + half_at], core_r.at[span, near * 2 + half_at], dp=flip(here.me, CORE),
-        )
-
-    def to_tensor(span, near):
-        return remote(
-            own.at[near, here.other, piece(span)], from_tensor.at[near, piece(span)],
-            tensor_s.at[span, near], tensor_r.at[span, near], tensor=here.other,
-        )
-
-    def to_near(span):
-        return remote(
-            from_tensor.at[1 - here.near, piece(span)], from_near.at[piece(span)],
-            near_s.at[span], near_r.at[span], dp=flip(here.me, NEAR),
-        )
-
-    def start(span):
-        for near in range(2):
-            for half_at in range(2):
-                to_core(span, near, half_at).start()
-                load(span, near, half_at).start()
-
-    def after_core(span):
-        for near in range(2):
-            for half_at in range(2):
-                load(span, near, half_at).wait()
-                to_core(span, near, half_at).wait()
-            own[near, here.other, piece(span)] += from_core[near, here.other, piece(span)]
-            to_tensor(span, near).start()
-        for near in range(2):
-            own[near, here.tensor, piece(span)] += from_core[near, here.tensor, piece(span)]
-
-    def after_tensor(span):
-        for near in range(2):
-            to_tensor(span, near).wait()
-        far = 1 - here.near
-        from_tensor[far, piece(span)] += own[far, here.tensor, piece(span)]
-        to_near(span).start()
-        from_tensor[here.near, piece(span)] += own[here.near, here.tensor, piece(span)]
-
-    def after_near(span):
-        to_near(span).wait()
-
-    return start, after_core, after_tensor, after_near
-
-
 def join_kernel(
-    part, streams, out_cot, small, mix_out, next_cot,
+    part, streams, out_cot, small, mix_raw, next_raw,
     o_grad, o_wide, o_block, o_next, o_mixin, o_tiny,
-    own, from_core, from_tensor, from_near, residual, wide, normed, block, cot, cot_in, back, low, next_rows, mixin, tiny,
-    core_s, core_r, tensor_s, tensor_r, near_s, near_r, local, share_s, share_r, own_sem,
+    mix_out, next_cot, own, from_core, from_first, from_second, residual, wide, normed, block, cot, cot_in, back, low, next_rows, mixin, tiny,
+    core_s, core_r, first_s, first_r, second_s, second_r, local, share_s, share_r, own_sem,
 ):
     here = Place()
     me, tensor = here.me, here.tensor
@@ -1567,20 +1505,83 @@
     def piece(span):
         return pl.ds(span * size, size)
 
-    start, after_core, after_tensor, after_near = reduce_group(
-        here, half, part, None, own, from_core, from_tensor, from_near,
-        (core_s, core_r, tensor_s, tensor_r, near_s, near_r), local, spans, piece,
-    )
+    def tensor_first(span):
+        return span < spans // 2
+
+    def load(span, near, half_at):
+        return pltpu.make_async_copy(
+            part.at[piece(span), lane_block(half, near, here.core, half_at, 1)],
+            own.at[near, half_at, piece(span)], local.at[span, near * 2 + half_at],
+        )
+
+    def to_core(span, near, half_at):
+        return remote(
+            part.at[piece(span), lane_block(half, near, 1 - here.core, half_at, 1)],
+            from_core.at[near, half_at, piece(span)],
+            core_s.at[span, near * 2 + half_at], core_r.at[span, near * 2 + half_at], dp=flip(me, CORE),
+        )
+
+    across = {"tensor": here.other}
+    beside = {"dp": flip(me, NEAR)}
+
+    def first_hop(span, block):
+        source = own.at[block, here.other, piece(span)] if tensor_first(span) else own.at[1 - here.near, block, piece(span)]
+        return remote(
+            source, from_first.at[block, piece(span)], first_s.at[span, block], first_r.at[span, block],
+            **(across if tensor_first(span) else beside),
+        )
+
+    def kept(span):
+        return here.near if tensor_first(span) else tensor
+
+    def second_hop(span):
+        return remote(
+            from_first.at[1 - kept(span), piece(span)], from_second.at[piece(span)], second_s.at[span], second_r.at[span],
+            **(beside if tensor_first(span) else across),
+        )
+
+    def start(span):
+        for near in range(2):
+            for half_at in range(2):
+                to_core(span, near, half_at).start()
+                load(span, near, half_at).start()
+
+    def after_core(span):
+        for near in range(2):
+            for half_at in range(2):
+                load(span, near, half_at).wait()
+                to_core(span, near, half_at).wait()
+                own[near, half_at, piece(span)] += from_core[near, half_at, piece(span)]
+        for block in range(2):
+            first_hop(span, block).start()
+
+    def after_first(span):
+        for block in range(2):
+            first_hop(span, block).wait()
+
+        def add(block):
+            mine = own[block, tensor, piece(span)] if tensor_first(span) else own[here.near, block, piece(span)]
+            from_first[block, piece(span)] += mine
+
+        add(1 - kept(span))
+        second_hop(span).start()
+        add(kept(span))
+
+    mix_out[...] = jnp.zeros_like(mix_out)
+    next_cot[...] = jnp.zeros_like(next_cot)
+    mix_out[:MIXH, : STREAMS * NEXT] = mix_raw[...]
+    next_cot[: STREAMS * NEXT, :] = next_raw[...]
     fetch = pltpu.make_async_copy(streams.at[3], residual, own_sem.at[0])
     fetch.start()
     cot_fetch = pltpu.make_async_copy(out_cot.at[at(tensor * half, half), :], cot_in, own_sem.at[7])
     cot_fetch.start()
-    for span in range(spans):
+    order = [span for pair in zip(range(spans // 2), range(spans // 2, spans)) for span in pair]
+    for span in order:
         start(span)
-    for span in range(spans):
+    for span in order:
         after_core(span)
-    for span in range(spans):
-        after_tensor(span)
+    for span in order:
+        after_first(span)
     fetch.wait()
     cot_fetch.wait()
 
@@ -1590,12 +1591,12 @@
 
     loop(0, depth // chunk, turn)
     squares = jnp.zeros((1, half), F32)
-    for span in range(spans):
-        after_near(span)
+    for span in order:
+        second_hop(span).wait()
 
         def widen(index, total):
             rows = at(span * size + index * chunk, chunk)
-            branch = from_tensor[here.near, rows, :].astype(F32) + from_near[rows, :].astype(F32)
+            branch = from_first[kept(span), rows, :].astype(F32) + from_second[rows, :].astype(F32)
             value = residual[rows, :].astype(F32) + branch
             wide[rows, :] = value
             block[:, rows] = value.T.astype(BF16)
@@ -1644,20 +1645,23 @@
 
     loop(0, depth // chunk, finish)
 
-    def share(kind, index):
-        if kind == 0:
-            source, lanes, where = low, lane_block(half, here.near, here.core, tensor, 1), {"dp": flip(me, NEAR)}
-        elif kind == 1:
-            lanes = lane_block(half, 1 - here.near if index else here.near, here.core, tensor, 1)
-            source, where = (o_grad.at[:, lanes] if index else low), {"tensor": here.other}
+    def share(part_at, kind, index=0):
+        rows = pl.ds(part_at * (depth // 2), depth // 2)
+        number = 2 + part_at * 5 + kind + index
+        if kind < 2:
+            source, lanes, where = low.at[rows], lane_block(half, here.near, here.core, tensor, 1), (beside, across)[kind]
+        elif kind == 2:
+            far, where = (1 - here.near, across) if part_at == 0 else (here.near, beside)
+            lanes = lane_block(half, far, here.core, tensor if part_at == 0 else here.other, 1)
+            source = o_grad.at[rows, lanes]
         else:
             lanes, where = lane_block(half, index, here.core, 0, 2), {"dp": flip(me, CORE)}
-            source = o_grad.at[:, lanes]
-        number = 1 + 2 * kind + index
-        return remote(source, o_grad.at[:, lanes], share_s.at[number], share_r.at[number], **where)
-
-    share(0, 0).start()
-    share(1, 0).start()
+            source = o_grad.at[rows, lanes]
+        return remote(source, o_grad.at[rows, lanes], share_s.at[number], share_r.at[number], **where)
+
+    for part_at in range(2):
+        share(part_at, 0).start()
+        share(part_at, 1).start()
     keep = pltpu.make_async_copy(
         low, o_grad.at[:, lane_block(half, here.near, here.core, tensor, 1)], own_sem.at[2]
     )
@@ -1668,10 +1672,11 @@
         mixin[rows, :] = nt(normed[rows, :], inner_grad)
 
     loop(0, depth // chunk, mixin_rows)
-    share(0, 0).wait()
-    share(1, 1).start()
+    for part_at in range(2):
+        share(part_at, part_at).wait()
+        share(part_at, 2).start()
     lanes = at(tensor * half, half)
-    next_share = remote(next_rows, o_next.at[:, lanes], share_s.at[7], share_r.at[7], tensor=here.other)
+    next_share = remote(next_rows, o_next.at[:, lanes], share_s.at[1], share_r.at[1], tensor=here.other)
     next_share.start()
     finals = [
         pltpu.make_async_copy(next_rows, o_next.at[:, lanes], own_sem.at[3]),
@@ -1682,12 +1687,14 @@
     for copy in finals:
         copy.start()
     keep.wait()
-    share(1, 0).wait()
-    share(1, 1).wait()
-    for near in range(2):
-        share(2, near).start()
-    for near in range(2):
-        share(2, near).wait()
+    for part_at in range(2):
+        share(part_at, 1 - part_at).wait()
+        share(part_at, 2).wait()
+        for near in range(2):
+            share(part_at, 3, near).start()
+    for part_at in range(2):
+        for near in range(2):
+            share(part_at, 3, near).wait()
     share_block(0).wait()
     share_block(1).wait()
     next_share.wait()
@@ -1712,6 +1719,8 @@
         in_specs=[ANY] * 3 + [VM] * 3,
         out_specs=[ANY] * 6,
         scratch_shapes=[
+            pltpu.VMEM((128, 128), BF16),
+            pltpu.VMEM((128, half), F32),
             pltpu.VMEM((2, 2, depth, half), BF16),
             pltpu.VMEM((2, 2, depth, half), BF16),
             pltpu.VMEM((2, depth, half), BF16),
@@ -1734,8 +1743,8 @@
             DMA((spans,)),
             DMA((spans,)),
             DMA((spans, 4)),
-            DMA((8,)),
-            DMA((8,)),
+            DMA((12,)),
+            DMA((12,)),
             DMA((8,)),
         ],
         compiler_params=pltpu.CompilerParams(
@@ -1746,55 +1755,47 @@
 
 
 def back_kernel(
-    grad, act, w_qkv, w_out, w_up, w_down, rows, context, sums, hidden, slope, cos, sin,
-    o_attn, o_mlp, o_qkv, o_out, o_up, o_down,
-    grad_in, act_in, qkv_in, out_in, up_in, down_in, rows_in, context_in, sums_in, hidden_in, slope_in,
-    up_grad, context_grad, row_grad, tall, wide, load_sem, tall_sem, wide_sem,
+    grad, w_qkv, w_out, w_up, w_down, rows, sums, slope, cos, sin,
+    o_attn, o_mlp, o_up_grad, o_row_grad,
+    grad_in, qkv_in, out_in, up_in, down_in, rows_in, sums_in, slope_in,
+    up_grad, context_grad, row_grad, tall, load_sem, tall_sem, save_sem,
 ):
     depth, tokens = grad.shape
     seq_len = sums.shape[1]
-    heads = context.shape[0] // HD
+    heads = rows.shape[1] // HD
     tile = 256
     loads = {}
     pairs = (
-        ("grad", grad, grad_in), ("down", w_down, down_in), ("slope", slope, slope_in), ("hidden", hidden, hidden_in),
-        ("up", w_up, up_in), ("out", w_out, out_in), ("rows", rows, rows_in), ("sums", sums, sums_in),
-        ("context", context, context_in), ("qkv", w_qkv, qkv_in), ("act3", act.at[3], act_in.at[0]),
+        ("grad", grad, grad_in), ("down", w_down, down_in), ("slope", slope, slope_in), ("up", w_up, up_in),
+        ("out", w_out, out_in), ("rows", rows, rows_in), ("sums", sums, sums_in), ("qkv", w_qkv, qkv_in),
     )
     for number, (name, source, target) in enumerate(pairs):
         loads[name] = pltpu.make_async_copy(source, target, load_sem.at[number])
         loads[name].start()
 
-    def act_load(stream):
-        slot = (stream + 1) % 2
-        return pltpu.make_async_copy(act.at[stream], act_in.at[slot], load_sem.at[len(pairs) + slot])
-
-    act_load(0).start()
-
     pending = {}
 
-    def write(kind, turn, out, width, compute):
-        buf, sem = (tall, tall_sem) if kind == "tall" else (wide, wide_sem)
-        slots = buf.shape[1]
-        if (kind, turn) in pending:
-            pending.pop((kind, turn))()
+    def write(turn, out, compute):
+        slots = tall.shape[1]
+        if turn in pending:
+            pending.pop(turn)()
 
         def copy(index):
             slot = lax.rem(index, slots)
             target = out.at[at(index * tile, tile), :]
-            return pltpu.make_async_copy(buf.at[turn, slot, :, pl.ds(0, width)], target, sem.at[turn, slot])
+            return pltpu.make_async_copy(tall.at[turn, slot], target, tall_sem.at[turn, slot])
 
         def body(index):
             @pl.when(index >= slots)
             def _():
                 copy(index - slots).wait()
 
-            buf[turn, lax.rem(index, slots), :, :width] = compute(at(index * tile, tile)).astype(BF16)
+            tall[turn, lax.rem(index, slots)] = compute(at(index * tile, tile)).astype(BF16)
             copy(index).start()
 
         steps = depth // tile
         loop(0, steps, body)
-        pending[kind, turn] = lambda: loop(steps - slots, steps, lambda index: copy(index).wait())
+        pending[turn] = lambda: loop(steps - slots, steps, lambda index: copy(index).wait())
 
     for name in ("grad", "down", "slope"):
         loads[name].wait()
@@ -1803,10 +1804,12 @@
         span = at(index * tile, tile)
         up_grad[span, :] = (tn(down_in[:, span], grad_in[...]) * slope_in[span, :]).astype(BF16)
 
-    loop(0, hidden.shape[0] // tile, lift)
+    loop(0, up_grad.shape[0] // tile, lift)
     loads["up"].wait()
-    write("tall", 1, o_mlp, tokens, lambda span: nn(up_in[span, :], up_grad[...]))
-    for name in ("out", "rows", "sums", "context"):
+    save_up = pltpu.make_async_copy(up_grad, o_up_grad, save_sem.at[0])
+    save_up.start()
+    write(1, o_mlp, lambda span: nn(up_in[span, :], up_grad[...]))
+    for name in ("out", "rows", "sums"):
         loads[name].wait()
     context_grad[...] = tn(out_in[...], grad_in[...]).astype(BF16)
 
@@ -1828,61 +1831,50 @@
             row_grad[2, lane, span] = value_grad.astype(BF16)
 
     loop(0, tokens // seq_len, attend)
+    save_rows = pltpu.make_async_copy(row_grad, o_row_grad, save_sem.at[1])
+    save_rows.start()
     loads["qkv"].wait()
     for stream in range(3):
-        write("tall", stream % 2, o_attn.at[stream], tokens, lambda span: nn(qkv_in[stream, span, :], row_grad[stream]))
-    loads["hidden"].wait()
-    width, narrow = hidden.shape[0], context.shape[0]
-    write("wide", 0, o_down, width, lambda span: nt(grad_in[span, :], hidden_in[...]))
-    write("wide", 1, o_out, narrow, lambda span: nt(grad_in[span, :], context_in[...]))
-    loads["act3"].wait()
-    write("wide", 0, o_up, width, lambda span: nt(act_in[0, span, :], up_grad[...]))
-    for stream in range(3):
-        slot = (stream + 1) % 2
-        act_load(stream).wait()
-        if stream < 2:
-            act_load(stream + 1).start()
-        write(
-            "wide", (stream + 1) % 2, o_qkv.at[stream], narrow,
-            lambda span: nt(act_in[slot, span, :], row_grad[stream]),
-        )
+        write(stream % 2, o_attn.at[stream], lambda span: nn(qkv_in[stream, span, :], row_grad[stream]))
     for drain in pending.values():
         drain()
-
-
-def back(grad, act, w_qkv, w_out, w_up, w_down, rows, context, sums, hidden, slope, cos, sin):
+    save_up.wait()
+    save_rows.wait()
+
+
+def back(grad, w_qkv, w_out, w_up, w_down, rows, sums, slope, cos, sin):
     depth, tokens = grad.shape
-    weights = (w_qkv, w_out, w_up, w_down)
-    shapes = [(3, depth, tokens), (depth, tokens)] + [w.shape for w in weights]
+    operands = (grad, w_qkv, w_out, w_up, w_down, rows, sums, slope)
+    shapes = [(3, depth, tokens), (depth, tokens), slope.shape, rows.shape]
     return pl.pallas_call(
         back_kernel,
         out_shape=[jax.ShapeDtypeStruct(shape, BF16) for shape in shapes],
-        in_specs=[ANY] * 11 + [VM] * 2,
-        out_specs=[ANY] * 6,
-        scratch_shapes=[pltpu.VMEM((depth, tokens), BF16), pltpu.VMEM((2, depth, tokens), BF16)]
-        + [pltpu.VMEM(v.shape, v.dtype) for v in weights + (rows, context, sums, hidden, slope)]
+        in_specs=[ANY] * 8 + [VM] * 2,
+        out_specs=[ANY] * 4,
+        scratch_shapes=[pltpu.VMEM(v.shape, v.dtype) for v in operands]
         + [
-            pltpu.VMEM(hidden.shape, BF16),
-            pltpu.VMEM(context.shape, BF16),
+            pltpu.VMEM(slope.shape, BF16),
+            pltpu.VMEM(rows.shape[1:], BF16),
             pltpu.VMEM(rows.shape, BF16),
             pltpu.VMEM((2, 4, 256, tokens), BF16),
-            pltpu.VMEM((2, 4, 256, hidden.shape[0]), BF16),
-            DMA((13,)),
+            DMA((8,)),
             DMA((2, 4)),
-            DMA((2, 4)),
+            DMA((2,)),
         ],
         compiler_params=pltpu.CompilerParams(vmem_limit_bytes=56 * 1024 * 1024),
         name="back",
-    )(grad, act, w_qkv, w_out, w_up, w_down, rows, context, sums, hidden, slope, cos, sin)
+    )(*operands, cos, sin)
 
 
 def scatter_kernel(
-    n_dp, attn_grad, mlp_grad, streams, small, wide_grad, mixin_part, mix_tiny, hist, g_qkv, g_up, g_down, g_out,
-    o_stream, o_mix, o_small, o_tiny, o_qkv, o_up, o_down, o_out,
+    n_dp, attn_grad, mlp_grad, streams, small, wide_grad, mixin_part, mix_tiny, hist,
+    branch_grad, act, hidden, up_grad, context, row_grad,
+    o_stream, o_mix, o_small, o_tiny, o_qkv, o_up, o_down, o_out, sent_qkv, sent_up, sent_down, sent_out,
     own, from_core, from_tensor, from_near, rows_in, wide, stream_grad, gains, biases, tiny, tiny_in, tiny_out,
     hist_in, arrived, mix_part, mix_in, mix_sum, tiny_sum, ring, side_in, mine, high_in,
+    hidden_in, up_in, context_in, rows_grad_in, tile_in, stage, tile_sem, stage_sem, right_sem,
     core_s, core_r, tensor_s, tensor_r, near_s, near_r, local, in_sem,
-    side_s, side_r, side_local, high_s, high_r, peer_s, peer_r, peer_local,
+    side_s, side_r, high_s, high_r, peer_s, peer_r, peer_local,
     a2a_s, a2a_r, a2a_own, keep_sem, pass_s, pass_r, tiny_s, tiny_r, mix_s, mix_r, hist_sem,
     ring_s, ring_r, last_s, last_r, last_local,
 ):
@@ -1894,26 +1886,85 @@
     chunk = min(256, depth)
     greet_all(n_dp, me, here.other)
 
-    units = []
-    for g, o in ((g_qkv, o_qkv), (g_up, o_up), (g_down, o_down), (g_out, o_out)):
-        if len(o.shape) == 3:
-            units += [(g.at[part], o.at[part], 0) for part in range(o.shape[0])]
-        else:
-            units += [(g, o, first) for first in range(0, g.shape[-1], UNIT)]
+    highs = n_dp // HIGH
+    tall = 2 * rows
+    arrays = (
+        (branch_grad, hidden_in, sent_down, o_down),
+        (act.at[3], up_in, sent_up, o_up),
+        (branch_grad, context_in, sent_out, o_out),
+    ) + tuple((act.at[s], rows_grad_in.at[s], sent_qkv.at[s], o_qkv.at[s]) for s in range(3))
+    units, first_unit = [], []
+    for _, right, sent, o in arrays:
+        first_unit.append(len(units))
+        units += [(sent, o, first) for first in range(0, right.shape[0], UNIT)]
     total = len(units)
+    rights = [
+        pltpu.make_async_copy(source, target, right_sem.at[number])
+        for number, (source, target) in enumerate(
+            ((hidden, hidden_in), (up_grad, up_in), (context, context_in), (row_grad, rows_grad_in))
+        )
+    ]
 
     def side_hop(unit):
-        g, _, first = units[unit]
+        sent, _, first = units[unit]
         return remote(
-            g.at[:, :, 1 - here.side, :, pl.ds(first, UNIT)], side_in.at[unit], side_s.at[unit], side_r.at[unit],
-            dp=flip(me, SIDE),
-        )
-
-    def side_load(unit):
-        g, _, first = units[unit]
-        return pltpu.make_async_copy(
-            g.at[:, :, here.side, :, pl.ds(first, UNIT)], mine.at[unit], side_local.at[unit]
-        )
+            sent.at[:, :, :, pl.ds(first, UNIT)], side_in.at[unit], side_s.at[unit], side_r.at[unit], dp=flip(me, SIDE)
+        )
+
+    count = highs * 2
+
+    def tile_load(array, block):
+        mine_now = lax.div(block, count)
+        side = here.side * mine_now + (1 - here.side) * (1 - mine_now)
+        row = (lax.rem(block, count) * 2 + side) * tall
+        slot = lax.rem(block, 2)
+        return pltpu.make_async_copy(arrays[array][0].at[at(row, tall), :], tile_in.at[slot], tile_sem.at[slot])
+
+    def product(array, block):
+        @pl.when(block + 1 < 2 * count)
+        def _():
+            tile_load(array, block + 1).start()
+
+        tile_load(array, block).wait()
+        return nt(tile_in[lax.rem(block, 2)], arrays[array][1][...]).astype(BF16)
+
+    def compute_sent(array):
+        _, right, sent, _ = arrays[array]
+        width = right.shape[0]
+
+        def put(block):
+            slot = lax.rem(block, 2)
+            return pltpu.make_async_copy(
+                stage.at[slot, :, pl.ds(0, width)], sent.at[lax.div(block, 2), slot], stage_sem.at[slot]
+            )
+
+        def body(block):
+            value = product(array, block)
+
+            @pl.when(block >= 2)
+            def _():
+                put(block - 2).wait()
+
+            stage[lax.rem(block, 2), :, :width] = value
+            put(block).start()
+
+        tile_load(array, 0).start()
+        loop(0, count, body)
+        put(count - 2).wait()
+        put(count - 1).wait()
+
+    def compute_mine(array):
+        width = arrays[array][1].shape[0]
+
+        def body(block):
+            value = product(array, block)
+            flat = block - count
+            for part in range(width // UNIT):
+                mine[first_unit[array] + part, lax.div(flat, 2), lax.rem(flat, 2)] = value[
+                    :, part * UNIT : (part + 1) * UNIT
+                ]
+
+        loop(count, 2 * count, body)
 
     def high_hop(unit, phase):
         span = 1 << phase
@@ -1941,7 +1992,6 @@
         )
 
     def add_blocks(unit, other, first_mine, first_other, count):
-        tall = 2 * rows
         step = min(64, tall)
 
         def add(flat):
@@ -1950,10 +2000,6 @@
             mine[unit, first_mine + high, near, span] += other[unit, first_other + high, near, span]
 
         loop(0, count * 2 * (tall // step), add)
-
-    def side_start(unit):
-        side_hop(unit).start()
-        side_load(unit).start()
 
     def finish_high(unit):
         for phase in reversed(range(high_bits)):
@@ -1967,10 +2013,9 @@
             peer_hop(unit, peer).start()
 
     def tick(unit):
-        side_load(unit).wait()
         side_hop(unit).wait()
         if unit + 2 < total:
-            side_start(unit + 2)
+            side_hop(unit + 2).start()
         add_blocks(unit, side_in, 0, 0, n_dp // HIGH)
         if unit:
             finish_high(unit - 1)
@@ -1987,7 +2032,7 @@
     def load(stream, near, half_at):
         part = attn_grad.at[stream] if stream < 3 else mlp_grad
         return pltpu.make_async_copy(
-            part.at[:, lane_block(half, near, here.core, half_at, 1)], own.at[stream, near, half_at],
+            part.at[:, lane_block(half, near, here.core, half_at, 1)], own.at[stream % 2, near, half_at],
             local.at[stream, near * 2 + half_at],
         )
 
@@ -2000,7 +2045,7 @@
 
     def to_tensor(stream, near):
         return remote(
-            own.at[stream, near, here.other], from_tensor.at[stream, near],
+            own.at[stream % 2, near, here.other], from_tensor.at[stream, near],
             tensor_s.at[stream, near], tensor_r.at[stream, near], tensor=here.other,
         )
 
@@ -2020,7 +2065,7 @@
             span = at(index * chunk, chunk)
             for near in range(2):
                 for half_at in range(2):
-                    own[stream, near, half_at, span] += from_core[stream, near, half_at, span]
+                    own[stream % 2, near, half_at, span] += from_core[stream, near, half_at, span]
 
         loop(0, depth // chunk, add)
 
@@ -2031,7 +2076,7 @@
         def add(index):
             span = at(index * chunk, chunk)
             for near in range(2):
-                from_tensor[stream, near, span] += own[stream, near, tensor, span]
+                from_tensor[stream, near, span] += own[stream % 2, near, tensor, span]
 
         loop(0, depth // chunk, add)
         to_near(stream).start()
@@ -2104,7 +2149,8 @@
         return at(source_of(step) * 2 * half + tensor * half, half)
 
     def fetch(step):
-        return pltpu.make_async_copy(hist.at[:, :, lanes_of(step)], hist_in.at[step], hist_sem.at[step])
+        slot = lax.rem(step, 2)
+        return pltpu.make_async_copy(hist.at[:, :, lanes_of(step)], hist_in.at[slot], hist_sem.at[slot])
 
     def keep(stream, step):
         return pltpu.make_async_copy(
@@ -2121,23 +2167,27 @@
         return remote(mix_part.at[step], mix_in.at[step], mix_s.at[step], mix_r.at[step], dp=source_of(step))
 
     def receive(stream):
+        fetch(0).start()
         send_own(stream).wait()
 
         def one(step):
+            @pl.when(step + 1 < n_dp)
+            def _():
+                fetch(step + 1).start()
+
             @pl.when(step > 0)
             def _():
                 send(stream, step).wait()
 
             keep(stream, step).start()
             pass_on(stream, step).start()
-            if stream == 0:
-                fetch(step).wait()
+            fetch(step).wait()
             totals = [jnp.zeros((8, half), F32) for _ in range(HIST)]
             for row in range(0, rows, 16):
                 span = pl.ds(row, 16)
                 grad = arrived[stream, step, span, :].astype(F32)
                 for source in range(HIST):
-                    product = grad * hist_in[step, source, span, :].astype(F32)
+                    product = grad * hist_in[lax.rem(step, 2), source, span, :].astype(F32)
                     totals[source] = totals[source] + product[:8] + product[8:]
             for source in range(HIST):
                 mix_part[step, pl.ds(stream * HIST + source, 1), :] = jnp.sum(totals[source], axis=0, keepdims=True)
@@ -2163,42 +2213,62 @@
         if hop + 1 < hops:
             ring_hop(hop + 1).start()
 
-    side_start(0)
+    rights[0].start()
+    inputs = [
+        pltpu.make_async_copy(streams, rows_in, in_sem.at[0]),
+        pltpu.make_async_copy(wide_grad, wide, in_sem.at[1]),
+        pltpu.make_async_copy(mix_tiny, ring.at[0, 0], in_sem.at[2]),
+    ]
+
+    def load_own(stream):
+        for near in range(2):
+            for half_at in range(2):
+                load(stream, near, half_at).start()
+
+    def tensor_start(stream):
+        for near in range(2):
+            to_tensor(stream, near).start()
+
     for stream in range(STREAMS):
         for near in range(2):
             for half_at in range(2):
                 to_core(stream, near, half_at).start()
-                load(stream, near, half_at).start()
-        if stream == 0:
-            side_start(1)
-    loads = [
-        pltpu.make_async_copy(streams, rows_in, in_sem.at[0]),
-        pltpu.make_async_copy(wide_grad, wide, in_sem.at[1]),
-        pltpu.make_async_copy(mix_tiny, ring.at[0, 0], in_sem.at[2]),
-    ]
-    for copy in loads:
+        if stream < 2:
+            load_own(stream)
+    for copy in rights[1:] + inputs:
         copy.start()
+    rights[0].wait()
+    compute_sent(0)
+    side_hop(0).start()
+    side_hop(1).start()
     after_core(0)
-    for near in range(2):
-        to_tensor(0, near).start()
-    for copy in loads:
+    tensor_start(0)
+    compute_mine(0)
+    for copy in rights[1:] + inputs:
         copy.wait()
     ring_hop(0).start()
-    loop(0, n_dp, lambda step: fetch(step).start())
     mix_part[...] = jnp.zeros_like(mix_part)
     for stream in range(STREAMS):
         measure(stream)
-    for stream in range(1, STREAMS):
-        after_core(stream)
+    after_core(1)
     ring_step(0)
+    compute_sent(1)
+    compute_mine(1)
     for stream in range(STREAMS):
         ticks(2)
         after_tensor(stream)
         if stream + 1 < STREAMS:
-            for near in range(2):
-                to_tensor(stream + 1, near).start()
+            tensor_start(stream + 1)
             if stream + 1 < hops:
                 ring_step(stream + 1)
+        if stream + 2 < STREAMS:
+            load_own(stream + 2)
+        if stream == 0:
+            for array in range(2, len(arrays)):
+                compute_sent(array)
+                compute_mine(array)
+        if stream + 2 < STREAMS:
+            after_core(stream + 2)
         if stream > 0:
             back_norm(stream - 1)
         if stream > 1:
@@ -2258,7 +2328,7 @@
     mix_keep.start()
     finish_high(total - 1)
     tiny_share.wait()
-    tiny_out[...] = tiny_sum[0] + tiny_sum[1]
+    tiny_out[...] = (tiny_sum[0] + tiny_sum[1]).T
     tiny_keep = pltpu.make_async_copy(tiny_out, o_small, last_local.at[2])
     tiny_keep.start()
     for unit in range(total):
@@ -2279,29 +2349,34 @@
 
 
 def scatter(
-    n_dp, attn_grad, mlp_grad, streams, small, wide_grad, mixin_part, mix_tiny, hist, g_qkv, g_up, g_down, g_out
+    n_dp, attn_grad, mlp_grad, streams, small, wide_grad, mixin_part, mix_tiny, hist,
+    branch_grad, act, hidden, up_grad, context, row_grad,
 ):
     depth, half = wide_grad.shape
     rows = depth // n_dp
     high = n_dp // HIGH
     high_bits = int(math.log2(high))
-    grads = (g_qkv, g_up, g_down, g_out)
-    units = sum(g.size for g in grads) // depth // UNIT
+    tokens = act.shape[2]
+    narrow, width = context.shape[0], hidden.shape[0]
+    widths = ((3,), narrow), ((), width), ((), width), ((), narrow)
+    units = (4 * narrow + 2 * width) // UNIT
     hops = high_bits + 4
 
     outs = [
         ((STREAMS, rows, 2 * half * n_dp), BF16),
         ((MIXH, 2 * half), F32),
-        ((rows, 128), F32),
+        ((128, rows), F32),
         (mix_tiny.shape, F32),
-    ] + [((3,) * (g.ndim == 6) + (rows, QUARTERS * g.shape[-1]), BF16) for g in grads]
+    ]
+    outs += [(lead + (rows, QUARTERS * size), BF16) for lead, size in widths]
+    outs += [(lead + (high, 2, 2 * rows, size), BF16) for lead, size in widths]
     return pl.pallas_call(
         functools.partial(scatter_kernel, n_dp),
         out_shape=[jax.ShapeDtypeStruct(*shape) for shape in outs],
-        in_specs=[ANY, ANY, ANY, VM, ANY, ANY, ANY, ANY] + [ANY] * 4,
-        out_specs=[ANY] * 8,
+        in_specs=[ANY, ANY, ANY, VM] + [ANY] * 10,
+        out_specs=[ANY] * 12,
         scratch_shapes=[
-            pltpu.VMEM((STREAMS, 2, 2, depth, half), BF16),
+            pltpu.VMEM((2, 2, 2, depth, half), BF16),
             pltpu.VMEM((STREAMS, 2, 2, depth, half), BF16),
             pltpu.VMEM((STREAMS, 2, depth, half), BF16),
             pltpu.VMEM((STREAMS, depth, half), BF16),
@@ -2312,8 +2387,8 @@
             pltpu.VMEM((2, depth, half), F32),
             pltpu.VMEM((depth, 128), BF16),
             pltpu.VMEM((n_dp, rows, 128), BF16),
-            pltpu.VMEM((rows, 128), F32),
-            pltpu.VMEM((n_dp, HIST, rows, half), BF16),
+            pltpu.VMEM((128, rows), F32),
+            pltpu.VMEM((2, HIST, rows, half), BF16),
             pltpu.VMEM((STREAMS, n_dp, rows, half), BF16),
             pltpu.VMEM((n_dp, MIXH, half), F32),
             pltpu.VMEM((n_dp, MIXH, half), F32),
@@ -2323,6 +2398,15 @@
             pltpu.VMEM((units, high, 2, 2 * rows, UNIT), BF16),
             pltpu.VMEM((units, high, 2, 2 * rows, UNIT), BF16),
             pltpu.VMEM((units, high - 1, 2, 2 * rows, UNIT), BF16),
+            pltpu.VMEM(hidden.shape, BF16),
+            pltpu.VMEM(up_grad.shape, BF16),
+            pltpu.VMEM(context.shape, BF16),
+            pltpu.VMEM(row_grad.shape, BF16),
+            pltpu.VMEM((2, 2 * rows, tokens), BF16),
+            pltpu.VMEM((2, 2 * rows, width), BF16),
+            DMA((2,)),
+            DMA((2,)),
+            DMA((4,)),
             DMA((STREAMS, 4)),
             DMA((STREAMS, 4)),
             DMA((STREAMS, 2)),
@@ -2331,7 +2415,6 @@
             DMA((STREAMS,)),
             DMA((STREAMS, 4)),
             DMA((3,)),
-            DMA((units,)),
             DMA((units,)),
             DMA((units,)),
             DMA((units, high_bits)),
@@ -2349,7 +2432,7 @@
             DMA((n_dp,)),
             DMA((n_dp,)),
             DMA((n_dp,)),
-            DMA((n_dp,)),
+            DMA((2,)),
             DMA((hops,)),
             DMA((hops,)),
             DMA((2,)),
@@ -2360,7 +2443,10 @@
             collective_id=3, has_side_effects=True, vmem_limit_bytes=62 * 1024 * 1024
         ),
         name="scatter",
-    )(attn_grad, mlp_grad, streams, small, wide_grad, mixin_part, mix_tiny, hist, *grads)
+    )(
+        attn_grad, mlp_grad, streams, small, wide_grad, mixin_part, mix_tiny, hist, branch_grad, act, hidden, up_grad,
+        context, row_grad,
+    )[:8]
 
 
 def rotary_tables(length, rotary, float_type):
@@ -2371,6 +2457,52 @@
     )
     angles = places[:, None] * frequency[None, :]
     return (jnp.cos(angles), jnp.sin(angles))
+
+
+def finish_kernel(mix_rows, stream_grad, *refs):
+    narrow, history_grad, wide = refs[:4], refs[4], refs[5:]
+    rows = stream_grad.shape[1]
+    tile, span = min(32, rows), 512
+
+    def body(index):
+        row = at(lax.rem(index, rows // tile) * tile, tile)
+        lane = at(lax.div(index, rows // tile) * span, span)
+        grads = [stream_grad[stream, row, lane].astype(F32) for stream in range(STREAMS)]
+        for source in range(HIST):
+            total = sum(
+                mix_rows[pl.ds(stream * HIST + source, 1), lane] * grads[stream] for stream in range(STREAMS)
+            )
+            history_grad[source, row, lane] = total.astype(BF16)
+
+    loop(0, rows // tile * (stream_grad.shape[2] // span), body)
+    for low, full in zip(narrow, wide):
+        full[...] = low[...].astype(F32)
+
+
+def finish(mix_rows, stream_grad, *grads):
+    rows, tokens = stream_grad.shape[1:]
+    steps = rows // 16
+    lanes = tokens // steps
+
+    def weight(g):
+        if g.ndim == 3:
+            return pl.BlockSpec((g.shape[0], 16, g.shape[2]), lambda i: (0, i, 0))
+        return pl.BlockSpec((16, g.shape[1]), lambda i: (i, 0))
+
+    def along(count):
+        return pl.BlockSpec((count, rows, lanes), lambda i: (0, 0, i))
+
+    return pl.pallas_call(
+        finish_kernel,
+        grid=(steps,),
+        out_shape=[jax.ShapeDtypeStruct((HIST, rows, tokens), BF16)]
+        + [jax.ShapeDtypeStruct(g.shape, F32) for g in grads],
+        in_specs=[pl.BlockSpec((mix_rows.shape[0], lanes), lambda i: (0, i)), along(STREAMS)]
+        + [weight(g) for g in grads],
+        out_specs=[along(HIST)] + [weight(g) for g in grads],
+        compiler_params=pltpu.CompilerParams(vmem_limit_bytes=60 * 1024 * 1024),
+        name="finish",
+    )(mix_rows, stream_grad, *grads)
 
 
 def per_device(
@@ -2387,7 +2519,7 @@
 
     mix_rows = own_half(mix_weights.reshape(seq_len, -1)).T
     small = jnp.concatenate(
-        [mix_in, norm_gain.T, norm_bias.T, jnp.zeros((mix_in.shape[0], 128 - MIXH - 4), BF16)], axis=1
+        [mix_in.T, norm_gain, norm_bias, jnp.zeros((128 - MIXH - 4, mix_in.shape[0]), BF16)], axis=0
     )
     cos, sin = (table.T for table in rotary_tables(seq_len, ROT, F32))
     mix_rows, small_all, streams, act, qkv, out, up, down, rows, context, sums, hidden, slope, part = gather(
@@ -2398,43 +2530,32 @@
         qkv.reshape(3, depth, -1), up.reshape(depth, -1), down.reshape(depth, -1), out.reshape(depth, -1)
     )
 
-    def square(values):
-        return jnp.pad(values, ((0, 128 - values.shape[0]), (0, 128 - values.shape[1])))
-
-    next_rows = jnp.pad(own_half(next_cot.reshape(seq_len, -1)).T, ((0, 128 - STREAMS * NEXT), (0, 0)))
+    next_rows = own_half(next_cot.reshape(seq_len, -1)).T
     branch_grad, wide_grad, block, next_mix, mixin_part, tiny = join(
-        part, streams, out_cot, small_all, square(mix_out), next_rows
-    )
-    attn_in_grad, mlp_in_grad, g_qkv, g_out, g_up, g_down = back(
-        branch_grad, act, qkv, out, up, down, rows, context, sums, hidden, slope, cos, sin
-    )
-    grid = (n_dp // HIGH, 2, 2, 2 * mix_in.shape[0])
+        part, streams, out_cot, small_all, mix_out, next_rows
+    )
+    attn_in_grad, mlp_in_grad, up_grad, row_grad = back(
+        branch_grad, qkv, out, up, down, rows, sums, slope, cos, sin
+    )
     stream_grad, mix_grad, small_total, tiny, qkv_total, up_total, down_total, out_total = scatter(
         n_dp, attn_in_grad, mlp_in_grad, streams, small_all, wide_grad, mixin_part, tiny, history,
-        g_qkv.reshape((3,) + grid + (-1,)), g_up.reshape(grid + (-1,)), g_down.reshape(grid + (-1,)),
-        g_out.reshape(grid + (-1,)),
-    )
-    history_grad = jnp.stack(
-        [
-            sum(
-                mix_rows[stream * HIST + source][None, :] * stream_grad[stream].astype(F32)
-                for stream in range(STREAMS)
-            )
-            for source in range(HIST)
-        ]
-    ).astype(BF16)
+        branch_grad, act, hidden, up_grad, context, row_grad,
+    )
+    history_grad, qkv_total, up_total, down_total, out_total = finish(
+        mix_rows, stream_grad, qkv_total, up_total, down_total, out_total
+    )
     return (
         block,
         (next_mix.T + mix_static).reshape(seq_len, STREAMS, NEXT),
         history_grad,
         mix_grad[: STREAMS * HIST].T.reshape(seq_len, STREAMS, HIST),
-        qkv_total.astype(F32),
-        out_total.astype(F32),
-        up_total.astype(F32),
-        down_total.astype(F32),
-        small_total[:, MIXH : MIXH + 2].T,
-        small_total[:, MIXH + 2 : MIXH + 4].T,
-        small_total[:, :MIXH],
+        qkv_total,
+        out_total,
+        up_total,
+        down_total,
+        small_total[MIXH : MIXH + 2],
+        small_total[MIXH + 2 : MIXH + 4],
+        small_total[:MIXH].T,
         tiny[:, : STREAMS * NEXT],
         tiny[: STREAMS * NEXT, MIXH],
     )

time: 679 us -> 646 us (0.951)
  local copies, waits for them, and re-layouts: 23.3 us -> 10.7 us
  other arithmetic: 15.1 us -> 3.06 us
  Pallas kernels: 638 us -> 627 us
    pallas_call x1, Pallas kernels: 52.6 us -> 29.8 us  [back(): pl.pallas_call(back_kernel, out_shape=[jax.ShapeDtypeStruct(shape, BF16)...]
    pallas_call x1, Pallas kernels: 73.3 us -> 60.2 us  [join(): pl.pallas_call(join_kernel, out_shape=[jax.ShapeDtypeStruct(*shape) for s...]
    pallas_call x0 -> x1, Pallas kernels: none -> 12.2 us  [finish(): pl.pallas_call(finish_kernel, grid=(steps,), out_shape=[jax.ShapeDtypeStr...]
    pallas_call x1, Pallas kernels: 256 us -> 268 us  [scatter(): pl.pallas_call(functools.partial(scatter_kernel, n_dp), out_shape=[jax.Sh...]
    unnamed x30 -> x12, local copies, waits for them, and re-layouts: 13.1 us -> 4.45 us
where the time goes in v4:
time: 646 us; the launch traced here: 641 us
  Pallas kernels  627 us (97%)
  local copies, waits for them, and re-layouts  10.7 us (2%)
    pallas_call x1, Pallas kernels, scatter(): pl.pallas_call(functools.partial(scatter_kernel, n_dp), out_shape=[jax.Sh...  268 us
    pallas_call x1, Pallas kernels, gather(): pl.pallas_call(functools.partial(gather_kernel, n_dp), out_shape=[jax.Sha...  256 us
    pallas_call x1, Pallas kernels, join(): pl.pallas_call(join_kernel, out_shape=[jax.ShapeDtypeStruct(*shape) for s...  60.2 us
    pallas_call x1, Pallas kernels, back(): pl.pallas_call(back_kernel, out_shape=[jax.ShapeDtypeStruct(shape, BF16)...  29.8 us

profile of v4, /device:TPU:7, one launch (start us, length us, event | category | flops | bytes accessed | tf_op | source)
XLA Modules:
  0.0 641.2 jit_solution(1679769900234949125)
XLA Ops:
  0.7 0.1 pad.3.clone
  0.7 0.8 multiply_sine_fusion
  1.5 1.4 maximum_maximum_fusion.small
  2.9 0.8 copy.30
  3.7 0.6 dynamic-slice_bitcast_fusion.1.mix
  4.4 0.8 copy.31
  5.2 0.6 dynamic-slice_bitcast_fusion.next_raw
  5.8 256.4 %gather.1 = (f32[36,4096]{1,0:T(8,128)}, bf16[2,2,2,2,128,128]{5,4,3,2,1,0:T(8,128)(2,1)}, bf16[4,2048,128]{2,1,0:T(8,128)(2,1)}, bf16[4,2048,1024]{2,1,0:T(8,12...) custom-call(bf16[9,128,4096]{2,1,0:T(8,128)(2,1)} %hist.3, ...), custom_call_target="tpu_custom_call" | custom-call | tf_op jit(solution)/shard_map/gather/pallas_call | solution.py:549
  262.2 0.0 copy-start.2
  262.2 60.2 %join.1 = (bf16[2048,1024]{1,0:T(8,128)(2,1)}, f32[2048,128]{1,0:T(8,128)}, bf16[256,2048]{1,0:T(8,128)(2,1)}, f32[40,256]{1,0:T(8,128)}, f32[2048,128]{1,0:T(8,128)}, /*index=5*/f32[40,128]{1,0:T(8,128)}) custom-call(bf16[2048,1024]{1,0:T(8,128)(2,1)} %get-tuple-element.50.part, bf16[4,2048,128]{2,1,0:T(8,128)(2,1)} %get-tuple-element.51.streams, ...), custom_call_target="tpu_custom_call" | custom-call | tf_op jit(solution)/shard_map/join/pallas_call | solution.py:1716
  322.4 0.0 copy-done.2
  322.4 0.9 add_bitcast_fusion
  323.3 0.6 copy.32
  323.9 29.8 %back.1 = (bf16[3,2048,1024]{2,1,0:T(8,128)(2,1)}, bf16[2048,1024]{1,0:T(8,128)(2,1)}, bf16[1024,1024]{1,0:T(8,128)(2,1)}, bf16[3,256,1024]{2,1,0:T(8,128)(2,1)}) custom-call(bf16[2048,1024]{1,0:T(8,128)(2,1)} %get-tuple-element.56.grad.branch_grad, bf16[3,2048,256]{2,1,0:T(8,128)(2,1)} %bitcast.27, bf16[2048,256]{1,0:T(8,128)(2,1)} %bitcast.30, ...), custom_call_target="tpu_custom_call" | custom-call | tf_op jit(solution)/shard_map/back/pallas_call | solution.py:1849
  353.7 268.1 %scatter.1 = (bf16[4,128,4096]{2,1,0:T(8,128)(2,1)}, f32[40,256]{1,0:T(8,128)}, f32[128,128]{1,0:T(8,128)}, f32[40,128]{1,0:T(8,128)}, bf16[3,128,1024]{2,1,0:T(...) custom-call(bf16[3,2048,1024]{2,1,0:T(8,128)(2,1)} %get-tuple-elemen, ...), custom_call_target="tpu_custom_call" | custom-call | tf_op jit(solution)/shard_map/scatter/pallas_call | solution.py:2373
  621.9 1.4 slice_reduce_fusion
  623.3 1.3 fusion
  624.6 1.3 slice_bitcast_fusion.1
  626.0 0.8 slice_bitcast_fusion
  626.8 0.6 copy.33
  627.4 12.2 %finish.1 = (bf16[9,128,4096]{2,1,0:T(8,128)(2,1)}, f32[3,128,1024]{2,1,0:T(8,128)}, f32[128,4096]{1,0:T(8,128)}, f32[128,4096]{1,0:T(8,128)}, f32[128,1024]{1,0:T(8,128)}) custom-call(f32[36,4096]{1,0:T(8,128)} %get-tuple-element.55.mix_rows, bf16[4,128,4096]{2,1,0:T(8,128)(2,1)} %get-tuple-element.74.stream_grad, ...), custom_call_target="tpu_custom_call" | custom-call | tf_op jit(solution)/shard_map/finish/pallas_call | solution.py:2495
  639.6 0.0 copy-done
  639.6 1.0 copy.36
  640.6 0.6 copy.37
  (10 shorter events, 0.1 us)
Async XLA Ops:
  262.2 60.2 %copy-start.2 = (f32[40]{0:T(128)S(1)}, f32[40]{0:T(128)}, u32[]{:S(2)}) copy-start(f32[40]{0:T(128)} %param.23) | copy-start | bytes 484
  627.4 12.2 %copy-start = (bf16[256,2048]{1,0:T(8,128)(2,1)S(1)}, bf16[256,2048]{1,0:T(8,128)(2,1)}, u32[]{:S(2)}) copy-start(bf16[256,2048]{1,0:T(8,128)(2,1)} %get-tuple-element.130) | copy-start | bytes 3145732
  627.4 13.2 %copy-start.1 = (f32[40,128]{1,0:T(8,128)S(1)}, f32[40,128]{1,0:T(8,128)}, u32[]{:S(2)}) copy-start(f32[40,128]{1,0:T(8,128)} %get-tuple-element.86) | copy-start | bytes 61444

commit v5 on v4

--- a/solution.py
+++ b/solution.py
@@ -1755,19 +1755,17 @@
 
 
 def back_kernel(
-    grad, w_qkv, w_out, w_up, w_down, rows, sums, slope, cos, sin,
-    o_attn, o_mlp, o_up_grad, o_row_grad,
-    grad_in, qkv_in, out_in, up_in, down_in, rows_in, sums_in, slope_in,
-    up_grad, context_grad, row_grad, tall, load_sem, tall_sem, save_sem,
+    grad, w_out, w_up, w_down, slope,
+    o_mlp, o_up_grad, o_context,
+    grad_in, out_in, up_in, down_in, slope_in,
+    up_grad, context_grad, tall, load_sem, tall_sem, save_sem,
 ):
-    depth, tokens = grad.shape
-    seq_len = sums.shape[1]
-    heads = rows.shape[1] // HD
+    depth = grad.shape[0]
     tile = 256
     loads = {}
     pairs = (
-        ("grad", grad, grad_in), ("down", w_down, down_in), ("slope", slope, slope_in), ("up", w_up, up_in),
-        ("out", w_out, out_in), ("rows", rows, rows_in), ("sums", sums, sums_in), ("qkv", w_qkv, qkv_in),
+        ("grad", grad, grad_in), ("out", w_out, out_in), ("down", w_down, down_in), ("slope", slope, slope_in),
+        ("up", w_up, up_in),
     )
     for number, (name, source, target) in enumerate(pairs):
         loads[name] = pltpu.make_async_copy(source, target, load_sem.at[number])
@@ -1797,7 +1795,12 @@
         loop(0, steps, body)
         pending[turn] = lambda: loop(steps - slots, steps, lambda index: copy(index).wait())
 
-    for name in ("grad", "down", "slope"):
+    for name in ("grad", "out"):
+        loads[name].wait()
+    context_grad[...] = tn(out_in[...], grad_in[...]).astype(BF16)
+    save_context = pltpu.make_async_copy(context_grad, o_context, save_sem.at[1])
+    save_context.start()
+    for name in ("down", "slope"):
         loads[name].wait()
 
     def lift(index):
@@ -1809,70 +1812,47 @@
     save_up = pltpu.make_async_copy(up_grad, o_up_grad, save_sem.at[0])
     save_up.start()
     write(1, o_mlp, lambda span: nn(up_in[span, :], up_grad[...]))
-    for name in ("out", "rows", "sums"):
-        loads[name].wait()
-    context_grad[...] = tn(out_in[...], grad_in[...]).astype(BF16)
-
-    def attend(seq):
-        span = at(seq * seq_len, seq_len)
-        for head in range(heads):
-            lane = pl.ds(head * HD, HD)
-            queries, keys, values = (rows_in[s, lane, span] for s in range(3))
-            prob = jnp.exp(causal_scores(keys, queries) - sums_in[pl.ds(seq * heads + head, 1), :])
-            outer = context_grad[lane, span]
-            value_grad = nt(outer, prob.astype(BF16))
-            prob_grad = tn(values, outer)
-            inner = jnp.sum(prob * prob_grad, axis=0, keepdims=True)
-            score_grad = (prob * (prob_grad - inner)).astype(BF16)
-            query_grad = nn(keys, score_grad) * (1.0 / math.sqrt(HD))
-            key_grad = nt(queries, score_grad) * (1.0 / math.sqrt(HD))
-            row_grad[0, lane, span] = turned(query_grad, cos[...], -sin[...]).astype(BF16)
-            row_grad[1, lane, span] = turned(key_grad, cos[...], -sin[...]).astype(BF16)
-            row_grad[2, lane, span] = value_grad.astype(BF16)
-
-    loop(0, tokens // seq_len, attend)
-    save_rows = pltpu.make_async_copy(row_grad, o_row_grad, save_sem.at[1])
-    save_rows.start()
-    loads["qkv"].wait()
-    for stream in range(3):
-        write(stream % 2, o_attn.at[stream], lambda span: nn(qkv_in[stream, span, :], row_grad[stream]))
     for drain in pending.values():
         drain()
     save_up.wait()
-    save_rows.wait()
-
-
-def back(grad, w_qkv, w_out, w_up, w_down, rows, sums, slope, cos, sin):
+    save_context.wait()
+
+
+def back(grad, w_out, w_up, w_down, slope):
     depth, tokens = grad.shape
-    operands = (grad, w_qkv, w_out, w_up, w_down, rows, sums, slope)
-    shapes = [(3, depth, tokens), (depth, tokens), slope.shape, rows.shape]
+    operands = (grad, w_out, w_up, w_down, slope)
+    shapes = [(depth, tokens), slope.shape, (w_out.shape[1], tokens)]
     return pl.pallas_call(
         back_kernel,
         out_shape=[jax.ShapeDtypeStruct(shape, BF16) for shape in shapes],
-        in_specs=[ANY] * 8 + [VM] * 2,
-        out_specs=[ANY] * 4,
+        in_specs=[ANY] * 5,
+        out_specs=[ANY] * 3,
         scratch_shapes=[pltpu.VMEM(v.shape, v.dtype) for v in operands]
         + [
             pltpu.VMEM(slope.shape, BF16),
-            pltpu.VMEM(rows.shape[1:], BF16),
-            pltpu.VMEM(rows.shape, BF16),
+            pltpu.VMEM((w_out.shape[1], tokens), BF16),
             pltpu.VMEM((2, 4, 256, tokens), BF16),
-            DMA((8,)),
+            DMA((5,)),
             DMA((2, 4)),
             DMA((2,)),
         ],
         compiler_params=pltpu.CompilerParams(vmem_limit_bytes=56 * 1024 * 1024),
         name="back",
-    )(*operands, cos, sin)
+    )(*operands)
+
+
+ORDER = (3, 0, 1, 2)
+SLOT = (1, 0, 1, 0)
 
 
 def scatter_kernel(
-    n_dp, attn_grad, mlp_grad, streams, small, wide_grad, mixin_part, mix_tiny, hist,
-    branch_grad, act, hidden, up_grad, context, row_grad,
-    o_stream, o_mix, o_small, o_tiny, o_qkv, o_up, o_down, o_out, sent_qkv, sent_up, sent_down, sent_out,
+    n_dp, mlp_grad, streams, small, wide_grad, mixin_part, mix_tiny, hist,
+    branch_grad, act, hidden, up_grad, context, heads_rows, sums, context_grad, w_qkv, cos, sin,
+    o_stream, o_mix, o_small, o_tiny, o_qkv, o_up, o_down, o_out, sent_qkv, sent_up, sent_down, sent_out, attn_grad,
     own, from_core, from_tensor, from_near, rows_in, wide, stream_grad, gains, biases, tiny, tiny_in, tiny_out,
     hist_in, arrived, mix_part, mix_in, mix_sum, tiny_sum, ring, side_in, mine, high_in,
-    hidden_in, up_in, context_in, rows_grad_in, tile_in, stage, tile_sem, stage_sem, right_sem,
+    hidden_in, up_in, context_in, rows_grad_in, heads_in, sums_in, outer_in, qkv_in, tile_in, stage, tile_sem, stage_sem,
+    right_sem, qkv_sem,
     core_s, core_r, tensor_s, tensor_r, near_s, near_r, local, in_sem,
     side_s, side_r, high_s, high_r, peer_s, peer_r, peer_local,
     a2a_s, a2a_r, a2a_own, keep_sem, pass_s, pass_r, tiny_s, tiny_r, mix_s, mix_r, hist_sem,
@@ -1901,7 +1881,10 @@
     rights = [
         pltpu.make_async_copy(source, target, right_sem.at[number])
         for number, (source, target) in enumerate(
-            ((hidden, hidden_in), (up_grad, up_in), (context, context_in), (row_grad, rows_grad_in))
+            (
+                (hidden, hidden_in), (up_grad, up_in), (context, context_in), (heads_rows, heads_in), (sums, sums_in),
+                (context_grad, outer_in),
+            )
         )
     ]
 
@@ -2032,7 +2015,7 @@
     def load(stream, near, half_at):
         part = attn_grad.at[stream] if stream < 3 else mlp_grad
         return pltpu.make_async_copy(
-            part.at[:, lane_block(half, near, here.core, half_at, 1)], own.at[stream % 2, near, half_at],
+            part.at[:, lane_block(half, near, here.core, half_at, 1)], own.at[SLOT[stream], near, half_at],
             local.at[stream, near * 2 + half_at],
         )
 
@@ -2045,7 +2028,7 @@
 
     def to_tensor(stream, near):
         return remote(
-            own.at[stream % 2, near, here.other], from_tensor.at[stream, near],
+            own.at[SLOT[stream], near, here.other], from_tensor.at[stream, near],
             tensor_s.at[stream, near], tensor_r.at[stream, near], tensor=here.other,
         )
 
@@ -2065,7 +2048,7 @@
             span = at(index * chunk, chunk)
             for near in range(2):
                 for half_at in range(2):
-                    own[stream % 2, near, half_at, span] += from_core[stream, near, half_at, span]
+                    own[SLOT[stream], near, half_at, span] += from_core[stream, near, half_at, span]
 
         loop(0, depth // chunk, add)
 
@@ -2076,7 +2059,7 @@
         def add(index):
             span = at(index * chunk, chunk)
             for near in range(2):
-                from_tensor[stream, near, span] += own[stream % 2, near, tensor, span]
+                from_tensor[stream, near, span] += own[SLOT[stream], near, tensor, span]
 
         loop(0, depth // chunk, add)
         to_near(stream).start()
@@ -2191,7 +2174,7 @@
                     totals[source] = totals[source] + product[:8] + product[8:]
             for source in range(HIST):
                 mix_part[step, pl.ds(stream * HIST + source, 1), :] = jnp.sum(totals[source], axis=0, keepdims=True)
-            if stream == STREAMS - 1:
+            if stream == ORDER[-1]:
 
                 @pl.when(step > 0)
                 def _():
@@ -2229,51 +2212,105 @@
         for near in range(2):
             to_tensor(stream, near).start()
 
-    for stream in range(STREAMS):
+    def core_start(stream):
         for near in range(2):
             for half_at in range(2):
                 to_core(stream, near, half_at).start()
-        if stream < 2:
-            load_own(stream)
+
+    def qkv_load(stream):
+        return pltpu.make_async_copy(w_qkv.at[stream], qkv_in.at[stream % 2], qkv_sem.at[stream % 2])
+
+    seq_len = sums_in.shape[1]
+    heads = heads_in.shape[1] // HD
+    scale = 1.0 / math.sqrt(HD)
+
+    def attend_back(seq):
+        span = at(seq * seq_len, seq_len)
+        for head in range(heads):
+            lane = pl.ds(head * HD, HD)
+            queries, keys, values = (heads_in[s, lane, span] for s in range(3))
+            prob = jnp.exp(causal_scores(keys, queries) - sums_in[pl.ds(seq * heads + head, 1), :])
+            outer = outer_in[lane, span]
+            prob_grad = tn(values, outer)
+            inner = jnp.sum(prob * prob_grad, axis=0, keepdims=True)
+            score_grad = (prob * (prob_grad - inner)).astype(BF16)
+            turn_back = (cos[...], -sin[...])
+            rows_grad_in[0, lane, span] = turned(nn(keys, score_grad) * scale, *turn_back).astype(BF16)
+            rows_grad_in[1, lane, span] = turned(nt(queries, score_grad) * scale, *turn_back).astype(BF16)
+            rows_grad_in[2, lane, span] = nt(outer, prob.astype(BF16)).astype(BF16)
+
+    def input_grad(stream):
+        def put(block):
+            slot = lax.rem(block, 2)
+            return pltpu.make_async_copy(
+                stage.at[slot, :, pl.ds(0, 8 * half)], attn_grad.at[stream, at(block * tall, tall), :], stage_sem.at[slot]
+            )
+
+        def body(block):
+            value = nn(qkv_in[stream % 2, at(block * tall, tall), :], rows_grad_in[stream]).astype(BF16)
+
+            @pl.when(block >= 2)
+            def _():
+                put(block - 2).wait()
+
+            stage[lax.rem(block, 2), :, : 8 * half] = value
+            put(block).start()
+
+        qkv_load(stream).wait()
+        loop(0, depth // tall, body)
+        put(depth // tall - 2).wait()
+        put(depth // tall - 1).wait()
+        if stream + 2 < 3:
+            qkv_load(stream + 2).start()
+        core_start(stream)
+
+    core_start(ORDER[0])
+    load_own(ORDER[0])
     for copy in rights[1:] + inputs:
         copy.start()
+    qkv_load(0).start()
+    qkv_load(1).start()
     rights[0].wait()
     compute_sent(0)
     side_hop(0).start()
     side_hop(1).start()
-    after_core(0)
-    tensor_start(0)
+    after_core(ORDER[0])
+    tensor_start(ORDER[0])
     compute_mine(0)
     for copy in rights[1:] + inputs:
         copy.wait()
     ring_hop(0).start()
+    loop(0, 8 * half // seq_len, attend_back)
+    for stream in range(3):
+        input_grad(stream)
+        if stream == 0:
+            ticks(1)
+        if stream == ORDER[1]:
+            load_own(stream)
     mix_part[...] = jnp.zeros_like(mix_part)
     for stream in range(STREAMS):
         measure(stream)
-    after_core(1)
+    after_core(ORDER[1])
     ring_step(0)
-    compute_sent(1)
-    compute_mine(1)
-    for stream in range(STREAMS):
-        ticks(2)
+    for turn, stream in enumerate(ORDER):
+        ticks((1, 3, 2, 2)[turn])
         after_tensor(stream)
-        if stream + 1 < STREAMS:
-            tensor_start(stream + 1)
-            if stream + 1 < hops:
-                ring_step(stream + 1)
-        if stream + 2 < STREAMS:
-            load_own(stream + 2)
-        if stream == 0:
-            for array in range(2, len(arrays)):
-                compute_sent(array)
-                compute_mine(array)
-        if stream + 2 < STREAMS:
-            after_core(stream + 2)
-        if stream > 0:
-            back_norm(stream - 1)
-        if stream > 1:
-            receive(stream - 2)
-    back_norm(STREAMS - 1)
+        if turn + 1 < STREAMS:
+            tensor_start(ORDER[turn + 1])
+            if turn + 1 < hops:
+                ring_step(turn + 1)
+        if turn + 2 < STREAMS:
+            load_own(ORDER[turn + 2])
+        for array in ((1,), (2, 3), (4, 5), ())[turn]:
+            compute_sent(array)
+            compute_mine(array)
+        if turn + 2 < STREAMS:
+            after_core(ORDER[turn + 2])
+        if turn > 0:
+            back_norm(ORDER[turn - 1])
+        if turn > 1:
+            receive(ORDER[turn - 2])
+    back_norm(ORDER[-1])
 
     column = lax.broadcasted_iota(jnp.int32, (chunk, 128), 1)
     pltpu.make_async_copy(mixin_part, wide, in_sem.at[0]).start()
@@ -2296,9 +2333,9 @@
         return remote(tiny.at[at(target * rows, rows), :], tiny_in.at[step], tiny_s.at[step], tiny_r.at[step], dp=target)
 
     loop(1, n_dp, lambda step: tiny_send(step).start())
-    receive(2)
+    receive(ORDER[2])
     ticks(2)
-    receive(3)
+    receive(ORDER[3])
     for hop in range(STREAMS, hops):
         ring_step(hop)
     tiny_final = pltpu.make_async_copy(ring.at[hops, 0], o_tiny, last_local.at[0])
@@ -2349,8 +2386,8 @@
 
 
 def scatter(
-    n_dp, attn_grad, mlp_grad, streams, small, wide_grad, mixin_part, mix_tiny, hist,
-    branch_grad, act, hidden, up_grad, context, row_grad,
+    n_dp, mlp_grad, streams, small, wide_grad, mixin_part, mix_tiny, hist, branch_grad, act, hidden, up_grad, context,
+    rows_all, sums, context_grad, w_qkv, cos, sin,
 ):
     depth, half = wide_grad.shape
     rows = depth // n_dp
@@ -2370,11 +2407,12 @@
     ]
     outs += [(lead + (rows, QUARTERS * size), BF16) for lead, size in widths]
     outs += [(lead + (high, 2, 2 * rows, size), BF16) for lead, size in widths]
+    outs.append(((3, depth, tokens), BF16))
     return pl.pallas_call(
         functools.partial(scatter_kernel, n_dp),
         out_shape=[jax.ShapeDtypeStruct(*shape) for shape in outs],
-        in_specs=[ANY, ANY, ANY, VM] + [ANY] * 10,
-        out_specs=[ANY] * 12,
+        in_specs=[ANY, ANY, VM] + [ANY] * 13 + [VM] * 2,
+        out_specs=[ANY] * 13,
         scratch_shapes=[
             pltpu.VMEM((2, 2, 2, depth, half), BF16),
             pltpu.VMEM((STREAMS, 2, 2, depth, half), BF16),
@@ -2401,12 +2439,17 @@
             pltpu.VMEM(hidden.shape, BF16),
             pltpu.VMEM(up_grad.shape, BF16),
             pltpu.VMEM(context.shape, BF16),
-            pltpu.VMEM(row_grad.shape, BF16),
+            pltpu.VMEM(rows_all.shape, BF16),
+            pltpu.VMEM(rows_all.shape, BF16),
+            pltpu.VMEM(sums.shape, F32),
+            pltpu.VMEM(context_grad.shape, BF16),
+            pltpu.VMEM((2,) + w_qkv.shape[1:], BF16),
             pltpu.VMEM((2, 2 * rows, tokens), BF16),
-            pltpu.VMEM((2, 2 * rows, width), BF16),
+            pltpu.VMEM((2, 2 * rows, max(width, tokens)), BF16),
             DMA((2,)),
             DMA((2,)),
-            DMA((4,)),
+            DMA((6,)),
+            DMA((2,)),
             DMA((STREAMS, 4)),
             DMA((STREAMS, 4)),
             DMA((STREAMS, 2)),
@@ -2444,8 +2487,8 @@
         ),
         name="scatter",
     )(
-        attn_grad, mlp_grad, streams, small, wide_grad, mixin_part, mix_tiny, hist, branch_grad, act, hidden, up_grad,
-        context, row_grad,
+        mlp_grad, streams, small, wide_grad, mixin_part, mix_tiny, hist, branch_grad, act, hidden, up_grad, context,
+        rows_all, sums, context_grad, w_qkv, cos, sin,
     )[:8]
 
 
@@ -2459,8 +2502,9 @@
     return (jnp.cos(angles), jnp.sin(angles))
 
 
-def finish_kernel(mix_rows, stream_grad, *refs):
-    narrow, history_grad, wide = refs[:4], refs[4], refs[5:]
+def finish_kernel(mix_rows, stream_grad, small, tiny, block, *refs):
+    narrow, history_grad, wide = refs[:4], refs[4], refs[5:9]
+    gain, bias, mix_in_grad, mix_out_grad, block_out = refs[9:]
     rows = stream_grad.shape[1]
     tile, span = min(32, rows), 512
 
@@ -2477,9 +2521,14 @@
     loop(0, rows // tile * (stream_grad.shape[2] // span), body)
     for low, full in zip(narrow, wide):
         full[...] = low[...].astype(F32)
-
-
-def finish(mix_rows, stream_grad, *grads):
+    block_out[...] = block[...]
+    gain[...] = small[MIXH : MIXH + 2]
+    bias[...] = small[MIXH + 2 : MIXH + 4]
+    mix_in_grad[...] = small[:MIXH]
+    mix_out_grad[...] = tiny[:, : STREAMS * NEXT]
+
+
+def finish(mix_rows, stream_grad, small, tiny, block, *grads):
     rows, tokens = stream_grad.shape[1:]
     steps = rows // 16
     lanes = tokens // steps
@@ -2492,17 +2541,25 @@
     def along(count):
         return pl.BlockSpec((count, rows, lanes), lambda i: (0, 0, i))
 
+    def whole(shape):
+        return pl.BlockSpec(shape, lambda i: (0, 0))
+
+    blocks = pl.BlockSpec((block.shape[0] // steps, block.shape[1]), lambda i: (i, 0))
+    smalls = [(2, rows), (2, rows), (MIXH, rows), (MIXH, STREAMS * NEXT)]
     return pl.pallas_call(
         finish_kernel,
         grid=(steps,),
         out_shape=[jax.ShapeDtypeStruct((HIST, rows, tokens), BF16)]
-        + [jax.ShapeDtypeStruct(g.shape, F32) for g in grads],
+        + [jax.ShapeDtypeStruct(g.shape, F32) for g in grads]
+        + [jax.ShapeDtypeStruct(shape, F32) for shape in smalls]
+        + [jax.ShapeDtypeStruct(block.shape, BF16)],
         in_specs=[pl.BlockSpec((mix_rows.shape[0], lanes), lambda i: (0, i)), along(STREAMS)]
+        + [whole(small.shape), whole(tiny.shape), blocks]
         + [weight(g) for g in grads],
-        out_specs=[along(HIST)] + [weight(g) for g in grads],
+        out_specs=[along(HIST)] + [weight(g) for g in grads] + [whole(shape) for shape in smalls] + [blocks],
         compiler_params=pltpu.CompilerParams(vmem_limit_bytes=60 * 1024 * 1024),
         name="finish",
-    )(mix_rows, stream_grad, *grads)
+    )(mix_rows, stream_grad, small, tiny, block, *grads)
 
 
 def per_device(
@@ -2534,15 +2591,15 @@
     branch_grad, wide_grad, block, next_mix, mixin_part, tiny = join(
         part, streams, out_cot, small_all, mix_out, next_rows
     )
-    attn_in_grad, mlp_in_grad, up_grad, row_grad = back(
-        branch_grad, qkv, out, up, down, rows, sums, slope, cos, sin
-    )
+    mlp_in_grad, up_grad, context_grad = back(branch_grad, out, up, down, slope)
     stream_grad, mix_grad, small_total, tiny, qkv_total, up_total, down_total, out_total = scatter(
-        n_dp, attn_in_grad, mlp_in_grad, streams, small_all, wide_grad, mixin_part, tiny, history,
-        branch_grad, act, hidden, up_grad, context, row_grad,
-    )
-    history_grad, qkv_total, up_total, down_total, out_total = finish(
-        mix_rows, stream_grad, qkv_total, up_total, down_total, out_total
+        n_dp, mlp_in_grad, streams, small_all, wide_grad, mixin_part, tiny, history, branch_grad, act, hidden, up_grad,
+        context, rows, sums, context_grad, qkv, cos, sin,
+    )
+    (
+        history_grad, qkv_total, up_total, down_total, out_total, gain_total, bias_total, mixin_total, mixout_total, block,
+    ) = finish(
+        mix_rows, stream_grad, small_total, tiny, block, qkv_total, up_total, down_total, out_total
     )
     return (
         block,
@@ -2553,10 +2610,10 @@
         out_total,
         up_total,
         down_total,
-        small_total[MIXH : MIXH + 2],
-        small_total[MIXH + 2 : MIXH + 4],
-        small_total[:MIXH].T,
-        tiny[:, : STREAMS * NEXT],
+        gain_total,
+        bias_total,
+        mixin_total.T,
+        mixout_total,
         tiny[: STREAMS * NEXT, MIXH],
     )
 

time: 646 us -> 620 us (0.960)
  Pallas kernels: 627 us -> 607 us
    pallas_call x1, Pallas kernels: 29.8 us -> 17.2 us  [back(): pl.pallas_call(back_kernel, out_shape=[jax.ShapeDtypeStruct(shape, BF16)...]
    pallas_call x1, Pallas kernels: 268 us -> 260 us  [scatter(): pl.pallas_call(functools.partial(scatter_kernel, n_dp), out_shape=[jax.Sh...]
where the time goes in v5:
time: 620 us; the launch traced here: 616 us
  Pallas kernels  607 us (98%)
  local copies, waits for them, and re-layouts  6.42 us (1%)
    pallas_call x1, Pallas kernels, scatter(): pl.pallas_call(functools.partial(scatter_kernel, n_dp), out_shape=[jax.Sh...  260 us
    pallas_call x1, Pallas kernels, gather(): pl.pallas_call(functools.partial(gather_kernel, n_dp), out_shape=[jax.Sha...  257 us
    pallas_call x1, Pallas kernels, join(): pl.pallas_call(join_kernel, out_shape=[jax.ShapeDtypeStruct(*shape) for s...  60.2 us
    pallas_call x1, Pallas kernels, back(): pl.pallas_call(back_kernel, out_shape=[jax.ShapeDtypeStruct(shape, BF16)...  17.2 us
    pallas_call x1, Pallas kernels, finish(): pl.pallas_call(finish_kernel, grid=(steps,), out_shape=[jax.ShapeDtypeStr...  12.7 us

profile of v5, /device:TPU:7, one launch (start us, length us, event | category | flops | bytes accessed | tf_op | source)
XLA Modules:
  0.0 616.4 jit_solution(5199728162703742620)
XLA Ops:
  0.7 0.1 pad.3.clone
  0.7 0.8 multiply_sine_fusion
  1.5 1.4 maximum_maximum_fusion.small
  2.9 0.8 copy.30
  3.7 0.6 dynamic-slice_bitcast_fusion.1.mix
  4.4 0.8 copy.31
  5.2 0.6 dynamic-slice_bitcast_fusion.next_raw
  5.8 256.5 %gather.1 = (f32[36,4096]{1,0:T(8,128)}, bf16[2,2,2,2,128,128]{5,4,3,2,1,0:T(8,128)(2,1)}, bf16[4,2048,128]{2,1,0:T(8,128)(2,1)}, bf16[4,2048,1024]{2,1,0:T(8,12...) custom-call(bf16[9,128,4096]{2,1,0:T(8,128)(2,1)} %hist.3, ...), custom_call_target="tpu_custom_call" | custom-call | tf_op jit(solution)/shard_map/gather/pallas_call | solution.py:549
  262.3 60.2 %join.1 = (bf16[2048,1024]{1,0:T(8,128)(2,1)}, f32[2048,128]{1,0:T(8,128)}, bf16[256,2048]{1,0:T(8,128)(2,1)}, f32[40,256]{1,0:T(8,128)}, f32[2048,128]{1,0:T(8,128)}, /*index=5*/f32[40,128]{1,0:T(8,128)}) custom-call(bf16[2048,1024]{1,0:T(8,128)(2,1)} %get-tuple-element.55.part, bf16[4,2048,128]{2,1,0:T(8,128)(2,1)} %get-tuple-element.56.streams, ...), custom_call_target="tpu_custom_call" | custom-call | tf_op jit(solution)/shard_map/join/pallas_call | solution.py:1716
  322.5 17.2 %back.1 = (bf16[2048,1024]{1,0:T(8,128)(2,1)}, bf16[1024,1024]{1,0:T(8,128)(2,1)}, bf16[256,1024]{1,0:T(8,128)(2,1)}) custom-call(bf16[2048,1024]{1,0:T(8,128)(2,1)} %get-tuple-element.58.grad.branch_grad, bf16[2048,256]{1,0:T(8,128)(2,1)} %bitcast.28, bf16[2048,1024]{1,0:T(8,128)(2,1)} %bitcast.23, bf16[2048,1024]{1,0:T(8,128)(2,1)} %bitcast.24, ...), custom_call_target="tpu_custom_call" | custom-call | tf_op jit(solution)/shard_map/back/pallas_call | solution.py:1825
  339.7 0.0 copy-start
  339.7 0.0 copy-start.1
  339.7 260.2 %scatter.1 = (bf16[4,128,4096]{2,1,0:T(8,128)(2,1)}, f32[40,256]{1,0:T(8,128)}, f32[128,128]{1,0:T(8,128)}, f32[40,128]{1,0:T(8,128)}, bf16[3,128,1024]{2,1,0:T(...) custom-call(bf16[2048,1024]{1,0:T(8,128)(2,1)} %get-tuple-element.63, ...), custom_call_target="tpu_custom_call" | custom-call | tf_op jit(solution)/shard_map/scatter/pallas_call | solution.py:2411
  599.9 1.4 slice_reduce_fusion
  601.4 0.8 slice_bitcast_fusion
  602.2 0.6 copy.33
  602.8 0.0 copy-done
  602.8 0.0 copy-done.1
  602.8 0.1 add_bitcast_fusion
  602.9 0.6 copy.32
  603.5 12.7 %finish.1 = (bf16[9,128,4096]{2,1,0:T(8,128)(2,1)}, f32[3,128,1024]{2,1,0:T(8,128)}, f32[128,4096]{1,0:T(8,128)}, f32[128,4096]{1,0:T(8,128)}, f32[128,1024]{1,0...) custom-call(f32[36,4096]{1,0:T(8,128)} %get-tuple-element.54.mix_row, ...), custom_call_target="tpu_custom_call" | custom-call | tf_op jit(solution)/shard_map/finish/pallas_call | solution.py:2549
  (7 shorter events, 0.0 us)
Async XLA Ops:
  339.7 263.1 %copy-start = (f32[40,256]{1,0:T(8,128)S(1)}, f32[40,256]{1,0:T(8,128)}, u32[]{:S(2)}) copy-start(f32[40,256]{1,0:T(8,128)} %get-tuple-element.84) | copy-start | bytes 122884
  339.7 263.1 %copy-start.1 = (f32[40]{0:T(128)S(1)}, f32[40]{0:T(128)}, u32[]{:S(2)}) copy-start(f32[40]{0:T(128)} %param.23) | copy-start | bytes 484

commit v6 on v5

--- a/solution.py
+++ b/solution.py
@@ -365,7 +365,7 @@
         for which, buf in early_pairs:
             early(which, buf, phase - 1).wait()
             early(which, buf, phase).start()
-        if phase == 2:
+        if phase == 1:
             second(0)
     early(0, mix_all, last).wait()
     def mix_lanes(index):

time: 620 us -> 616 us (level)
    pallas_call x1, Pallas kernels: 257 us -> 248 us  [gather(): pl.pallas_call(functools.partial(gather_kernel, n_dp), out_shape=[jax.Sha...]
where the time goes in v6:
time: 616 us; the launch traced here: 613 us
  Pallas kernels  603 us (98%)
  local copies, waits for them, and re-layouts  6.42 us (1%)
    pallas_call x1, Pallas kernels, scatter(): pl.pallas_call(functools.partial(scatter_kernel, n_dp), out_shape=[jax.Sh...  260 us
    pallas_call x1, Pallas kernels, gather(): pl.pallas_call(functools.partial(gather_kernel, n_dp), out_shape=[jax.Sha...  248 us
    pallas_call x1, Pallas kernels, join(): pl.pallas_call(join_kernel, out_shape=[jax.ShapeDtypeStruct(*shape) for s...  65.3 us
    pallas_call x1, Pallas kernels, back(): pl.pallas_call(back_kernel, out_shape=[jax.ShapeDtypeStruct(shape, BF16)...  17.2 us
    pallas_call x1, Pallas kernels, finish(): pl.pallas_call(finish_kernel, grid=(steps,), out_shape=[jax.ShapeDtypeStr...  12.7 us

profile of v6, /device:TPU:7, one launch (start us, length us, event | category | flops | bytes accessed | tf_op | source)
XLA Modules:
  0.0 612.7 jit_solution(12488604182075669917)
XLA Ops:
  0.7 0.1 pad.3.clone
  0.7 0.8 multiply_sine_fusion
  1.5 1.4 maximum_maximum_fusion.small
  2.9 0.8 copy.30
  3.7 0.6 dynamic-slice_bitcast_fusion.1.mix
  4.4 0.8 copy.31
  5.2 0.6 dynamic-slice_bitcast_fusion.next_raw
  5.8 248.1 %gather.1 = (f32[36,4096]{1,0:T(8,128)}, bf16[2,2,2,2,128,128]{5,4,3,2,1,0:T(8,128)(2,1)}, bf16[4,2048,128]{2,1,0:T(8,128)(2,1)}, bf16[4,2048,1024]{2,1,0:T(8,12...) custom-call(bf16[9,128,4096]{2,1,0:T(8,128)(2,1)} %hist.3, ...), custom_call_target="tpu_custom_call" | custom-call | tf_op jit(solution)/shard_map/gather/pallas_call | solution.py:549
  253.9 65.3 %join.1 = (bf16[2048,1024]{1,0:T(8,128)(2,1)}, f32[2048,128]{1,0:T(8,128)}, bf16[256,2048]{1,0:T(8,128)(2,1)}, f32[40,256]{1,0:T(8,128)}, f32[2048,128]{1,0:T(8,128)}, /*index=5*/f32[40,128]{1,0:T(8,128)}) custom-call(bf16[2048,1024]{1,0:T(8,128)(2,1)} %get-tuple-element.55.part, bf16[4,2048,128]{2,1,0:T(8,128)(2,1)} %get-tuple-element.56.streams, ...), custom_call_target="tpu_custom_call" | custom-call | tf_op jit(solution)/shard_map/join/pallas_call | solution.py:1716
  319.1 17.2 %back.1 = (bf16[2048,1024]{1,0:T(8,128)(2,1)}, bf16[1024,1024]{1,0:T(8,128)(2,1)}, bf16[256,1024]{1,0:T(8,128)(2,1)}) custom-call(bf16[2048,1024]{1,0:T(8,128)(2,1)} %get-tuple-element.58.grad.branch_grad, bf16[2048,256]{1,0:T(8,128)(2,1)} %bitcast.28, bf16[2048,1024]{1,0:T(8,128)(2,1)} %bitcast.23, bf16[2048,1024]{1,0:T(8,128)(2,1)} %bitcast.24, ...), custom_call_target="tpu_custom_call" | custom-call | tf_op jit(solution)/shard_map/back/pallas_call | solution.py:1825
  336.3 0.0 copy-start
  336.4 0.0 copy-start.1
  336.4 259.8 %scatter.1 = (bf16[4,128,4096]{2,1,0:T(8,128)(2,1)}, f32[40,256]{1,0:T(8,128)}, f32[128,128]{1,0:T(8,128)}, f32[40,128]{1,0:T(8,128)}, bf16[3,128,1024]{2,1,0:T(...) custom-call(bf16[2048,1024]{1,0:T(8,128)(2,1)} %get-tuple-element.63, ...), custom_call_target="tpu_custom_call" | custom-call | tf_op jit(solution)/shard_map/scatter/pallas_call | solution.py:2411
  596.2 1.4 slice_reduce_fusion
  597.6 0.8 slice_bitcast_fusion
  598.4 0.6 copy.33
  599.1 0.0 copy-done
  599.1 0.0 copy-done.1
  599.1 0.1 add_bitcast_fusion
  599.1 0.6 copy.32
  599.8 12.7 %finish.1 = (bf16[9,128,4096]{2,1,0:T(8,128)(2,1)}, f32[3,128,1024]{2,1,0:T(8,128)}, f32[128,4096]{1,0:T(8,128)}, f32[128,4096]{1,0:T(8,128)}, f32[128,1024]{1,0...) custom-call(f32[36,4096]{1,0:T(8,128)} %get-tuple-element.54.mix_row, ...), custom_call_target="tpu_custom_call" | custom-call | tf_op jit(solution)/shard_map/finish/pallas_call | solution.py:2549
  (7 shorter events, 0.0 us)
Async XLA Ops:
  336.3 262.7 %copy-start = (f32[40,256]{1,0:T(8,128)S(1)}, f32[40,256]{1,0:T(8,128)}, u32[]{:S(2)}) copy-start(f32[40,256]{1,0:T(8,128)} %get-tuple-element.84) | copy-start | bytes 122884
  336.4 262.7 %copy-start.1 = (f32[40]{0:T(128)S(1)}, f32[40]{0:T(128)}, u32[]{:S(2)}) copy-start(f32[40]{0:T(128)} %param.23) | copy-start | bytes 484

commit v7 on v6

--- a/solution.py
+++ b/solution.py
@@ -1764,8 +1764,16 @@
     tile = 256
     loads = {}
     pairs = (
-        ("grad", grad, grad_in), ("out", w_out, out_in), ("down", w_down, down_in), ("slope", slope, slope_in),
-        ("up", w_up, up_in),
+        [("grad", grad, grad_in), ("out", w_out, out_in)]
+        + [
+            pair
+            for first in range(0, slope.shape[0], tile)
+            for pair in (
+                (("down", first), w_down.at[:, pl.ds(first, tile)], down_in.at[:, pl.ds(first, tile)]),
+                (("slope", first), slope.at[pl.ds(first, tile)], slope_in.at[pl.ds(first, tile)]),
+            )
+        ]
+        + [("up", w_up, up_in)]
     )
     for number, (name, source, target) in enumerate(pairs):
         loads[name] = pltpu.make_async_copy(source, target, load_sem.at[number])
@@ -1800,14 +1808,11 @@
     context_grad[...] = tn(out_in[...], grad_in[...]).astype(BF16)
     save_context = pltpu.make_async_copy(context_grad, o_context, save_sem.at[1])
     save_context.start()
-    for name in ("down", "slope"):
-        loads[name].wait()
-
-    def lift(index):
-        span = at(index * tile, tile)
+    for first in range(0, slope.shape[0], tile):
+        loads["down", first].wait()
+        loads["slope", first].wait()
+        span = pl.ds(first, tile)
         up_grad[span, :] = (tn(down_in[:, span], grad_in[...]) * slope_in[span, :]).astype(BF16)
-
-    loop(0, up_grad.shape[0] // tile, lift)
     loads["up"].wait()
     save_up = pltpu.make_async_copy(up_grad, o_up_grad, save_sem.at[0])
     save_up.start()
@@ -1832,7 +1837,7 @@
             pltpu.VMEM(slope.shape, BF16),
             pltpu.VMEM((w_out.shape[1], tokens), BF16),
             pltpu.VMEM((2, 4, 256, tokens), BF16),
-            DMA((5,)),
+            DMA((3 + 2 * (slope.shape[0] // 256),)),
             DMA((2, 4)),
             DMA((2,)),
         ],

time: 616 us -> 614 us (level)
  no operation moved by 1% of the time
where the time goes in v7:
time: 614 us; the launch traced here: 611 us
  Pallas kernels  601 us (98%)
  local copies, waits for them, and re-layouts  6.42 us (1%)
    pallas_call x1, Pallas kernels, scatter(): pl.pallas_call(functools.partial(scatter_kernel, n_dp), out_shape=[jax.Sh...  259 us
    pallas_call x1, Pallas kernels, gather(): pl.pallas_call(functools.partial(gather_kernel, n_dp), out_shape=[jax.Sha...  248 us
    pallas_call x1, Pallas kernels, join(): pl.pallas_call(join_kernel, out_shape=[jax.ShapeDtypeStruct(*shape) for s...  65.3 us
    pallas_call x1, Pallas kernels, back(): pl.pallas_call(back_kernel, out_shape=[jax.ShapeDtypeStruct(shape, BF16)...  15.6 us
    pallas_call x1, Pallas kernels, finish(): pl.pallas_call(finish_kernel, grid=(steps,), out_shape=[jax.ShapeDtypeStr...  12.7 us

profile of v7, /device:TPU:7, one launch (start us, length us, event | category | flops | bytes accessed | tf_op | source)
XLA Modules:
  0.0 610.7 jit_solution(14843846276677561379)
XLA Ops:
  0.7 0.1 pad.3.clone
  0.7 0.8 multiply_sine_fusion
  1.5 1.4 maximum_maximum_fusion.small
  2.9 0.8 copy.30
  3.7 0.6 dynamic-slice_bitcast_fusion.1.mix
  4.4 0.8 copy.31
  5.2 0.6 dynamic-slice_bitcast_fusion.next_raw
  5.8 248.1 %gather.1 = (f32[36,4096]{1,0:T(8,128)}, bf16[2,2,2,2,128,128]{5,4,3,2,1,0:T(8,128)(2,1)}, bf16[4,2048,128]{2,1,0:T(8,128)(2,1)}, bf16[4,2048,1024]{2,1,0:T(8,12...) custom-call(bf16[9,128,4096]{2,1,0:T(8,128)(2,1)} %hist.3, ...), custom_call_target="tpu_custom_call" | custom-call | tf_op jit(solution)/shard_map/gather/pallas_call | solution.py:549
  253.9 65.3 %join.1 = (bf16[2048,1024]{1,0:T(8,128)(2,1)}, f32[2048,128]{1,0:T(8,128)}, bf16[256,2048]{1,0:T(8,128)(2,1)}, f32[40,256]{1,0:T(8,128)}, f32[2048,128]{1,0:T(8,128)}, /*index=5*/f32[40,128]{1,0:T(8,128)}) custom-call(bf16[2048,1024]{1,0:T(8,128)(2,1)} %get-tuple-element.55.part, bf16[4,2048,128]{2,1,0:T(8,128)(2,1)} %get-tuple-element.56.streams, ...), custom_call_target="tpu_custom_call" | custom-call | tf_op jit(solution)/shard_map/join/pallas_call | solution.py:1716
  319.1 15.6 %back.1 = (bf16[2048,1024]{1,0:T(8,128)(2,1)}, bf16[1024,1024]{1,0:T(8,128)(2,1)}, bf16[256,1024]{1,0:T(8,128)(2,1)}) custom-call(bf16[2048,1024]{1,0:T(8,128)(2,1)} %get-tuple-element.58.grad.branch_grad, bf16[2048,256]{1,0:T(8,128)(2,1)} %bitcast.28, bf16[2048,1024]{1,0:T(8,128)(2,1)} %bitcast.23, bf16[2048,1024]{1,0:T(8,128)(2,1)} %bitcast.24, ...), custom_call_target="tpu_custom_call" | custom-call | tf_op jit(solution)/shard_map/back/pallas_call | solution.py:1830
  334.8 0.0 copy-start
  334.8 0.0 copy-start.1
  334.8 259.5 %scatter.1 = (bf16[4,128,4096]{2,1,0:T(8,128)(2,1)}, f32[40,256]{1,0:T(8,128)}, f32[128,128]{1,0:T(8,128)}, f32[40,128]{1,0:T(8,128)}, bf16[3,128,1024]{2,1,0:T(...) custom-call(bf16[2048,1024]{1,0:T(8,128)(2,1)} %get-tuple-element.63, ...), custom_call_target="tpu_custom_call" | custom-call | tf_op jit(solution)/shard_map/scatter/pallas_call | solution.py:2416
  594.2 1.4 slice_reduce_fusion
  595.7 0.8 slice_bitcast_fusion
  596.5 0.6 copy.33
  597.1 0.0 copy-done
  597.1 0.0 copy-done.1
  597.1 0.1 add_bitcast_fusion
  597.2 0.6 copy.32
  597.8 12.7 %finish.1 = (bf16[9,128,4096]{2,1,0:T(8,128)(2,1)}, f32[3,128,1024]{2,1,0:T(8,128)}, f32[128,4096]{1,0:T(8,128)}, f32[128,4096]{1,0:T(8,128)}, f32[128,1024]{1,0...) custom-call(f32[36,4096]{1,0:T(8,128)} %get-tuple-element.54.mix_row, ...), custom_call_target="tpu_custom_call" | custom-call | tf_op jit(solution)/shard_map/finish/pallas_call | solution.py:2554
  (7 shorter events, 0.0 us)
Async XLA Ops:
  334.8 262.3 %copy-start = (f32[40,256]{1,0:T(8,128)S(1)}, f32[40,256]{1,0:T(8,128)}, u32[]{:S(2)}) copy-start(f32[40,256]{1,0:T(8,128)} %get-tuple-element.84) | copy-start | bytes 122884
  334.8 262.3 %copy-start.1 = (f32[40]{0:T(128)S(1)}, f32[40]{0:T(128)}, u32[]{:S(2)}) copy-start(f32[40]{0:T(128)} %param.23) | copy-start | bytes 484
